TPU v7x, 512 devices: a whole 4x8x8 slice. The times are simulated.
512 devices in a mesh: lat: 64 (over z, y), batch: 8 (over x, core).
Axes of the slice: x: 4, y: 8, z: 8, core: 2. Of those that a mesh axis runs over, the one named last changes fastest.
Arguments:
- fields: bfloat16 [8, 192, 384, 384], P('batch', 'lat'), may hold values from -6 to 6
- cotangent: bfloat16 [8, 192, 384, 384], P('batch', 'lat'), may hold values from -6 to 6
- weights: bfloat16 [128, 2, 384, 384], P('lat'), may hold values from -0.21875 to 0.21875
- degree_of: int32 [128], replicated, may hold values from 0 to 127, each once
Outputs:
- grad_fields: bfloat16 [8, 192, 384, 384], P('batch', 'lat')
- grad_weights: bfloat16 [128, 2, 384, 384], P('lat')
Inputs may be any that keep to these rules, and one draw needn't show every extreme that they name: `degree_of`: each degree 0 to 127 is held by exactly one slot.
All inputs are finite; a program needn't handle non-finite values.
Results may differ from a plain program's by a relative error of at most 0.018.
Values may be sent and summed in bfloat16 or wider, within the bound.
No kernel may reach another device: no remote copies, remote signals or barrier semaphores. Data moves between devices by JAX's collectives and lax.ppermute only.
A program may use at most 64 MiB of HBM per device.

v0:
```python
import jax
import jax.numpy as jnp
from jax import lax
from jax.sharding import PartitionSpec as P

LATS = 192
LONS = 384
ORDERS = 128
DEGREES = 128
CHANNELS = 384


def in_one_piece(arrays, axis, dim, along):
    widths = [a.shape[along] for a in arrays]
    both = jnp.concatenate(arrays, axis=along)
    out = lax.all_gather(both, axis, axis=dim, tiled=True)
    return tuple(jnp.split(out, [sum(widths[:k]) for k in range(1, len(widths))], axis=along))


def legendre_table(order_ids, lat_count, degree_count):
    colatitude = jnp.pi * (jnp.arange(lat_count, dtype=jnp.float32) + 0.5) / lat_count
    cosine = jnp.cos(colatitude)[None, :]
    log_sine = jnp.log(jnp.sin(colatitude))[None, :]
    order_col = order_ids[:, None]
    order_real = order_col.astype(jnp.float32)
    steps_up = jnp.arange(1, degree_count + 1, dtype=jnp.float32)[None, :]
    factor = jnp.where(
        steps_up <= order_real, 0.5 * jnp.log((2.0 * steps_up + 1.0) / (2.0 * steps_up)), 0.0
    )
    log_start = 0.5 * jnp.log(1.0 / (4.0 * jnp.pi)) + jnp.sum(factor, axis=1, keepdims=True)
    diagonal = jnp.exp(log_start + order_real * log_sine)
    squared = order_real * order_real

    def advance(carry, degree):
        previous, older = carry
        degree_real = degree.astype(jnp.float32)
        lead = jnp.sqrt(
            jnp.maximum(4.0 * degree_real * degree_real - 1.0, 0.0)
            / jnp.maximum(degree_real * degree_real - squared, 1.0)
        )
        lower = degree_real - 1.0
        back = jnp.sqrt(
            jnp.maximum(lower * lower - squared, 0.0) / jnp.maximum(4.0 * lower * lower - 1.0, 1.0)
        )
        general = lead * (cosine * previous - back * older)
        first = jnp.sqrt(2.0 * order_real + 3.0) * cosine * previous
        value = jnp.where(
            degree == order_col,
            diagonal,
            jnp.where(
                degree == order_col + 1, first, jnp.where(degree > order_col + 1, general, 0.0)
            ),
        )
        return ((value, previous), value)

    zeros = jnp.zeros((order_ids.shape[0], lat_count), jnp.float32)
    final_state, table = lax.scan(
        advance, (zeros, zeros), jnp.arange(degree_count, dtype=jnp.int32)
    )
    return jnp.transpose(table, (1, 0, 2))


def spectral_tables(start, ord_dev, degree_of):
    order_ids = start + jnp.arange(ord_dev, dtype=jnp.int32)
    mine = legendre_table(order_ids, LATS, DEGREES)
    selector = (degree_of[:, None] == jnp.arange(DEGREES, dtype=jnp.int32)[None, :]).astype(
        jnp.float32
    )
    chosen = jnp.einsum("mli,jl->mji", mine, selector, precision=lax.Precision.HIGHEST)
    colatitude = jnp.pi * (jnp.arange(LATS, dtype=jnp.float32) + 0.5) / LATS
    quadrature = 2.0 * jnp.pi * jnp.pi / LATS * jnp.sin(colatitude)
    return ((chosen * quadrature[None, None, :]).astype(jnp.bfloat16), chosen.astype(jnp.bfloat16))


def fourier_tables(lon_count, order_count):
    lon_ids = jnp.arange(lon_count, dtype=jnp.int32)[:, None]
    order_ids = jnp.arange(order_count, dtype=jnp.int32)[None, :]
    phase = 2.0 * jnp.pi * (lon_ids * order_ids % lon_count).astype(jnp.float32) / lon_count
    forward = (
        jnp.stack([jnp.cos(phase), -jnp.sin(phase)], axis=2).reshape(lon_count, 2 * order_count)
        / lon_count
    )
    doubled = jnp.where(order_ids == 0, 1.0, 2.0)
    inverse = jnp.stack([doubled * jnp.cos(phase), -doubled * jnp.sin(phase)], axis=2).reshape(
        lon_count, 2 * order_count
    )
    return (forward.astype(jnp.bfloat16), jnp.transpose(inverse).astype(jnp.bfloat16))


def to_orders(values):
    return lax.all_to_all(values, "lat", split_axis=1, concat_axis=0, tiled=True)


def to_degrees(values):
    return lax.all_to_all(values, "lat", split_axis=0, concat_axis=1, tiled=True)


def back_to_orders(values):
    return lax.all_to_all(values, "lat", split_axis=1, concat_axis=0, tiled=True)


def to_bands(values):
    return lax.all_to_all(values, "lat", split_axis=0, concat_axis=1, tiled=True)


def product(spec, left, right):
    return jnp.einsum(spec, left, right, preferred_element_type=jnp.float32)


def apply_filter(coeffs, weights):
    c_real = coeffs[:, :, 0]
    c_imag = coeffs[:, :, 1]
    w_real = weights[:, 0]
    w_imag = weights[:, 1]
    f_real = product("jmsc,jcd->jmsd", c_real, w_real) - product("jmsc,jcd->jmsd", c_imag, w_imag)
    f_imag = product("jmsc,jcd->jmsd", c_real, w_imag) + product("jmsc,jcd->jmsd", c_imag, w_real)
    return jnp.stack([f_real, f_imag], axis=2).astype(jnp.bfloat16)


def adjoint_filter(grads, weights):
    g_real = grads[:, :, 0]
    g_imag = grads[:, :, 1]
    w_real = weights[:, 0]
    w_imag = weights[:, 1]
    a_real = product("jmsd,jcd->jmsc", g_real, w_real) + product("jmsd,jcd->jmsc", g_imag, w_imag)
    a_imag = product("jmsd,jcd->jmsc", g_imag, w_real) - product("jmsd,jcd->jmsc", g_real, w_imag)
    return jnp.stack([a_real, a_imag], axis=2).astype(jnp.bfloat16)


def filter_grad(coeffs, grads):
    c_real = coeffs[:, :, 0]
    c_imag = coeffs[:, :, 1]
    g_real = grads[:, :, 0]
    g_imag = grads[:, :, 1]
    dw_real = product("jmsc,jmsd->jcd", c_real, g_real) + product("jmsc,jmsd->jcd", c_imag, g_imag)
    dw_imag = product("jmsc,jmsd->jcd", c_real, g_imag) - product("jmsc,jmsd->jcd", c_imag, g_real)
    return jnp.stack([dw_real, dw_imag], axis=1)


def local(fields, cotangent, weights, degree_of):
    samples = fields.shape[0]
    band_rows = fields.shape[1]
    ord_dev = ORDERS // lax.axis_size("lat")
    forward, inverse = fourier_tables(LONS, ORDERS)
    qslot, pslot = spectral_tables(lax.axis_index("lat") * ord_dev, ord_dev, degree_of)
    spectra = product("sikc,kf->ifsc", fields, forward).astype(jnp.bfloat16)
    spectra = spectra.reshape(band_rows, ORDERS, 2, samples, CHANNELS)
    gathered = to_orders(spectra)
    coeffs_local = product("mji,imrsc->jmrsc", qslot, gathered).astype(jnp.bfloat16)
    coeffs = to_degrees(coeffs_local)
    filtered = apply_filter(coeffs, weights)
    returned = back_to_orders(filtered)
    synth_local = product("mji,jmrsc->imrsc", pslot, returned).astype(jnp.bfloat16)
    synth = to_bands(synth_local)
    response = product(
        "ifsc,fk->sikc", synth.reshape(band_rows, 2 * ORDERS, samples, CHANNELS), inverse
    )
    activated, pullback = jax.vjp(jax.nn.gelu, response)
    upstream = pullback(cotangent.astype(jnp.float32))[0].astype(jnp.bfloat16)
    grad_synth = product("sikc,fk->ifsc", upstream, inverse).astype(jnp.bfloat16)
    grad_synth = grad_synth.reshape(band_rows, ORDERS, 2, samples, CHANNELS)
    grad_gathered = to_orders(grad_synth)
    grad_local = product("mji,imrsc->jmrsc", pslot, grad_gathered).astype(jnp.bfloat16)
    grad_filtered = to_degrees(grad_local)
    all_coeffs, all_grads = in_one_piece((coeffs, grad_filtered), "batch", 3, 0)
    weight_total = filter_grad(all_coeffs, all_grads)
    grad_coeffs = adjoint_filter(grad_filtered, weights)
    grad_back = back_to_orders(grad_coeffs)
    grad_local_spec = product("mji,jmrsc->imrsc", qslot, grad_back).astype(jnp.bfloat16)
    grad_bands = to_bands(grad_local_spec)
    delta = product(
        "ifsc,kf->sikc", grad_bands.reshape(band_rows, 2 * ORDERS, samples, CHANNELS), forward
    )
    grad_fields = (cotangent.astype(jnp.float32) + delta).astype(jnp.bfloat16)
    return (grad_fields, weight_total.astype(jnp.bfloat16))


def solution(mesh):
    return jax.shard_map(
        local,
        mesh=mesh,
        in_specs=(
            P("batch", "lat", None, None),
            P("batch", "lat", None, None),
            P("lat", None, None, None),
            P(),
        ),
        out_specs=(P("batch", "lat", None, None), P("lat", None, None, None)),
        check_vma=False,
    )
```

profile of v0, /device:TPU:6, one launch (start us, length us, event | category | flops | bytes accessed | tf_op | source)
XLA Modules:
  0.0 588.7 jit_solution(4414124567485048653)
XLA Ops:
  9.7 1.2 copy.172
  11.0 16.6 %all-to-all-start = ((bf16[3,128,2,1,384]{4,2,0,3,1:T(2,128)(2,1)}), bf16[3,128,2,1,384]{4,2,0,3,1:T(2,128)(2,1)S(1)}, u32[]{:S(2)}, u32[]{:S(2)}) async-start(bf16[3,128,2,1,384]{4,2,0,3,1:T(2,128)(2,1)} %copy.172), calls=%async_computation | async-start | bytes 1179648 | tf_op jit(solution)/shard_map/all_to_all | solution.py:91
  27.9 350.0 %while.21 = (s32[]{:T(128)}, f32[2,192]{1,0:T(2,128)S(1)}, f32[2,192]{1,0:T(2,128)S(1)}, f32[128,2,192]{2,1,0:T(2,128)S(1)}, s32[128]{0:T(128)S(1)}, /*index=5*/...) while((s32[]{:T(128)}, f32[2,192]{1,0:T(2,128)S(1)}, ...), condition=%wide.region_2.3_spmd.clone.clone.clone.clone, body=%wide.region_1.2_spmd.clone.clone.clone.clone.sunk | while | flops 5047 | bytes 17529 | solution.py:57
  379.3 1.3 fusion.38
  380.6 1.4 copy.177
  382.0 29.2 %all_to_all.126 = bf16[128,2,2,1,384]{4,2,1,3,0:T(2,128)(2,1)S(1)} all-to-all(bf16[128,2,2,1,384]{4,2,1,3,0:T(2,128)(2,1)S(1)} %copy.177), channel_id=1, replica_groups=mesh['lat'=64,'batch'=8] {'lat'}, dimensions={0} | all-to-all | bytes 786432 | tf_op jit(solution)/shard_map/all_to_all | solution.py:95
  413.3 20.7 %all_to_all.127 = bf16[2,128,2,1,384]{4,0,3,2,1:T(2,128)(2,1)S(1)} all-to-all(bf16[2,128,2,1,384]{4,0,3,2,1:T(2,128)(2,1)S(1)} %copy.181), channel_id=1, replica_groups=mesh['lat'=64,'batch'=8] {'lat'}, dimensions={1} | all-to-all | bytes 786432 | tf_op jit(solution)/shard_map/all_to_all | solution.py:99
  435.2 1.3 fusion.32
  436.5 1.4 copy.183
  437.9 5.5 all-to-all-start.3
  446.2 16.2 %all-to-all-done.3 = bf16[192,2,2,1,384]{4,2,1,3,0:T(2,128)(2,1)} async-done(((bf16[192,2,2,1,384]{4,2,1,3,0:T(2,128)(2,1)}), bf16[192,2,2,1,384]{4,2,1,3,0:T(2,128)(2,1)}, u32[]{:S(2)}, u32[]{:S(2)}) %all-to-all-start.3) | async-done | bytes 589856 | tf_op jit(solution)/shard_map/all_to_all | solution.py:103
  462.4 1.5 copy.184
  463.9 1.0 reshape.469
  464.9 4.0 fusion.36
  468.9 1.9 reshape.471
  471.2 24.4 %all_to_all.128 = bf16[3,128,2,1,384]{4,2,0,3,1:T(2,128)(2,1)S(1)} all-to-all(bf16[3,128,2,1,384]{4,2,0,3,1:T(2,128)(2,1)S(1)} %copy.186), channel_id=1, replica_groups=mesh['lat'=64,'batch'=8] {'lat'}, dimensions={1} | all-to-all | bytes 1179648 | tf_op jit(solution)/shard_map/all_to_all | solution.py:91
  496.4 1.2 fusion.39
  497.6 1.3 copy.190
  498.9 20.7 %all_to_all.129 = bf16[128,2,2,1,384]{4,2,1,3,0:T(2,128)(2,1)S(1)} all-to-all(bf16[128,2,2,1,384]{4,2,1,3,0:T(2,128)(2,1)S(1)} %copy.190), channel_id=1, replica_groups=mesh['lat'=64,'batch'=8] {'lat'}, dimensions={0} | all-to-all | bytes 786432 | tf_op jit(solution)/shard_map/all_to_all | solution.py:95
  519.7 1.0 copy.191
  520.7 1.1 all_to_all.111
  521.9 1.0 pad_maximum_fusion.1
  524.6 19.7 %all_to_all.130 = bf16[2,128,2,1,384]{4,0,3,2,1:T(2,128)(2,1)S(1)} all-to-all(bf16[2,128,2,1,384]{4,0,3,2,1:T(2,128)(2,1)S(1)} %copy.192), channel_id=1, replica_groups=mesh['lat'=64,'batch'=8] {'lat'}, dimensions={1} | all-to-all | bytes 786432 | tf_op jit(solution)/shard_map/all_to_all | solution.py:99
  545.1 1.4 copy.194
  546.5 4.6 all-to-all-start.7
  551.3 18.0 %all-to-all-done.7 = bf16[192,2,2,1,384]{4,2,1,3,0:T(2,128)(2,1)S(1)} async-done(((bf16[192,2,2,1,384]{4,2,1,3,0:T(2,128)(2,1)}), bf16[192,2,2,1,384]{4,2,1,3,0:T(2,128)(2,1)S(1)}, u32[]{:S(2)}, u32[]{:S(2)}) %all-to-all-start.7) | async-done | bytes 589856 | tf_op jit(solution)/shard_map/all_to_all | solution.py:103
  570.0 2.6 fusion.24
  572.5 3.1 convolution_bitcast_fusion.2
  575.6 2.9 convolution_bitcast_fusion
  578.5 1.0 fusion.34
  579.6 1.0 fusion.35
  580.7 1.1 copy.201
  (967 shorter events, 277.0 us)
Async XLA Ops:
  7.2 1.8 copy-start
  8.3 0.7 copy-start.2
  9.7 368.4 %copy-start.5 = (s32[128]{0:T(128)S(1)}, s32[128]{0:T(128)}, u32[]{:S(2)}) copy-start(s32[128]{0:T(128)} %param.9) | copy-start | bytes 1540
  11.0 367.5 %all-to-all-start = ((bf16[3,128,2,1,384]{4,2,0,3,1:T(2,128)(2,1)}), bf16[3,128,2,1,384]{4,2,0,3,1:T(2,128)(2,1)S(1)}, u32[]{:S(2)}, u32[]{:S(2)}) async-start(bf16[3,128,2,1,384]{4,2,0,3,1:T(2,128)(2,1)} %copy.172), calls=%async_computation | async-start | bytes 1179648 | tf_op jit(solution)/shard_map/all_to_all | solution.py:91
  380.6 31.1 %copy-start.1 = (bf16[2,2,384,384]{3,2,1,0:T(8,128)(2,1)S(1)}, bf16[2,2,384,384]{3,2,1,0:T(8,128)(2,1)}, u32[]{:S(2)}) copy-start(bf16[2,2,384,384]{3,2,1,0:T(8,128)(2,1)} %param.8) | copy-start | bytes 3538948
  437.9 24.5 %all-to-all-start.3 = ((bf16[192,2,2,1,384]{4,2,1,3,0:T(2,128)(2,1)}), bf16[192,2,2,1,384]{4,2,1,3,0:T(2,128)(2,1)}, u32[]{:S(2)}, u32[]{:S(2)}) async-start(bf16[192,2,2,1,384]{4,2,1,3,0:T(2,128)(2,1)} %copy.183), calls=%async_computation.3 | async-start | bytes 1179648 | tf_op jit(solution)/shard_map/all_to_all | solution.py:103
  443.4 129.2 %all-gather.2.cloned.1.call-start = ((), (), s32[]{:S(2)}) async-start(), calls=%async_computation.8 | async-start | bytes 7077888 | tf_op jit(solution)/shard_map/all_gather | solution.py:16
  446.2 18.7 %copy-start.4 = (bf16[384,256]{0,1:T(8,128)(2,1)S(1)}, bf16[384,256]{0,1:T(8,128)(2,1)}, u32[]{:S(2)}) copy-start(bf16[384,256]{0,1:T(8,128)(2,1)} %convert_element_type.174) | copy-start | bytes 589828
  544.7 6.4 %copy-start.3 = (bf16[384,128,2]{0,2,1:T(2,128)(2,1)S(1)}, bf16[384,128,2]{0,2,1:T(2,128)(2,1)}, u32[]{:S(2)}) copy-start(bf16[384,128,2]{0,2,1:T(2,128)(2,1)} %copy-done.2) | copy-start | bytes 589828
  546.5 22.8 %all-to-all-start.7 = ((bf16[192,2,2,1,384]{4,2,1,3,0:T(2,128)(2,1)}), bf16[192,2,2,1,384]{4,2,1,3,0:T(2,128)(2,1)S(1)}, u32[]{:S(2)}, u32[]{:S(2)}) async-start(bf16[192,2,2,1,384]{4,2,1,3,0:T(2,128)(2,1)} %copy.194), calls=%async_computation.7 | async-start | bytes 1179648 | tf_op jit(solution)/shard_map/all_to_all | solution.py:103
  572.5 6.0 %copy-start.6 = (bf16[4,128,2,8,384]{4,1,0,3,2:T(8,128)(2,1)S(1)}, bf16[4,128,2,8,384]{4,1,0,3,2:T(8,128)(2,1)}, u32[]{:S(2)}) copy-start(bf16[4,128,2,8,384]{4,1,0,3,2:T(8,128)(2,1)} %all-gather.2.cloned.1.call-done) | copy-start | bytes 18874372
Sparse Core Ops, SparseCore 0:
  523.0 36.7 all-gather.1
where the time goes:
time: 595 us; the launch traced here: 589 us
  other arithmetic  189 us (32%)
  blocking collectives  115 us (19%)
  local copies, waits for them, and re-layouts  99.9 us (17%)
  loops' own time  87.7 us (15%)
  waiting for transfers between devices  34.3 us (6%)
  starting transfers between devices  26.9 us (5%)
  matrix products  21.9 us (4%)
  between operations  14.5 us (2%)
    another operation x1, loops' own time, legendre_table(): lax.scan(advance, (zeros, zeros), jnp.arange(degree_count, dtype=jnp.int32))  87.7 us
    gt x128, other arithmetic, advance(): degree > order_col + 1  81.7 us
    eq x128, other arithmetic, advance(): degree == order_col  80.8 us
    dynamic_slice x128, local copies, waits for them, and re-layouts, legendre_table(): lax.scan(advance, (zeros, zeros), jnp.arange(degree_count, dtype=jnp.int32))  76.7 us
    all_to_all x2, blocking collectives, to_degrees(): lax.all_to_all(values, 'lat', split_axis=0, concat_axis=1, tiled=True)  50 us
    all_to_all x2, blocking collectives, back_to_orders(): lax.all_to_all(values, 'lat', split_axis=1, concat_axis=0, tiled=True)  40.3 us
    all_to_all x2, waiting for transfers between devices, to_bands(): lax.all_to_all(values, 'lat', split_axis=0, concat_axis=1, tiled=True)  34.3 us
    all_to_all x1, blocking collectives, to_orders(): lax.all_to_all(values, 'lat', split_axis=1, concat_axis=0, tiled=True)  24.4 us
  transfers between devices with their start and end apart: 4, of which 2 were waited for; matrix products, arithmetic and copies ran while one was open for 46% of the time, Pallas kernels for 0%

commit v1 on v0

--- a/solution.py
+++ b/solution.py
@@ -1,5 +1,6 @@
 import jax
 import jax.numpy as jnp
+import numpy as np
 from jax import lax
 from jax.sharding import PartitionSpec as P
 
@@ -17,59 +18,40 @@
     return tuple(jnp.split(out, [sum(widths[:k]) for k in range(1, len(widths))], axis=along))
 
 
-def legendre_table(order_ids, lat_count, degree_count):
-    colatitude = jnp.pi * (jnp.arange(lat_count, dtype=jnp.float32) + 0.5) / lat_count
-    cosine = jnp.cos(colatitude)[None, :]
-    log_sine = jnp.log(jnp.sin(colatitude))[None, :]
-    order_col = order_ids[:, None]
-    order_real = order_col.astype(jnp.float32)
-    steps_up = jnp.arange(1, degree_count + 1, dtype=jnp.float32)[None, :]
-    factor = jnp.where(
-        steps_up <= order_real, 0.5 * jnp.log((2.0 * steps_up + 1.0) / (2.0 * steps_up)), 0.0
-    )
-    log_start = 0.5 * jnp.log(1.0 / (4.0 * jnp.pi)) + jnp.sum(factor, axis=1, keepdims=True)
-    diagonal = jnp.exp(log_start + order_real * log_sine)
-    squared = order_real * order_real
-
-    def advance(carry, degree):
-        previous, older = carry
-        degree_real = degree.astype(jnp.float32)
-        lead = jnp.sqrt(
-            jnp.maximum(4.0 * degree_real * degree_real - 1.0, 0.0)
-            / jnp.maximum(degree_real * degree_real - squared, 1.0)
-        )
-        lower = degree_real - 1.0
-        back = jnp.sqrt(
-            jnp.maximum(lower * lower - squared, 0.0) / jnp.maximum(4.0 * lower * lower - 1.0, 1.0)
-        )
-        general = lead * (cosine * previous - back * older)
-        first = jnp.sqrt(2.0 * order_real + 3.0) * cosine * previous
-        value = jnp.where(
-            degree == order_col,
-            diagonal,
-            jnp.where(
-                degree == order_col + 1, first, jnp.where(degree > order_col + 1, general, 0.0)
-            ),
-        )
-        return ((value, previous), value)
-
-    zeros = jnp.zeros((order_ids.shape[0], lat_count), jnp.float32)
-    final_state, table = lax.scan(
-        advance, (zeros, zeros), jnp.arange(degree_count, dtype=jnp.int32)
-    )
-    return jnp.transpose(table, (1, 0, 2))
+def legendre_table():
+    colatitude = np.pi * (np.arange(LATS) + 0.5) / LATS
+    cosine, sine = np.cos(colatitude), np.sin(colatitude)
+    order = np.arange(ORDERS, dtype=np.float64)[:, None]
+    steps = np.arange(1, ORDERS)
+    growth = np.concatenate([[0.0], np.cumsum(0.5 * np.log((2.0 * steps + 1.0) / (2.0 * steps)))])
+    diagonal = np.exp(0.5 * np.log(1.0 / (4.0 * np.pi)) + growth[:, None] + order * np.log(sine))
+    table = np.zeros((ORDERS, DEGREES, LATS))
+    for degree in range(DEGREES):
+        table[degree, degree] = diagonal[degree]
+        if degree >= 1:
+            m = degree - 1
+            table[m, degree] = np.sqrt(2.0 * m + 3.0) * cosine * table[m, m]
+        if degree >= 2:
+            m = order[: degree - 1]
+            lead = np.sqrt((4.0 * degree**2 - 1.0) / (degree**2 - m**2))
+            back = np.sqrt(((degree - 1.0) ** 2 - m**2) / (4.0 * (degree - 1.0) ** 2 - 1.0))
+            table[: degree - 1, degree] = lead * (
+                cosine * table[: degree - 1, degree - 1] - back * table[: degree - 1, degree - 2]
+            )
+    return table, 2.0 * np.pi * np.pi / LATS * sine
 
 
 def spectral_tables(start, ord_dev, degree_of):
-    order_ids = start + jnp.arange(ord_dev, dtype=jnp.int32)
-    mine = legendre_table(order_ids, LATS, DEGREES)
+    table, quadrature = legendre_table()
+    both = jnp.asarray(np.stack([table * quadrature, table], axis=1).astype(jnp.bfloat16))
+    mine = lax.dynamic_slice_in_dim(both, start, ord_dev, 0)
     selector = (degree_of[:, None] == jnp.arange(DEGREES, dtype=jnp.int32)[None, :]).astype(
-        jnp.float32
+        jnp.bfloat16
     )
-    chosen = jnp.einsum("mli,jl->mji", mine, selector, precision=lax.Precision.HIGHEST)
-    colatitude = jnp.pi * (jnp.arange(LATS, dtype=jnp.float32) + 0.5) / LATS
-    quadrature = 2.0 * jnp.pi * jnp.pi / LATS * jnp.sin(colatitude)
-    return ((chosen * quadrature[None, None, :]).astype(jnp.bfloat16), chosen.astype(jnp.bfloat16))
+    chosen = jnp.einsum(
+        "mpli,jl->pmji", mine, selector, preferred_element_type=jnp.float32
+    ).astype(jnp.bfloat16)
+    return (chosen[0], chosen[1])
 
 
 def fourier_tables(lon_count, order_count):

time: 595 us -> 248 us (0.42)
  other arithmetic: 189 us -> 3.61 us
  loops' own time: 87.7 us -> 0 us
  local copies, waits for them, and re-layouts: 99.9 us -> 25.2 us
  waiting for transfers between devices: 34.3 us -> 50.5 us
  blocking collectives: 115 us -> 107 us
    another operation x1 -> x0, loops' own time: 87.7 us -> none  [legendre_table(): lax.scan(advance, (zeros, zeros), jnp.arange(degree_count, dtype=jnp.int32))]
    gt x128 -> x0, other arithmetic: 81.7 us -> none  [advance(): degree > order_col + 1]
    eq x128 -> x0, other arithmetic: 80.8 us -> none  [advance(): degree == order_col]
    dynamic_slice x128 -> x0, local copies, waits for them, and re-layouts: 76.7 us -> none  [legendre_table(): lax.scan(advance, (zeros, zeros), jnp.arange(degree_count, dtype=jnp.int32))]
    all_to_all x1, waiting for transfers between devices: 0.01 us -> 19.7 us  [to_orders(): lax.all_to_all(values, 'lat', split_axis=1, concat_axis=0, tiled=True)]
    dynamic_update_slice x128 -> x0, other arithmetic: 11.9 us -> none  [legendre_table(): lax.scan(advance, (zeros, zeros), jnp.arange(degree_count, dtype=jnp.int32))]
    all_to_all x2, blocking collectives: 50 us -> 42.3 us  [to_degrees(): lax.all_to_all(values, 'lat', split_axis=0, concat_axis=1, tiled=True)]
    cos x128 -> x0, other arithmetic: 7.34 us -> none  [legendre_table(): cosine = jnp.cos(colatitude)[None, :]]
  transfers between devices with their start and end apart: 4 -> 4, of which waited for: 2 -> 3; matrix products, arithmetic and copies ran while one was open for 46% -> 6% of each run, Pallas kernels for 0% -> 0%
where the time goes in v1:
time: 248 us; the launch traced here: 247 us
  blocking collectives  107 us (43%)
  waiting for transfers between devices  50.5 us (20%)
  starting transfers between devices  26.1 us (11%)
  local copies, waits for them, and re-layouts  25.2 us (10%)
  matrix products  20 us (8%)
  between operations  14.4 us (6%)
  other arithmetic  3.61 us (1%)
    all_to_all x2, blocking collectives, to_degrees(): lax.all_to_all(values, 'lat', split_axis=0, concat_axis=1, tiled=True)  42.3 us
    all_to_all x2, blocking collectives, back_to_orders(): lax.all_to_all(values, 'lat', split_axis=1, concat_axis=0, tiled=True)  40.3 us
    all_to_all x2, waiting for transfers between devices, to_bands(): lax.all_to_all(values, 'lat', split_axis=0, concat_axis=1, tiled=True)  30.8 us
    all_to_all x1, blocking collectives, to_orders(): lax.all_to_all(values, 'lat', split_axis=1, concat_axis=0, tiled=True)  24.5 us
    all_to_all x1, waiting for transfers between devices, to_orders(): lax.all_to_all(values, 'lat', split_axis=1, concat_axis=0, tiled=True)  19.7 us
    dot_general x19, matrix products, product(): return jnp.einsum(spec, left, right, preferred_element_type=jnp.float32)  18.7 us
    all_to_all x1, starting transfers between devices, to_orders(): lax.all_to_all(values, 'lat', split_axis=1, concat_axis=0, tiled=True)  16.6 us
    all_to_all x2, starting transfers between devices, to_bands(): lax.all_to_all(values, 'lat', split_axis=0, concat_axis=1, tiled=True)  9.27 us
  transfers between devices with their start and end apart: 4, of which 3 were waited for; matrix products, arithmetic and copies ran while one was open for 6% of the time, Pallas kernels for 0%

profile of v1, /device:TPU:6, one launch (start us, length us, event | category | flops | bytes accessed | tf_op | source)
XLA Modules:
  0.0 246.9 jit_solution(14235454149436628634)
XLA Ops:
  9.1 1.2 copy.138
  10.3 16.6 %all-to-all-start = ((bf16[3,128,2,1,384]{4,2,0,3,1:T(2,128)(2,1)}), bf16[3,128,2,1,384]{4,2,0,3,1:T(2,128)(2,1)S(1)}, u32[]{:S(2)}, u32[]{:S(2)}) async-start(bf16[3,128,2,1,384]{4,2,0,3,1:T(2,128)(2,1)} %copy.138), calls=%async_computation | async-start | bytes 1179648 | tf_op jit(solution)/shard_map/all_to_all | solution.py:73
  26.9 1.2 fusion.30
  28.1 19.7 %all-to-all-done = bf16[3,128,2,1,384]{4,2,0,3,1:T(2,128)(2,1)S(1)} async-done(((bf16[3,128,2,1,384]{4,2,0,3,1:T(2,128)(2,1)}), bf16[3,128,2,1,384]{4,2,0,3,1:T(2,128)(2,1)S(1)}, u32[]{:S(2)}, u32[]{:S(2)}) %all-to-all-start) | async-done | bytes 589856 | tf_op jit(solution)/shard_map/all_to_all | solution.py:73
  49.6 21.4 %all_to_all.126 = bf16[128,2,2,1,384]{4,2,1,3,0:T(2,128)(2,1)S(1)} all-to-all(bf16[128,2,2,1,384]{4,2,1,3,0:T(2,128)(2,1)S(1)} %copy.142), channel_id=1, replica_groups=mesh['lat'=64,'batch'=8] {'lat'}, dimensions={0} | all-to-all | bytes 786432 | tf_op jit(solution)/shard_map/all_to_all | solution.py:77
  73.1 20.6 %all_to_all.127 = bf16[2,128,2,1,384]{4,0,3,2,1:T(2,128)(2,1)S(1)} all-to-all(bf16[2,128,2,1,384]{4,0,3,2,1:T(2,128)(2,1)S(1)} %copy.146), channel_id=1, replica_groups=mesh['lat'=64,'batch'=8] {'lat'}, dimensions={1} | all-to-all | bytes 786432 | tf_op jit(solution)/shard_map/all_to_all | solution.py:81
  94.9 1.3 fusion.18
  96.2 1.4 copy.148
  97.6 4.6 %all-to-all-start.3 = ((bf16[192,2,2,1,384]{4,2,1,3,0:T(2,128)(2,1)}), bf16[192,2,2,1,384]{4,2,1,3,0:T(2,128)(2,1)S(1)}, u32[]{:S(2)}, u32[]{:S(2)}) async-start(bf16[192,2,2,1,384]{4,2,1,3,0:T(2,128)(2,1)} %copy.148), calls=%async_computation.3 | async-start | bytes 1179648 | tf_op jit(solution)/shard_map/all_to_all | solution.py:85
  104.0 1.8 copy.137
  105.8 1.7 convert_element_type.143
  107.5 1.7 reshape.332
  109.2 12.7 %all-to-all-done.3 = bf16[192,2,2,1,384]{4,2,1,3,0:T(2,128)(2,1)S(1)} async-done(((bf16[192,2,2,1,384]{4,2,1,3,0:T(2,128)(2,1)}), bf16[192,2,2,1,384]{4,2,1,3,0:T(2,128)(2,1)S(1)}, u32[]{:S(2)}, u32[]{:S(2)}) %all-to-all-start.3) | async-done | bytes 589856 | tf_op jit(solution)/shard_map/all_to_all | solution.py:85
  121.9 1.2 copy.149
  123.1 2.0 reshape.319
  125.1 3.9 %fusion.22 = bf16[3,256,1,384]{3,1,0,2:T(8,128)(2,1)} fusion(bf16[384,256,1]{0,1,2:T(8,128)(2,1)} %reshape.332, bf16[3,256,384]{2,1,0:T(8,128)(2,1)S(1)} %reshape.319, bf16[1,3,384,384]{3,2,1,0:T(8,128)(2,1)} %param.6, bf16[384,256]{0,1:T(8,128)(2,1)} %convert_element_type.143), kind=kOutput, calls=%fused_computation.38 | convolution fusion | flops 462569472 | bytes 2457600 | tf_op jit(solution)/shard_map/sikc,fk->ifsc/dot_general | solution.py:89
  129.0 1.9 reshape.321
  131.3 24.5 %all_to_all.128 = bf16[3,128,2,1,384]{4,2,0,3,1:T(2,128)(2,1)S(1)} all-to-all(bf16[3,128,2,1,384]{4,2,0,3,1:T(2,128)(2,1)S(1)} %copy.151), channel_id=1, replica_groups=mesh['lat'=64,'batch'=8] {'lat'}, dimensions={1} | all-to-all | bytes 1179648 | tf_op jit(solution)/shard_map/all_to_all | solution.py:73
  157.1 1.1 copy.155
  158.1 20.9 %all_to_all.129 = bf16[128,2,2,1,384]{4,2,1,3,0:T(2,128)(2,1)S(1)} all-to-all(bf16[128,2,2,1,384]{4,2,1,3,0:T(2,128)(2,1)} %copy.155), channel_id=1, replica_groups=mesh['lat'=64,'batch'=8] {'lat'}, dimensions={0} | all-to-all | bytes 786432 | tf_op jit(solution)/shard_map/all_to_all | solution.py:77
  179.1 1.0 copy.156
  180.1 1.1 all_to_all.111
  184.1 19.7 %all_to_all.130 = bf16[2,128,2,1,384]{4,0,3,2,1:T(2,128)(2,1)S(1)} all-to-all(bf16[2,128,2,1,384]{4,0,3,2,1:T(2,128)(2,1)S(1)} %copy.157), channel_id=1, replica_groups=mesh['lat'=64,'batch'=8] {'lat'}, dimensions={1} | all-to-all | bytes 786432 | tf_op jit(solution)/shard_map/all_to_all | solution.py:81
  204.5 1.4 copy.159
  205.9 4.6 %all-to-all-start.7 = ((bf16[192,2,2,1,384]{4,2,1,3,0:T(2,128)(2,1)}), bf16[192,2,2,1,384]{4,2,1,3,0:T(2,128)(2,1)S(1)}, u32[]{:S(2)}, u32[]{:S(2)}) async-start(bf16[192,2,2,1,384]{4,2,1,3,0:T(2,128)(2,1)} %copy.159), calls=%async_computation.7 | async-start | bytes 1179648 | tf_op jit(solution)/shard_map/all_to_all | solution.py:85
  210.6 18.0 %all-to-all-done.7 = bf16[192,2,2,1,384]{4,2,1,3,0:T(2,128)(2,1)S(1)} async-done(((bf16[192,2,2,1,384]{4,2,1,3,0:T(2,128)(2,1)}), bf16[192,2,2,1,384]{4,2,1,3,0:T(2,128)(2,1)S(1)}, u32[]{:S(2)}, u32[]{:S(2)}) %all-to-all-start.7) | async-done | bytes 589856 | tf_op jit(solution)/shard_map/all_to_all | solution.py:85
  229.3 1.4 fusion.10
  230.7 3.1 %convolution_bitcast_fusion.2 = f32[2,384,384]{2,1,0:T(8,128)S(1)} fusion(bf16[4,128,2,8,384]{4,1,0,3,2:T(8,128)(2,1)} %all-gather.2.cloned.1.call-done), kind=kOutput, calls=%fused_computation.22 | convolution fusion | flops 603979776 | bytes 4325376 | tf_op jit(solution)/shard_map/jmsc,jmsd->jcd/dot_general | solution.py:89
  233.8 2.9 %convolution_bitcast_fusion = f32[2,384,384]{2,1,0:T(8,128)S(1)} fusion(bf16[4,128,2,8,384]{4,1,0,3,2:T(8,128)(2,1)} %all-gather.2.cloned.1.call-done), kind=kOutput, calls=%fused_computation.20 | convolution fusion | flops 603979776 | bytes 4325376 | tf_op jit(solution)/shard_map/jmsc,jmsd->jcd/dot_general | solution.py:89
  236.7 1.0 fusion.20
  237.8 1.0 fusion.21
  238.9 1.1 copy.166
  (55 shorter events, 14.5 us)
Async XLA Ops:
  7.2 1.2 copy-start
  8.8 18.1 %copy-start.3 = (s32[128]{0:T(128)S(1)}, s32[128]{0:T(128)}, u32[]{:S(2)}) copy-start(s32[128]{0:T(128)} %param.8) | copy-start | bytes 1540
  10.3 37.6 %all-to-all-start = ((bf16[3,128,2,1,384]{4,2,0,3,1:T(2,128)(2,1)}), bf16[3,128,2,1,384]{4,2,0,3,1:T(2,128)(2,1)S(1)}, u32[]{:S(2)}, u32[]{:S(2)}) async-start(bf16[3,128,2,1,384]{4,2,0,3,1:T(2,128)(2,1)} %copy.138), calls=%async_computation | async-start | bytes 1179648 | tf_op jit(solution)/shard_map/all_to_all | solution.py:73
  49.2 22.3 %copy-start.1 = (bf16[2,2,384,384]{3,2,1,0:T(8,128)(2,1)S(1)}, bf16[2,2,384,384]{3,2,1,0:T(8,128)(2,1)}, u32[]{:S(2)}) copy-start(bf16[2,2,384,384]{3,2,1,0:T(8,128)(2,1)} %param.7) | copy-start | bytes 3538948
  97.6 24.3 %all-to-all-start.3 = ((bf16[192,2,2,1,384]{4,2,1,3,0:T(2,128)(2,1)}), bf16[192,2,2,1,384]{4,2,1,3,0:T(2,128)(2,1)S(1)}, u32[]{:S(2)}, u32[]{:S(2)}) async-start(bf16[192,2,2,1,384]{4,2,1,3,0:T(2,128)(2,1)} %copy.148), calls=%async_computation.3 | async-start | bytes 1179648 | tf_op jit(solution)/shard_map/all_to_all | solution.py:85
  102.3 128.5 %all-gather.2.cloned.1.call-start = ((), (), s32[]{:S(2)}) async-start(), calls=%async_computation.8 | async-start | bytes 7077888 | tf_op jit(solution)/shard_map/all_gather | solution.py:17
  205.9 22.8 %all-to-all-start.7 = ((bf16[192,2,2,1,384]{4,2,1,3,0:T(2,128)(2,1)}), bf16[192,2,2,1,384]{4,2,1,3,0:T(2,128)(2,1)S(1)}, u32[]{:S(2)}, u32[]{:S(2)}) async-start(bf16[192,2,2,1,384]{4,2,1,3,0:T(2,128)(2,1)} %copy.159), calls=%async_computation.7 | async-start | bytes 1179648 | tf_op jit(solution)/shard_map/all_to_all | solution.py:85
  210.6 18.8 %copy-start.2 = (bf16[1,3,384,384]{3,2,1,0:T(8,128)(2,1)S(1)}, bf16[1,3,384,384]{3,2,1,0:T(8,128)(2,1)}, u32[]{:S(2)}) copy-start(bf16[1,3,384,384]{3,2,1,0:T(8,128)(2,1)} %param.6) | copy-start | bytes 2654212
  230.7 6.0 %copy-start.4 = (bf16[4,128,2,8,384]{4,1,0,3,2:T(8,128)(2,1)S(1)}, bf16[4,128,2,8,384]{4,1,0,3,2:T(8,128)(2,1)}, u32[]{:S(2)}) copy-start(bf16[4,128,2,8,384]{4,1,0,3,2:T(8,128)(2,1)} %all-gather.2.cloned.1.call-done) | copy-start | bytes 18874372
Sparse Core Ops, SparseCore 0:
  182.4 36.8 all-gather.1

commit v2 on v1

v2 whole, which is shorter than its diff:
```python
import functools

import jax
import jax.numpy as jnp
import numpy as np
from jax import lax
from jax.experimental import pallas as pl
from jax.experimental.pallas import tpu as pltpu
from jax.sharding import PartitionSpec as P

LATS = 192
LONS = 384
ORDERS = 128
DEGREES = 128
CHANNELS = 384

GROUPS = 64
BAND = LATS // GROUPS
PARTS = CHANNELS // GROUPS
SLOTS = DEGREES // GROUPS
COEFS = 2 * ORDERS
BLOCKS = ORDERS // 16
SPEC_ROWS = BAND * PARTS * 2
FIRST_ROWS = 96
SLOT_ROWS = SLOTS * PARTS * 2
LAST_ROWS = 40
REACH = [DEGREES - 16 * t for t in range(BLOCKS)]
STARTS = [16 * sum(REACH[:t]) for t in range(BLOCKS + 1)]
PAIR_ROWS = 8 * LATS

f32 = jnp.float32
bf16 = jnp.bfloat16
TN = (((0,), (0,)), ((), ()))
NN = (((1,), (0,)), ((), ()))
NT = (((1,), (1,)), ((), ()))


def legendre_table():
    colatitude = np.pi * (np.arange(LATS) + 0.5) / LATS
    cosine, sine = np.cos(colatitude), np.sin(colatitude)
    order = np.arange(ORDERS, dtype=np.float64)[:, None]
    steps = np.arange(1, ORDERS)
    growth = np.concatenate([[0.0], np.cumsum(0.5 * np.log((2.0 * steps + 1.0) / (2.0 * steps)))])
    diagonal = np.exp(0.5 * np.log(1.0 / (4.0 * np.pi)) + growth[:, None] + order * np.log(sine))
    table = np.zeros((ORDERS, DEGREES, LATS))
    for degree in range(DEGREES):
        table[degree, degree] = diagonal[degree]
        if degree >= 1:
            m = degree - 1
            table[m, degree] = np.sqrt(2.0 * m + 3.0) * cosine * table[m, m]
        if degree >= 2:
            m = order[: degree - 1]
            lead = np.sqrt((4.0 * degree**2 - 1.0) / (degree**2 - m**2))
            back = np.sqrt(((degree - 1.0) ** 2 - m**2) / (4.0 * (degree - 1.0) ** 2 - 1.0))
            table[: degree - 1, degree] = lead * (
                cosine * table[: degree - 1, degree - 1] - back * table[: degree - 1, degree - 2]
            )
    return table, 2.0 * np.pi * np.pi / LATS * sine


def fourier_tables():
    lon = np.arange(LONS)[:, None]
    order = np.arange(ORDERS)[None, :]
    phase = 2.0 * np.pi * (lon * order % LONS) / LONS
    forward = np.stack([np.cos(phase), -np.sin(phase)], axis=2).reshape(LONS, COEFS) / LONS
    doubled = np.where(order == 0, 1.0, 2.0)
    inverse = np.stack([doubled * np.cos(phase), -doubled * np.sin(phase)], axis=2)
    return forward.astype(bf16), inverse.reshape(LONS, COEFS).astype(bf16)


@functools.cache
def constants():
    table, quadrature = legendre_table()
    where = np.arange(LATS).reshape(GROUPS, BAND).T.reshape(-1)
    table = table[:, :, where].astype(bf16)
    analysis = np.concatenate(
        [table[16 * t + k, 16 * t :] for t in range(BLOCKS) for k in range(16)], axis=0
    )
    synthesis = np.concatenate(
        [
            np.concatenate([table[16 * t + k].T, table[16 * t + k + 8].T], axis=1)
            for t in range(BLOCKS)
            for k in range(8)
        ],
        axis=0,
    )
    forward, inverse = fourier_tables()
    turn = np.zeros((COEFS, COEFS), np.float32)
    even = np.arange(0, COEFS, 2)
    turn[even + 1, even] = -1.0
    turn[even, even + 1] = 1.0
    return dict(
        analysis=analysis,
        synthesis=synthesis,
        forward=forward,
        inverse=inverse,
        inverse_t=np.ascontiguousarray(inverse.T),
        turn=turn.astype(bf16),
        weight=quadrature.astype(np.float32),
        weight_rows=quadrature[where].astype(np.float32)[:, None],
    )


def dot(left, right, dims=NN):
    return lax.dot_general(left, right, dims, preferred_element_type=f32)


def lane_of(shape):
    return lax.broadcasted_iota(jnp.int32, shape, 1)


def join(pieces, lanes):
    rolled = [pltpu.roll(x, s % 128, 1) if s % 128 else x for x, s in pieces]
    left = jnp.where(lanes < 32, rolled[0], rolled[1])
    right = jnp.where(lanes < 96, rolled[2], rolled[3])
    return jnp.where(lanes < 64, left, right)


def join_two(first, shift_first, second, shift_second, lanes):
    a = pltpu.roll(first, shift_first % 128, 1) if shift_first % 128 else first
    b = pltpu.roll(second, shift_second % 128, 1) if shift_second % 128 else second
    return jnp.where(lanes < 64, a, b)


def to_tiles(parts):
    lanes = lane_of(parts[0][0].shape)
    tiles = []
    for pair in range(BLOCKS // 2):
        h, at = pair // 2, 64 * (pair % 2)
        x = [parts[q][h] for q in range(PARTS)]
        a = join([(x[s], 32 * s - at) for s in range(4)], lanes)
        c = join([(x[s], 32 * s - at - 32) for s in range(4)], lanes)
        b = join_two(x[4], -at, x[5], 64 - at, lanes)
        tiles.append((a, b, c))
    return tiles


def from_tiles(tiles):
    lanes = lane_of(tiles[0][0].shape)
    parts = []
    for q in range(4):
        halves = []
        for h in range(2):
            pieces = []
            for k in range(4):
                a, _, c = tiles[2 * h + k // 2]
                pieces.append((c if k % 2 else a, 32 * (k - q)))
            halves.append(join(pieces, lanes))
        parts.append(halves)
    parts.append([join_two(tiles[2 * h][1], 0, tiles[2 * h + 1][1], 64, lanes) for h in range(2)])
    parts.append([join_two(tiles[2 * h][1], 64, tiles[2 * h + 1][1], 0, lanes) for h in range(2)])
    return parts


def as_bf16(tiles):
    return [tuple(x.astype(bf16) for x in tile) for tile in tiles]


def block_operand(tiles, t):
    a, b, c = tiles[t // 2]
    return jnp.concatenate([c if t % 2 else a, b], axis=1)


def merge_blocks(sums):
    tiles = []
    for pair in range(BLOCKS // 2):
        one, two = sums[2 * pair], sums[2 * pair + 1]
        lanes = lane_of((one.shape[0], 128))
        b = jnp.where((lanes // 32) % 2 == 0, one[:, 128:], two[:, 128:])
        tiles.append((one[:, :128], b, two[:, :128]))
    return tiles


def analyse(tiles, table, ready, rows_each=4):
    sums = []
    for t in range(BLOCKS):
        ready(t)
        operand = block_operand(tiles, t)
        reach = REACH[t]
        order = (lane_of((reach, 256)) % 32) // 2
        total = jnp.zeros((reach, 256), f32)
        for k in range(0, 16, rows_each):
            part = dot(table[pl.ds(STARTS[t] + k * reach, rows_each * reach), :], operand)
            for n in range(rows_each):
                total = jnp.where(order == k + n, part[n * reach : (n + 1) * reach], total)
        if t:
            total = jnp.concatenate([jnp.zeros((16 * t, 256), f32), total], axis=0)
        sums.append(total)
    return merge_blocks(sums)


def synthesise(tiles, table, ready, rows_each=2):
    sums = []
    for t in range(BLOCKS):
        ready(t)
        operand = block_operand(tiles, t)
        low = (lane_of((DEGREES, 256)) % 32) < 16
        none = jnp.zeros_like(operand)
        stacked = jnp.concatenate(
            [jnp.where(low, operand, none), jnp.where(low, none, operand)], axis=0
        )
        order = (lane_of((LATS, 256)) % 16) // 2
        total = jnp.zeros((LATS, 256), f32)
        for k in range(0, 8, rows_each):
            part = dot(table[pl.ds(t * PAIR_ROWS + k * LATS, rows_each * LATS), :], stacked)
            for n in range(rows_each):
                total = jnp.where(order == k + n, part[n * LATS : (n + 1) * LATS], total)
        sums.append(total)
    return merge_blocks(sums)


def permute_rows(matrix, tiles):
    out = []
    for tile in tiles:
        moved = dot(matrix, jnp.concatenate(tile, axis=1))
        out.append(tuple(moved[:, 128 * n : 128 * (n + 1)] for n in range(3)))
    return out


def slot_rows_out(tiles, degree_col, stage, out):
    pick = (degree_col[...] == lane_of((DEGREES, DEGREES))).astype(f32).astype(bf16)
    parts = from_tiles(permute_rows(pick, as_bf16(tiles)))
    for j in range(SLOTS):
        for q in range(PARTS):
            for h in range(2):
                stage[pl.ds((j * PARTS + q) * 2 + h, GROUPS, stride=SLOT_ROWS), :] = parts[q][h][
                    j * GROUPS : (j + 1) * GROUPS
                ]
    out[...] = stage[...].astype(bf16)


def slot_rows_in(received, degree_row, stage):
    stage[...] = received[...].astype(f32)
    parts = [
        [
            jnp.concatenate(
                [
                    stage[pl.ds((j * PARTS + q) * 2 + h, GROUPS, stride=SLOT_ROWS), :]
                    for j in range(SLOTS)
                ],
                axis=0,
            )
            for h in range(2)
        ]
        for q in range(PARTS)
    ]
    rows = lax.broadcasted_iota(jnp.int32, (DEGREES, DEGREES), 0)
    pick = (rows == degree_row[...]).astype(f32).astype(bf16)
    return as_bf16(permute_rows(pick, as_bf16(to_tiles(parts))))


def table_copies(source, target, sems, bounds):
    copies = []
    for t in range(BLOCKS):
        rows = pl.ds(bounds[t], bounds[t + 1] - bounds[t])
        copies.append(pltpu.make_async_copy(source.at[rows, :], target.at[rows, :], sems.at[t]))
    return copies


PAIR_STARTS = [PAIR_ROWS * t for t in range(BLOCKS + 1)]


def spread_kernel(fields, cotangent, forward, scale, out, stage):
    for i in range(BAND):
        spectra = dot(fields[i], forward[...], TN) * scale[i]
        turned = jnp.transpose(cotangent[i].astype(f32))
        for q in range(PARTS):
            rows = slice(q * GROUPS, (q + 1) * GROUPS)
            at = (i * PARTS + q) * 2
            for h in range(2):
                stage[pl.ds(at + h, GROUPS, stride=FIRST_ROWS), :] = spectra[
                    rows, 128 * h : 128 * (h + 1)
                ]
            at = SPEC_ROWS + (i * PARTS + q) * 3
            for h in range(3):
                stage[pl.ds(at + h, GROUPS, stride=FIRST_ROWS), :] = turned[
                    rows, 128 * h : 128 * (h + 1)
                ]
    for row in range(SPEC_ROWS + BAND * PARTS * 3, FIRST_ROWS):
        stage[pl.ds(row, GROUPS, stride=FIRST_ROWS), :] = jnp.zeros((GROUPS, 128), f32)
    out[...] = stage[...].astype(bf16)


def first_kernel(received, analysis, degree_col, out, rows, stage_in, stage, table, row_sem, sems):
    copies = table_copies(analysis, table, sems, STARTS)
    fetch = pltpu.make_async_copy(received.at[:, pl.ds(0, 48), :], rows, row_sem)
    fetch.start()
    for copy in copies:
        copy.start()
    fetch.wait()
    stage_in[...] = rows[...].astype(f32).reshape(GROUPS * 48, 128)
    parts = [
        [
            jnp.concatenate(
                [
                    stage_in[pl.ds((i * PARTS + q) * 2 + h, GROUPS, stride=48), :]
                    for i in range(BAND)
                ],
                axis=0,
            )
            for h in range(2)
        ]
        for q in range(PARTS)
    ]
    tiles = as_bf16(to_tiles(parts))
    sums = analyse(tiles, table, lambda t: copies[t].wait())
    slot_rows_out(sums, degree_col, stage, out)


def gelu_slope(x):
    c = np.float32(np.sqrt(2.0 / np.pi))
    squared = x * x
    th = jnp.tanh(c * (x + 0.044715 * (x * squared)))
    return 0.5 * (1.0 + th) + (0.5 * c) * x * (1.0 - th * th) * (1.0 + (3 * 0.044715) * squared)


def middle_kernel(
    received, cotangents, analysis, synthesis, degree_row, degree_col, inverse, inverse_t, out,
    rows, stage_in, stage, table, table_s, row_sem, sems, sems_s,
):
    copies_s = table_copies(synthesis, table_s, sems_s, PAIR_STARTS)
    copies = table_copies(analysis, table, sems, STARTS)
    fetch = pltpu.make_async_copy(cotangents.at[:, pl.ds(32, 64), :], rows, row_sem)
    for copy in copies_s:
        copy.start()
    fetch.start()
    for copy in copies:
        copy.start()
    tiles = slot_rows_in(received, degree_row, stage)
    synth = from_tiles(synthesise(tiles, table_s, lambda t: copies_s[t].wait()))
    fetch.wait()
    stage_in[...] = rows[...].astype(f32).reshape(GROUPS * 64, 128)
    parts = []
    for q in range(PARTS):
        response = dot(jnp.concatenate(synth[q], axis=1).astype(bf16), inverse_t[...])
        cotangent = jnp.concatenate(
            [
                jnp.concatenate(
                    [
                        stage_in[
                            pl.ds(SPEC_ROWS - 32 + (i * PARTS + q) * 3 + h, GROUPS, stride=64), :
                        ]
                        for h in range(3)
                    ],
                    axis=1,
                )
                for i in range(BAND)
            ],
            axis=0,
        )
        upstream = (cotangent * gelu_slope(response)).astype(bf16)
        grad = dot(upstream, inverse[...])
        parts.append([grad[:, :128], grad[:, 128:]])
    sums = analyse(as_bf16(to_tiles(parts)), table, lambda t: copies[t].wait())
    slot_rows_out(sums, degree_col, stage, out)


def last_kernel(received, synthesis, degree_row, weight_rows, out, stage, stage_out, table_s, sems_s):
    copies_s = table_copies(synthesis, table_s, sems_s, PAIR_STARTS)
    for copy in copies_s:
        copy.start()
    tiles = slot_rows_in(received, degree_row, stage)
    synth = from_tiles(synthesise(tiles, table_s, lambda t: copies_s[t].wait()))
    for q in range(PARTS):
        for h in range(2):
            scaled = synth[q][h] * weight_rows[...]
            for i in range(BAND):
                at = (i * PARTS + q) * 2 + h
                stage_out[pl.ds(at, GROUPS, stride=LAST_ROWS), :] = scaled[
                    i * GROUPS : (i + 1) * GROUPS
                ]
    for row in range(SPEC_ROWS, LAST_ROWS):
        stage_out[pl.ds(row, GROUPS, stride=LAST_ROWS), :] = jnp.zeros((GROUPS, 128), f32)
    out[...] = stage_out[...].astype(bf16)


def gather_kernel(received, forward, cotangent, out, stage):
    stage[...] = received[...].astype(f32)
    for i in range(BAND):
        halves = [
            jnp.concatenate(
                [
                    stage[pl.ds((i * PARTS + q) * 2 + h, GROUPS, stride=LAST_ROWS), :]
                    for q in range(PARTS)
                ],
                axis=0,
            )
            for h in range(2)
        ]
        rows = jnp.concatenate(halves, axis=1).astype(bf16)
        delta = dot(forward[...], rows, NT)
        out[i] = (cotangent[i].astype(f32) + delta).astype(bf16)


def mix_kernel(adjoint, received, weights, turn, out, kept, stage):
    stage[...] = received[...].astype(f32)
    results = []
    for j in range(SLOTS):
        halves = [
            jnp.concatenate(
                [
                    stage[pl.ds((j * PARTS + q) * 2 + h, GROUPS, stride=SLOT_ROWS), :]
                    for q in range(PARTS)
                ],
                axis=0,
            )
            for h in range(2)
        ]
        held = jnp.concatenate(halves, axis=1).astype(bf16)
        kept[j] = held
        turned = dot(held, turn[...])
        if adjoint:
            turned = -turned
        turned = turned.astype(bf16)
        results.append(dot(weights[j, 0], held) + dot(weights[j, 1], turned))
    for j in range(SLOTS):
        for q in range(PARTS):
            for h in range(2):
                stage[pl.ds((j * PARTS + q) * 2 + h, GROUPS, stride=SLOT_ROWS), :] = results[j][
                    q * GROUPS : (q + 1) * GROUPS, 128 * h : 128 * (h + 1)
                ]
    out[...] = stage[...].astype(bf16)


VMEM = pl.BlockSpec(memory_space=pltpu.VMEM)
SMEM = pl.BlockSpec(memory_space=pltpu.SMEM)
ANY = pl.BlockSpec(memory_space=pl.ANY)


def call(kernel, out_shape, in_specs, scratch, flops, moved, name):
    several = isinstance(out_shape, list)
    return pl.pallas_call(
        kernel,
        out_shape=out_shape,
        in_specs=in_specs,
        out_specs=[VMEM] * len(out_shape) if several else VMEM,
        scratch_shapes=scratch,
        compiler_params=pltpu.CompilerParams(vmem_limit_bytes=50 * 2**20),
        cost_estimate=pl.CostEstimate(flops=flops, bytes_accessed=moved, transcendentals=0),
        name=name,
    )


def slots_shape():
    return jax.ShapeDtypeStruct((GROUPS * SLOT_ROWS, 128), bf16)


SLOT_STAGE = pltpu.VMEM((GROUPS * SLOT_ROWS, 128), f32)
TABLE = pltpu.VMEM((STARTS[-1], LATS), bf16)
TABLE_S = pltpu.VMEM((PAIR_STARTS[-1], 256), bf16)
EIGHT = pltpu.SemaphoreType.DMA((BLOCKS,))
ONE = pltpu.SemaphoreType.DMA


def spread(fields, cotangent, forward, scale):
    return call(
        spread_kernel,
        jax.ShapeDtypeStruct((GROUPS * FIRST_ROWS, 128), bf16),
        [VMEM, VMEM, VMEM, SMEM],
        [pltpu.VMEM((GROUPS * FIRST_ROWS, 128), f32)],
        3 * 10**8, 4 * 10**6, "spread",
    )(fields, cotangent, forward, scale)


def first(received, analysis, degree_col):
    return call(
        first_kernel,
        slots_shape(),
        [ANY, ANY, VMEM],
        [
            pltpu.VMEM((GROUPS, 48, 128), bf16),
            pltpu.VMEM((GROUPS * 48, 128), f32),
            SLOT_STAGE, TABLE, ONE, EIGHT,
        ],
        10**9, 6 * 10**6, "first",
    )(received, analysis, degree_col)


def middle(received, cotangents, analysis, synthesis, degree_row, degree_col, inverse, inverse_t):
    return call(
        middle_kernel,
        slots_shape(),
        [VMEM, ANY, ANY, ANY, VMEM, VMEM, VMEM, VMEM],
        [
            pltpu.VMEM((GROUPS, 64, 128), bf16),
            pltpu.VMEM((GROUPS * 64, 128), f32),
            SLOT_STAGE, TABLE, TABLE_S, ONE, EIGHT, EIGHT,
        ],
        3 * 10**9, 12 * 10**6, "middle",
    )(received, cotangents, analysis, synthesis, degree_row, degree_col, inverse, inverse_t)


def last(received, synthesis, degree_row, weight_rows):
    return call(
        last_kernel,
        jax.ShapeDtypeStruct((GROUPS * LAST_ROWS, 128), bf16),
        [VMEM, ANY, VMEM, VMEM],
        [SLOT_STAGE, pltpu.VMEM((GROUPS * LAST_ROWS, 128), f32), TABLE_S, EIGHT],
        10**9, 7 * 10**6, "last",
    )(received, synthesis, degree_row, weight_rows)


def gather(received, forward, cotangent):
    return call(
        gather_kernel,
        jax.ShapeDtypeStruct((BAND, LONS, CHANNELS), bf16),
        [VMEM, VMEM, VMEM],
        [pltpu.VMEM((GROUPS * LAST_ROWS, 128), f32)],
        3 * 10**8, 3 * 10**6, "gather",
    )(received, forward, cotangent)


def mix(adjoint, received, weights, turn):
    return call(
        functools.partial(mix_kernel, adjoint),
        [slots_shape(), jax.ShapeDtypeStruct((SLOTS, CHANNELS, COEFS), bf16)],
        [VMEM, VMEM, VMEM],
        [SLOT_STAGE],
        6 * 10**8, 3 * 10**6, "adjoint_mix" if adjoint else "mix",
    )(received, weights, turn)


def exchange(rows):
    count = rows.shape[0] // GROUPS
    out = lax.all_to_all(
        rows.reshape(GROUPS, count, 128), "lat", split_axis=0, concat_axis=0, tiled=True
    )
    return out.reshape(GROUPS * count, 128)


def weight_gradient(coeffs, grads, turn):
    turned = jnp.einsum("sjcf,fe->sjce", coeffs, turn, preferred_element_type=f32).astype(bf16)
    real = jnp.einsum("sjcf,sjdf->jcd", coeffs, grads, preferred_element_type=f32)
    imag = jnp.einsum("sjcf,sjdf->jcd", turned, grads, preferred_element_type=f32)
    return jnp.stack([real, imag], axis=1).astype(bf16)


def local(fields, cotangent, weights, degree_of):
    table = {k: jnp.asarray(v) for k, v in constants().items()}
    slots = degree_of.reshape(GROUPS, SLOTS).T.reshape(DEGREES)
    degree_col, degree_row = slots[:, None], slots[None, :]
    scale = lax.dynamic_slice(table["weight"], (lax.axis_index("lat") * BAND,), (BAND,))
    turned_weights = jnp.swapaxes(weights, 2, 3)
    on_bands = exchange(spread(fields[0], cotangent[0], table["forward"], scale))
    on_bands = on_bands.reshape(GROUPS, FIRST_ROWS, 128)
    coeffs_sent = exchange(first(on_bands, table["analysis"], degree_col))
    filtered, coeffs = mix(False, coeffs_sent, turned_weights, table["turn"])
    grad_sent = exchange(
        middle(
            exchange(filtered), on_bands, table["analysis"], table["synthesis"],
            degree_row, degree_col, table["inverse"], table["inverse_t"],
        )
    )
    grad_coeffs, grads = mix(True, grad_sent, weights, table["turn"])
    all_coeffs = lax.all_gather(coeffs, "batch", axis=0)
    all_grads = lax.all_gather(grads, "batch", axis=0)
    grad_weights = weight_gradient(all_coeffs, all_grads, table["turn"])
    returned = exchange(last(exchange(grad_coeffs), table["synthesis"], degree_row, table["weight_rows"]))
    grad_fields = gather(returned, table["forward"], cotangent[0])[None]
    return grad_fields, grad_weights


def solution(mesh):
    return jax.shard_map(
        local,
        mesh=mesh,
        in_specs=(
            P("batch", "lat", None, None),
            P("batch", "lat", None, None),
            P("lat", None, None, None),
            P(),
        ),
        out_specs=(P("batch", "lat", None, None), P("lat", None, None, None)),
        check_vma=False,
    )
```

time: 248 us -> 225 us (0.907)
  blocking collectives: 107 us -> 61.3 us
  Pallas kernels: 0 us -> 29.4 us
  waiting for transfers between devices: 50.5 us -> 70.2 us
  local copies, waits for them, and re-layouts: 25.2 us -> 10 us
  matrix products: 20 us -> 10.2 us
  other arithmetic: 3.61 us -> 0.14 us
  starting transfers between devices: 26.1 us -> 29.2 us
    all_to_all x5 -> x3, blocking collectives: 107 us -> 61.3 us  [exchange(): lax.all_to_all(rows.reshape(GROUPS, count, 128), 'lat', split_axis=0, con...]
    pallas_call x0 -> x7, Pallas kernels: none -> 29.4 us  [the longest x1 10.4 us: middle(): call(middle_kernel, slots_shape(), [VMEM, ANY, ANY, ANY, VMEM, VMEM, VMEM...]
    all_to_all x3, waiting for transfers between devices: 50.5 us -> 70.2 us  [exchange(): lax.all_to_all(rows.reshape(GROUPS, count, 128), 'lat', split_axis=0, con...]
    dot_general x20 -> x2, matrix products: 20 us -> 10.2 us  [the longest x1 5.54 us: weight_gradient(): jnp.einsum('sjcf,sjdf->jcd', turned, grads, preferred_element_type=f32)]
    convert_element_type x9 -> x0, local copies, waits for them, and re-layouts: 8.05 us -> none  [the longest x2 3.35 us: fourier_tables(): jnp.transpose(inverse).astype(jnp.bfloat16)]
    unnamed x11 -> x30, local copies, waits for them, and re-layouts: 1.16 us -> 8.83 us
    all_to_all x12 -> x0, local copies, waits for them, and re-layouts: 6.44 us -> none  [the longest x4 2.65 us: to_degrees(): lax.all_to_all(values, 'lat', split_axis=0, concat_axis=1, tiled=True)]
    another operation x7 -> x2, local copies, waits for them, and re-layouts: 5.82 us -> 0.24 us  [local(): degree_col, degree_row = (slots[:, None], slots[None, :])]
  transfers between devices with their start and end apart: 4 -> 5, of which waited for: 3 -> 3; matrix products, arithmetic and copies ran while one was open for 6% -> 1% of each run, Pallas kernels for 0% -> 8%
where the time goes in v2:
time: 225 us
  waiting for transfers between devices  70.2 us (31%)
  blocking collectives  61.3 us (27%)
  Pallas kernels  29.4 us (13%)
  starting transfers between devices  29.2 us (13%)
  between operations  14.2 us (6%)
  matrix products  10.2 us (5%)
  local copies, waits for them, and re-layouts  10 us (4%)
    all_to_all x3, waiting for transfers between devices, exchange(): lax.all_to_all(rows.reshape(GROUPS, count, 128), 'lat', split_axis=0, con...  70.2 us
    all_to_all x3, blocking collectives, exchange(): lax.all_to_all(rows.reshape(GROUPS, count, 128), 'lat', split_axis=0, con...  61.3 us
    all_to_all x3, starting transfers between devices, exchange(): lax.all_to_all(rows.reshape(GROUPS, count, 128), 'lat', split_axis=0, con...  29 us
    pallas_call x1, Pallas kernels, middle(): call(middle_kernel, slots_shape(), [VMEM, ANY, ANY, ANY, VMEM, VMEM, VMEM...  10.4 us
    unnamed x30, local copies, waits for them, and re-layouts  8.83 us
    dot_general x1, matrix products, weight_gradient(): jnp.einsum('sjcf,sjdf->jcd', turned, grads, preferred_element_type=f32)  5.54 us
    pallas_call x1, Pallas kernels, last(): call(last_kernel, jax.ShapeDtypeStruct((GROUPS * LAST_ROWS, 128), bf16),...  5.44 us
    pallas_call x1, Pallas kernels, first(): call(first_kernel, slots_shape(), [ANY, ANY, VMEM], [pltpu.VMEM((GROUPS,...  5.24 us
  transfers between devices with their start and end apart: 5, of which 3 were waited for; matrix products, arithmetic and copies ran while one was open for 1% of the time, Pallas kernels for 8%

profile of v2, /device:TPU:6, one launch (start us, length us, event | category | flops | bytes accessed | tf_op | source)
XLA Modules:
  0.0 224.7 jit_solution(5938983218100722784)
XLA Ops:
  7.2 0.8 dynamic_slice.3.scale
  7.9 1.2 copy-done
  9.1 1.2 copy-done.4
  10.3 0.9 copy-done.5
  11.2 4.2 %spread.1 = bf16[6144,128]{1,0:T(8,128)(2,1)} custom-call(bf16[3,384,384]{2,1,0:T(8,128)(2,1)S(1)} %bitcast.47, bf16[3,384,384]{2,1,0:T(8,128)(2,1)S(1)} %bitcast.39, bf16[384,256]{1,0:T(8,128)(2,1)S(1)} %copy-done.5, f32[3]{0:T(128)S(1)} %dynamic_slice.3.scale), custom_call_target="tpu_custom_call" | custom-call | flops 300000000 | bytes 4000000 | tf_op jit(solution)/shard_map/spread/pallas_call | solution.py:456
  15.4 16.6 %all-to-all-start = ((bf16[64,96,128]{2,1,0:T(8,128)(2,1)}), bf16[64,96,128]{2,1,0:T(8,128)(2,1)S(1)}, u32[]{:S(2)}, u32[]{:S(2)}) async-start(bf16[64,96,128]{2,1,0:T(8,128)(2,1)} %bitcast.2), calls=%async_computation | async-start | bytes 3145728 | tf_op jit(solution)/shard_map/all_to_all | solution.py:525
  32.0 0.1 reshape.41
  32.2 0.2 broadcast_in_dim_reshape.8.degree_col
  32.3 40.9 %all-to-all-done.received.cotangents = bf16[64,96,128]{2,1,0:T(8,128)(2,1)S(1)} async-done(((bf16[64,96,128]{2,1,0:T(8,128)(2,1)}), bf16[64,96,128]{2,1,0:T(8,128)(2,1)S(1)}, u32[]{:S(2)}, u32[]{:S(2)}) %all-to-all-start) | async-done | bytes 1572896 | tf_op jit(solution)/shard_map/all_to_all | solution.py:525
  73.2 5.2 %first.1 = bf16[1536,128]{1,0:T(8,128)(2,1)} custom-call(bf16[64,96,128]{2,1,0:T(8,128)(2,1)S(1)} %all-to-all-done.received.cotangents, bf16[9216,192]{1,0:T(8,128)(2,1)} %constant.28.clone.analysis, s32[128,1]{1,0:T(8,128)S(1)} %broadcast_in_dim_reshape.8.degree_col), custom_call_target="tpu_custom_call" | custom-call | flops 1000000000 | bytes 6000000 | tf_op jit(solution)/shard_map/first/pallas_call | solution.py:466
  78.5 7.7 %all-to-all-start.1 = ((bf16[64,24,128]{2,1,0:T(8,128)(2,1)}), bf16[64,24,128]{2,1,0:T(8,128)(2,1)S(1)}, u32[]{:S(2)}, u32[]{:S(2)}) async-start(bf16[64,24,128]{2,1,0:T(8,128)(2,1)} %bitcast.4), calls=%async_computation.1 | async-start | bytes 786432 | tf_op jit(solution)/shard_map/all_to_all | solution.py:525
  86.3 1.5 copy.34
  87.8 14.4 %all-to-all-done.1 = bf16[64,24,128]{2,1,0:T(8,128)(2,1)S(1)} async-done(((bf16[64,24,128]{2,1,0:T(8,128)(2,1)}), bf16[64,24,128]{2,1,0:T(8,128)(2,1)S(1)}, u32[]{:S(2)}, u32[]{:S(2)}) %all-to-all-start.1) | async-done | bytes 393248 | tf_op jit(solution)/shard_map/all_to_all | solution.py:525
  102.1 1.3 copy-done.3
  103.4 1.3 mix.1
  104.7 0.7 copy-done.7
  105.5 4.6 %all-to-all-start.2 = ((bf16[64,24,128]{2,1,0:T(8,128)(2,1)}), bf16[64,24,128]{2,1,0:T(8,128)(2,1)S(1)}, u32[]{:S(2)}, u32[]{:S(2)}) async-start(bf16[64,24,128]{2,1,0:T(8,128)(2,1)} %bitcast.48), calls=%async_computation.2 | async-start | bytes 786432 | tf_op jit(solution)/shard_map/all_to_all | solution.py:525
  110.1 0.2 all-gather.7.cloned.1.call-start
  110.4 0.1 broadcast_in_dim_reshape.7.degree_row
  110.5 15.0 %all-to-all-done.2 = bf16[64,24,128]{2,1,0:T(8,128)(2,1)S(1)} async-done(((bf16[64,24,128]{2,1,0:T(8,128)(2,1)}), bf16[64,24,128]{2,1,0:T(8,128)(2,1)S(1)}, u32[]{:S(2)}, u32[]{:S(2)}) %all-to-all-start.2) | async-done | bytes 393248 | tf_op jit(solution)/shard_map/all_to_all | solution.py:525
  125.4 0.9 copy-done.9
  126.3 10.4 %middle.1 = bf16[1536,128]{1,0:T(8,128)(2,1)S(1)} custom-call(bf16[1536,128]{1,0:T(8,128)(2,1)S(1)} %bitcast.43, bf16[64,96,128]{2,1,0:T(8,128)(2,1)S(1)} %all-to-all-done.received.cotangents, bf16[9216,192]{1,0:T(8,128)(2,1)} %constant.28.clone.analysis, bf16[12288,256]{1,0:T(8,128)(2,1)} %constant.29.clone.synthesis, ...), custom_call_target="tpu_custom_call" | custom-call | flops 3000000000 | bytes 12000000 | tf_op jit(solution)/shard_map/middle/pallas_call | solution.py:480
  136.8 19.6 %all_to_all.30 = bf16[64,24,128]{2,1,0:T(8,128)(2,1)S(1)} all-to-all(bf16[64,24,128]{2,1,0:T(8,128)(2,1)S(1)} %bitcast.44), channel_id=1, replica_groups=mesh['lat'=64,'batch'=8] {'lat'}, dimensions={0} | all-to-all | bytes 786432 | tf_op jit(solution)/shard_map/all_to_all | solution.py:525
  156.5 1.3 adjoint_mix.1
  157.8 19.0 %all_to_all.31 = bf16[64,24,128]{2,1,0:T(8,128)(2,1)S(1)} all-to-all(bf16[64,24,128]{2,1,0:T(8,128)(2,1)S(1)} %bitcast.50), channel_id=1, replica_groups=mesh['lat'=64,'batch'=8] {'lat'}, dimensions={0} | all-to-all | bytes 786432 | tf_op jit(solution)/shard_map/all_to_all | solution.py:525
  176.8 5.4 %last.1 = bf16[2560,128]{1,0:T(8,128)(2,1)S(1)} custom-call(bf16[1536,128]{1,0:T(8,128)(2,1)S(1)} %bitcast.45, bf16[12288,256]{1,0:T(8,128)(2,1)} %constant.29.clone.synthesis, s32[1,128]{1,0:T(1,128)S(1)} %broadcast_in_dim_reshape.7.degree_row, f32[192,1]{1,0:T(8,128)S(1)} %copy-done.10), custom_call_target="tpu_custom_call" | custom-call | flops 1000000000 | bytes 7000000 | tf_op jit(solution)/shard_map/last/pallas_call | solution.py:494
  182.3 22.6 %all_to_all.32 = bf16[64,40,128]{2,1,0:T(8,128)(2,1)S(1)} all-to-all(bf16[64,40,128]{2,1,0:T(8,128)(2,1)S(1)} %bitcast.42), channel_id=1, replica_groups=mesh['lat'=64,'batch'=8] {'lat'}, dimensions={0} | all-to-all | bytes 1310720 | tf_op jit(solution)/shard_map/all_to_all | solution.py:525
  204.9 1.5 gather.1
  206.4 4.7 %fusion.31 = bf16[2,1,384,384]{3,2,0,1:T(8,128)(2,1)S(1)} fusion(bf16[8,2,384,256]{3,2,1,0:T(8,128)(2,1)} %bitcast.54, bf16[8,2,384,256]{3,2,1,0:T(8,128)(2,1)} %bitcast.56), kind=kOutput, calls=%fused_computation.10 | convolution fusion | flops 1208254464 | bytes 6881280 | tf_op jit(solution)/shard_map/sjcf,sjdf->jcd/dot_general | solution.py:533
  211.0 5.5 %fusion.24 = bf16[2,1,384,384]{3,2,0,1:T(8,128)(2,1)S(1)} fusion(bf16[8,2,384,256]{3,2,1,0:T(8,128)(2,1)} %bitcast.57, bf16[256,256,1,1]{1,0,2,3:T(8,128)(2,1)S(1)} %copy-done.13, bf16[8,2,384,256]{3,2,1,0:T(8,128)(2,1)} %bitcast.55), kind=kOutput, calls=%fused_computation.9 | convolution fusion | flops 2015133696 | bytes 7012352 | tf_op jit(solution)/shard_map/sjcf,sjdf->jcd/dot_general | solution.py:534
  216.6 0.1 pad_maximum_fusion
  216.7 1.1 copy.39
  (28 shorter events, 0.2 us)
Async XLA Ops:
  7.9 1.2 copy-start
  9.1 1.2 copy-start.4
  10.3 0.9 copy-start.5
  11.2 20.8 %copy-start.12 = (s32[128]{0:T(128)S(1)}, s32[128]{0:T(128)}, u32[]{:S(2)}) copy-start(s32[128]{0:T(128)} %param.15) | copy-start | bytes 1540
  15.4 57.9 %all-to-all-start = ((bf16[64,96,128]{2,1,0:T(8,128)(2,1)}), bf16[64,96,128]{2,1,0:T(8,128)(2,1)S(1)}, u32[]{:S(2)}, u32[]{:S(2)}) async-start(bf16[64,96,128]{2,1,0:T(8,128)(2,1)} %bitcast.2), calls=%async_computation | async-start | bytes 3145728 | tf_op jit(solution)/shard_map/all_to_all | solution.py:525
  32.3 54.0 %copy-start.2 = (bf16[2,2,384,384]{3,2,1,0:T(8,128)(2,1)S(1)}, bf16[2,2,384,384]{3,2,1,0:T(8,128)(2,1)}, u32[]{:S(2)}) copy-start(bf16[2,2,384,384]{3,2,1,0:T(8,128)(2,1)} %weights.1) | copy-start | bytes 3538948
  78.5 23.7 %copy-start.11 = (bf16[256,256]{1,0:T(8,128)(2,1)S(1)}, bf16[256,256]{1,0:T(8,128)(2,1)}, u32[]{:S(2)}) copy-start(bf16[256,256]{1,0:T(8,128)(2,1)} %constant.33.clone.turn) | copy-start | bytes 393220
  78.5 46.9 %copy-start.8 = (bf16[384,256]{1,0:T(8,128)(2,1)S(1)}, bf16[384,256]{1,0:T(8,128)(2,1)}, u32[]{:S(2)}) copy-start(bf16[384,256]{1,0:T(8,128)(2,1)} %constant.31.clone.inverse) | copy-start | bytes 589828
  78.5 23.6 %all-to-all-start.1 = ((bf16[64,24,128]{2,1,0:T(8,128)(2,1)}), bf16[64,24,128]{2,1,0:T(8,128)(2,1)S(1)}, u32[]{:S(2)}, u32[]{:S(2)}) async-start(bf16[64,24,128]{2,1,0:T(8,128)(2,1)} %bitcast.4), calls=%async_computation.1 | async-start | bytes 786432 | tf_op jit(solution)/shard_map/all_to_all | solution.py:525
  86.2 120.1 %all-gather.5.cloned.1.call-start = ((), (), s32[]{:S(2)}) async-start(), calls=%async_computation.6 | async-start | bytes 3538944 | tf_op jit(solution)/shard_map/all_gather | solution.py:555
  102.1 1.3 copy-start.3
  104.7 0.7 copy-start.7
  105.5 19.9 %all-to-all-start.2 = ((bf16[64,24,128]{2,1,0:T(8,128)(2,1)}), bf16[64,24,128]{2,1,0:T(8,128)(2,1)S(1)}, u32[]{:S(2)}, u32[]{:S(2)}) async-start(bf16[64,24,128]{2,1,0:T(8,128)(2,1)} %bitcast.48), calls=%async_computation.2 | async-start | bytes 786432 | tf_op jit(solution)/shard_map/all_to_all | solution.py:525
  110.1 96.2 %all-gather.7.cloned.1.call-start = ((), (), s32[]{:S(2)}) async-start(), calls=%async_computation.7 | async-start | bytes 3538944 | tf_op jit(solution)/shard_map/all_gather | solution.py:556
  125.4 0.9 copy-start.9
  136.8 40.0 %copy-start.10 = (f32[192,1]{1,0:T(8,128)S(1)}, f32[192,1]{1,0:T(8,128)}, u32[]{:S(2)}) copy-start(f32[192,1]{1,0:T(8,128)} %constant.35.clone.weight_rows) | copy-start | bytes 2308
  176.8 28.1 %copy-start.1 = (bf16[1,3,384,384]{3,2,1,0:T(8,128)(2,1)S(1)}, bf16[1,3,384,384]{3,2,1,0:T(8,128)(2,1)}, u32[]{:S(2)}) copy-start(bf16[1,3,384,384]{3,2,1,0:T(8,128)(2,1)} %param.13) | copy-start | bytes 2654212
  176.8 28.1 %copy-start.6 = (bf16[384,256]{1,0:T(8,128)(2,1)S(1)}, bf16[384,256]{1,0:T(8,128)(2,1)}, u32[]{:S(2)}) copy-start(bf16[384,256]{1,0:T(8,128)(2,1)} %constant.30.clone.forward) | copy-start | bytes 589828
  206.4 4.7 %copy-start.13 = (bf16[256,256,1,1]{1,0,2,3:T(8,128)(2,1)S(1)}, bf16[256,256,1,1]{1,0,2,3:T(8,128)(2,1)}, u32[]{:S(2)}) copy-start(bf16[256,256,1,1]{1,0,2,3:T(8,128)(2,1)} %constant.39) | copy-start | bytes 393220
Sparse Core Ops, SparseCore 0:
  105.6 24.4 all-gather.4
  157.9 24.4 all-gather.6

commit v3 on v2

--- a/solution.py
+++ b/solution.py
@@ -21,7 +21,8 @@
 COEFS = 2 * ORDERS
 BLOCKS = ORDERS // 16
 SPEC_ROWS = BAND * PARTS * 2
-FIRST_ROWS = 96
+SENT_ROWS = 48
+COT_CUTS = (0, 12, 36, 54)
 SLOT_ROWS = SLOTS * PARTS * 2
 LAST_ROWS = 40
 REACH = [DEGREES - 16 * t for t in range(BLOCKS)]
@@ -72,10 +73,16 @@
 def constants():
     table, quadrature = legendre_table()
     where = np.arange(LATS).reshape(GROUPS, BAND).T.reshape(-1)
-    table = table[:, :, where].astype(bf16)
-    analysis = np.concatenate(
-        [table[16 * t + k, 16 * t :] for t in range(BLOCKS) for k in range(16)], axis=0
-    )
+    table = table[:, :, where]
+
+    def by_block(values):
+        values = values.astype(bf16)
+        return np.concatenate(
+            [values[16 * t + k, 16 * t :] for t in range(BLOCKS) for k in range(16)], axis=0
+        )
+
+    analysis, weighted = by_block(table), by_block(table * quadrature[where])
+    table = table.astype(bf16)
     synthesis = np.concatenate(
         [
             np.concatenate([table[16 * t + k].T, table[16 * t + k + 8].T], axis=1)
@@ -91,12 +98,12 @@
     turn[even, even + 1] = 1.0
     return dict(
         analysis=analysis,
+        weighted=weighted,
         synthesis=synthesis,
         forward=forward,
         inverse=inverse,
         inverse_t=np.ascontiguousarray(inverse.T),
         turn=turn.astype(bf16),
-        weight=quadrature.astype(np.float32),
         weight_rows=quadrature[where].astype(np.float32)[:, None],
     )
 
@@ -217,25 +224,31 @@
     return out
 
 
-def slot_rows_out(tiles, degree_col, stage, out):
-    pick = (degree_col[...] == lane_of((DEGREES, DEGREES))).astype(f32).astype(bf16)
-    parts = from_tiles(permute_rows(pick, as_bf16(tiles)))
+def put_slots(parts, carried, stage, out):
+    stride = SLOT_ROWS if carried is None else SENT_ROWS
     for j in range(SLOTS):
         for q in range(PARTS):
             for h in range(2):
-                stage[pl.ds((j * PARTS + q) * 2 + h, GROUPS, stride=SLOT_ROWS), :] = parts[q][h][
+                stage[pl.ds((j * PARTS + q) * 2 + h, GROUPS, stride=stride), :] = parts[q][h][
                     j * GROUPS : (j + 1) * GROUPS
                 ]
-    out[...] = stage[...].astype(bf16)
-
-
-def slot_rows_in(received, degree_row, stage):
-    stage[...] = received[...].astype(f32)
-    parts = [
+    if carried is None:
+        out[...] = stage[pl.ds(0, GROUPS * SLOT_ROWS), :].astype(bf16)
+    else:
+        rows = stage[...].reshape(GROUPS, SENT_ROWS, 128)[:, :SLOT_ROWS]
+        more = carried[...].astype(f32).reshape(GROUPS, SLOT_ROWS, 128)
+        both = jnp.concatenate([rows, more], axis=1)
+        out[...] = both.reshape(GROUPS * SENT_ROWS, 128).astype(bf16)
+
+
+def get_slots(received, stage):
+    count = received.shape[0]
+    stage[pl.ds(0, count), :] = received[...].astype(f32)
+    return [
         [
             jnp.concatenate(
                 [
-                    stage[pl.ds((j * PARTS + q) * 2 + h, GROUPS, stride=SLOT_ROWS), :]
+                    stage[pl.ds((j * PARTS + q) * 2 + h, GROUPS, stride=count // GROUPS), :]
                     for j in range(SLOTS)
                 ],
                 axis=0,
@@ -244,9 +257,17 @@
         ]
         for q in range(PARTS)
     ]
+
+
+def slot_rows_out(tiles, degree_col, carried, stage, out):
+    pick = (degree_col[...] == lane_of((DEGREES, DEGREES))).astype(f32).astype(bf16)
+    put_slots(from_tiles(permute_rows(pick, as_bf16(tiles))), carried, stage, out)
+
+
+def slot_rows_in(received, degree_row, stage):
     rows = lax.broadcasted_iota(jnp.int32, (DEGREES, DEGREES), 0)
     pick = (rows == degree_row[...]).astype(f32).astype(bf16)
-    return as_bf16(permute_rows(pick, as_bf16(to_tiles(parts))))
+    return as_bf16(permute_rows(pick, as_bf16(to_tiles(get_slots(received, stage)))))
 
 
 def table_copies(source, target, sems, bounds):
@@ -260,40 +281,66 @@
 PAIR_STARTS = [PAIR_ROWS * t for t in range(BLOCKS + 1)]
 
 
-def spread_kernel(fields, cotangent, forward, scale, out, stage):
+def cot_place(i, q, h):
+    row = (i * PARTS + q) * 3 + h
+    which = sum(row >= cut for cut in COT_CUTS[1:3])
+    return which, row - COT_CUTS[which]
+
+
+def spread_kernel(fields, cotangent, forward, out, cot_two, cot_three, field, cot, stages, sems):
+    copies = []
     for i in range(BAND):
-        spectra = dot(fields[i], forward[...], TN) * scale[i]
-        turned = jnp.transpose(cotangent[i].astype(f32))
+        copies.append(
+            (
+                pltpu.make_async_copy(fields.at[i], field.at[i], sems.at[2 * i]),
+                pltpu.make_async_copy(cotangent.at[i], cot.at[i], sems.at[2 * i + 1]),
+            )
+        )
+    for pair in copies:
+        for copy in pair:
+            copy.start()
+    stage, stage_two, stage_three = stages.at[0], stages.at[1], stages.at[2]
+    spots = ((stage, SPEC_ROWS, SENT_ROWS), (stage_two, 0, SLOT_ROWS), (stage_three, 0, SLOT_ROWS))
+    for i in range(BAND):
+        copies[i][0].wait()
+        spectra = dot(field[i], forward[...], TN)
         for q in range(PARTS):
             rows = slice(q * GROUPS, (q + 1) * GROUPS)
             at = (i * PARTS + q) * 2
             for h in range(2):
-                stage[pl.ds(at + h, GROUPS, stride=FIRST_ROWS), :] = spectra[
+                stage[pl.ds(at + h, GROUPS, stride=SENT_ROWS), :] = spectra[
                     rows, 128 * h : 128 * (h + 1)
                 ]
-            at = SPEC_ROWS + (i * PARTS + q) * 3
+        copies[i][1].wait()
+        turned = jnp.transpose(cot[i].astype(f32))
+        for q in range(PARTS):
+            rows = slice(q * GROUPS, (q + 1) * GROUPS)
             for h in range(3):
-                stage[pl.ds(at + h, GROUPS, stride=FIRST_ROWS), :] = turned[
+                which, at = cot_place(i, q, h)
+                place, base, stride = spots[which]
+                place[pl.ds(base + at, GROUPS, stride=stride), :] = turned[
                     rows, 128 * h : 128 * (h + 1)
                 ]
-    for row in range(SPEC_ROWS + BAND * PARTS * 3, FIRST_ROWS):
-        stage[pl.ds(row, GROUPS, stride=FIRST_ROWS), :] = jnp.zeros((GROUPS, 128), f32)
+    for row in range(COT_CUTS[3] - COT_CUTS[2], SLOT_ROWS):
+        stage_three[pl.ds(row, GROUPS, stride=SLOT_ROWS), :] = jnp.zeros((GROUPS, 128), f32)
     out[...] = stage[...].astype(bf16)
-
-
-def first_kernel(received, analysis, degree_col, out, rows, stage_in, stage, table, row_sem, sems):
+    short = GROUPS * SLOT_ROWS
+    cot_two[...] = stage_two[pl.ds(0, short), :].astype(bf16)
+    cot_three[...] = stage_three[pl.ds(0, short), :].astype(bf16)
+
+
+def first_kernel(
+    received, analysis, degree_col, carried, early, out, stage_in, stage, table, sems
+):
     copies = table_copies(analysis, table, sems, STARTS)
-    fetch = pltpu.make_async_copy(received.at[:, pl.ds(0, 48), :], rows, row_sem)
-    fetch.start()
     for copy in copies:
         copy.start()
-    fetch.wait()
-    stage_in[...] = rows[...].astype(f32).reshape(GROUPS * 48, 128)
+    stage_in[...] = received[...].astype(f32)
     parts = [
         [
             jnp.concatenate(
                 [
-                    stage_in[pl.ds((i * PARTS + q) * 2 + h, GROUPS, stride=48), :]
+                    stage_in[pl.ds((i * PARTS + q) * 2 + h, GROUPS, stride=SENT_ROWS), :]
                     for i in range(BAND)
                 ],
                 axis=0,
@@ -304,7 +351,7 @@
     ]
     tiles = as_bf16(to_tiles(parts))
     sums = analyse(tiles, table, lambda t: copies[t].wait())
-    slot_rows_out(sums, degree_col, stage, out)
+    slot_rows_out(sums, degree_col, carried, stage, out)
 
 
 def gelu_slope(x):
@@ -315,35 +362,36 @@
 
 
 def middle_kernel(
-    received, cotangents, analysis, synthesis, degree_row, degree_col, inverse, inverse_t, out,
-    rows, stage_in, stage, table, table_s, row_sem, sems, sems_s,
+    received, one, two, analysis, synthesis, degree_row, degree_col, inverse, inverse_t, out,
+    rows_one, rows_two, stage_one, stage_two, stage, table, table_s, row_sems, sems, sems_s,
 ):
     copies_s = table_copies(synthesis, table_s, sems_s, PAIR_STARTS)
     copies = table_copies(analysis, table, sems, STARTS)
-    fetch = pltpu.make_async_copy(cotangents.at[:, pl.ds(32, 64), :], rows, row_sem)
-    for copy in copies_s:
-        copy.start()
-    fetch.start()
-    for copy in copies:
+    fetches = (
+        pltpu.make_async_copy(one.at[:, pl.ds(32, 16), :], rows_one, row_sems.at[0]),
+        pltpu.make_async_copy(two.at[:, pl.ds(16, 32), :], rows_two, row_sems.at[1]),
+    )
+    for copy in (*copies_s, *fetches, *copies):
         copy.start()
     tiles = slot_rows_in(received, degree_row, stage)
     synth = from_tiles(synthesise(tiles, table_s, lambda t: copies_s[t].wait()))
-    fetch.wait()
-    stage_in[...] = rows[...].astype(f32).reshape(GROUPS * 64, 128)
+    for fetch in fetches:
+        fetch.wait()
+    stage_one[...] = rows_one[...].astype(f32).reshape(GROUPS * 16, 128)
+    stage_two[...] = rows_two[...].astype(f32).reshape(GROUPS * 32, 128)
+    spots = ((stage_one, SPEC_ROWS - 32, 16), (stage_two, 8, 32), (stage, SLOT_ROWS, SENT_ROWS))
+
+    def cot_rows(i, q, h):
+        which, at = cot_place(i, q, h)
+        place, base, stride = spots[which]
+        return place[pl.ds(base + at, GROUPS, stride=stride), :]
+
     parts = []
     for q in range(PARTS):
         response = dot(jnp.concatenate(synth[q], axis=1).astype(bf16), inverse_t[...])
         cotangent = jnp.concatenate(
             [
-                jnp.concatenate(
-                    [
-                        stage_in[
-                            pl.ds(SPEC_ROWS - 32 + (i * PARTS + q) * 3 + h, GROUPS, stride=64), :
-                        ]
-                        for h in range(3)
-                    ],
-                    axis=1,
-                )
+                jnp.concatenate([cot_rows(i, q, h) for h in range(3)], axis=1)
                 for i in range(BAND)
             ],
             axis=0,
@@ -352,7 +400,7 @@
         grad = dot(upstream, inverse[...])
         parts.append([grad[:, :128], grad[:, 128:]])
     sums = analyse(as_bf16(to_tiles(parts)), table, lambda t: copies[t].wait())
-    slot_rows_out(sums, degree_col, stage, out)
+    slot_rows_out(sums, degree_col, None, stage, out)
 
 
 def last_kernel(received, synthesis, degree_row, weight_rows, out, stage, stage_out, table_s, sems_s):
@@ -374,7 +422,7 @@
     out[...] = stage_out[...].astype(bf16)
 
 
-def gather_kernel(received, forward, cotangent, out, stage):
+def gather_kernel(received, forward, cotangent, weight_grads, out, stage):
     stage[...] = received[...].astype(f32)
     for i in range(BAND):
         halves = [
@@ -392,34 +440,32 @@
         out[i] = (cotangent[i].astype(f32) + delta).astype(bf16)
 
 
-def mix_kernel(adjoint, received, weights, turn, out, kept, stage):
-    stage[...] = received[...].astype(f32)
+def mix_kernel(adjoint, received, weights, turn, *rest):
+    carried, out, kept, stage = (None, *rest) if adjoint else rest
+    parts = get_slots(received, stage)
     results = []
     for j in range(SLOTS):
-        halves = [
-            jnp.concatenate(
-                [
-                    stage[pl.ds((j * PARTS + q) * 2 + h, GROUPS, stride=SLOT_ROWS), :]
-                    for q in range(PARTS)
-                ],
-                axis=0,
-            )
-            for h in range(2)
-        ]
-        held = jnp.concatenate(halves, axis=1).astype(bf16)
+        own = slice(j * GROUPS, (j + 1) * GROUPS)
+        held = jnp.concatenate(
+            [jnp.concatenate([x[own] for x in parts[q]], axis=1) for q in range(PARTS)], axis=0
+        ).astype(bf16)
         kept[j] = held
         turned = dot(held, turn[...])
         if adjoint:
             turned = -turned
         turned = turned.astype(bf16)
         results.append(dot(weights[j, 0], held) + dot(weights[j, 1], turned))
-    for j in range(SLOTS):
-        for q in range(PARTS):
-            for h in range(2):
-                stage[pl.ds((j * PARTS + q) * 2 + h, GROUPS, stride=SLOT_ROWS), :] = results[j][
-                    q * GROUPS : (q + 1) * GROUPS, 128 * h : 128 * (h + 1)
-                ]
-    out[...] = stage[...].astype(bf16)
+    mixed = [
+        [
+            jnp.concatenate(
+                [x[q * GROUPS : (q + 1) * GROUPS, 128 * h : 128 * (h + 1)] for x in results],
+                axis=0,
+            )
+            for h in range(2)
+        ]
+        for q in range(PARTS)
+    ]
+    put_slots(mixed, carried, stage, out)
 
 
 VMEM = pl.BlockSpec(memory_space=pltpu.VMEM)
@@ -427,7 +473,7 @@
 ANY = pl.BlockSpec(memory_space=pl.ANY)
 
 
-def call(kernel, out_shape, in_specs, scratch, flops, moved, name):
+def call(kernel, out_shape, in_specs, scratch, flops, moved, name, limit=50):
     several = isinstance(out_shape, list)
     return pl.pallas_call(
         kernel,
@@ -435,89 +481,92 @@
         in_specs=in_specs,
         out_specs=[VMEM] * len(out_shape) if several else VMEM,
         scratch_shapes=scratch,
-        compiler_params=pltpu.CompilerParams(vmem_limit_bytes=50 * 2**20),
+        compiler_params=pltpu.CompilerParams(vmem_limit_bytes=limit * 2**20),
         cost_estimate=pl.CostEstimate(flops=flops, bytes_accessed=moved, transcendentals=0),
         name=name,
     )
 
 
-def slots_shape():
-    return jax.ShapeDtypeStruct((GROUPS * SLOT_ROWS, 128), bf16)
-
-
-SLOT_STAGE = pltpu.VMEM((GROUPS * SLOT_ROWS, 128), f32)
+def message(rows):
+    return jax.ShapeDtypeStruct((GROUPS * rows, 128), bf16)
+
+
+def stage_of(rows):
+    return pltpu.VMEM((GROUPS * rows, 128), f32)
+
+
 TABLE = pltpu.VMEM((STARTS[-1], LATS), bf16)
 TABLE_S = pltpu.VMEM((PAIR_STARTS[-1], 256), bf16)
-EIGHT = pltpu.SemaphoreType.DMA((BLOCKS,))
-ONE = pltpu.SemaphoreType.DMA
-
-
-def spread(fields, cotangent, forward, scale):
+
+
+def sems(count):
+    return pltpu.SemaphoreType.DMA((count,))
+
+
+def spread(fields, cotangent, forward):
+    cycle = pltpu.VMEM((BAND, LONS, CHANNELS), bf16)
     return call(
         spread_kernel,
-        jax.ShapeDtypeStruct((GROUPS * FIRST_ROWS, 128), bf16),
-        [VMEM, VMEM, VMEM, SMEM],
-        [pltpu.VMEM((GROUPS * FIRST_ROWS, 128), f32)],
-        3 * 10**8, 4 * 10**6, "spread",
-    )(fields, cotangent, forward, scale)
-
-
-def first(received, analysis, degree_col):
+        [message(SENT_ROWS), message(SLOT_ROWS), message(SLOT_ROWS)],
+        [ANY, ANY, VMEM],
+        [cycle, cycle, pltpu.VMEM((3, GROUPS * SENT_ROWS, 128), f32), sems(2 * BAND)],
+        3 * 10**8, 4 * 10**6, "spread", 60,
+    )(fields, cotangent, forward)
+
+
+def first(received, weighted, degree_col, carried, early):
     return call(
         first_kernel,
-        slots_shape(),
-        [ANY, ANY, VMEM],
-        [
-            pltpu.VMEM((GROUPS, 48, 128), bf16),
-            pltpu.VMEM((GROUPS * 48, 128), f32),
-            SLOT_STAGE, TABLE, ONE, EIGHT,
-        ],
+        message(SENT_ROWS),
+        [VMEM, ANY, VMEM, VMEM, ANY],
+        [stage_of(SENT_ROWS), stage_of(SENT_ROWS), TABLE, sems(BLOCKS)],
         10**9, 6 * 10**6, "first",
-    )(received, analysis, degree_col)
-
-
-def middle(received, cotangents, analysis, synthesis, degree_row, degree_col, inverse, inverse_t):
+    )(received, weighted, degree_col, carried, early)
+
+
+def middle(received, one, two, analysis, synthesis, degree_row, degree_col, inverse, inverse_t):
     return call(
         middle_kernel,
-        slots_shape(),
-        [VMEM, ANY, ANY, ANY, VMEM, VMEM, VMEM, VMEM],
+        message(SLOT_ROWS),
+        [VMEM, ANY, ANY, ANY, ANY, VMEM, VMEM, VMEM, VMEM],
         [
-            pltpu.VMEM((GROUPS, 64, 128), bf16),
-            pltpu.VMEM((GROUPS * 64, 128), f32),
-            SLOT_STAGE, TABLE, TABLE_S, ONE, EIGHT, EIGHT,
+            pltpu.VMEM((GROUPS, 16, 128), bf16), pltpu.VMEM((GROUPS, 32, 128), bf16),
+            stage_of(16), stage_of(32), stage_of(SENT_ROWS),
+            TABLE, TABLE_S, sems(2), sems(BLOCKS), sems(BLOCKS),
         ],
         3 * 10**9, 12 * 10**6, "middle",
-    )(received, cotangents, analysis, synthesis, degree_row, degree_col, inverse, inverse_t)
+    )(received, one, two, analysis, synthesis, degree_row, degree_col, inverse, inverse_t)
 
 
 def last(received, synthesis, degree_row, weight_rows):
     return call(
         last_kernel,
-        jax.ShapeDtypeStruct((GROUPS * LAST_ROWS, 128), bf16),
+        message(LAST_ROWS),
         [VMEM, ANY, VMEM, VMEM],
-        [SLOT_STAGE, pltpu.VMEM((GROUPS * LAST_ROWS, 128), f32), TABLE_S, EIGHT],
+        [stage_of(SLOT_ROWS), stage_of(LAST_ROWS), TABLE_S, sems(BLOCKS)],
         10**9, 7 * 10**6, "last",
     )(received, synthesis, degree_row, weight_rows)
 
 
-def gather(received, forward, cotangent):
+def gather(received, forward, cotangent, weight_grads):
     return call(
         gather_kernel,
         jax.ShapeDtypeStruct((BAND, LONS, CHANNELS), bf16),
-        [VMEM, VMEM, VMEM],
-        [pltpu.VMEM((GROUPS * LAST_ROWS, 128), f32)],
+        [VMEM, VMEM, VMEM, ANY],
+        [stage_of(LAST_ROWS)],
         3 * 10**8, 3 * 10**6, "gather",
-    )(received, forward, cotangent)
-
-
-def mix(adjoint, received, weights, turn):
+    )(received, forward, cotangent, weight_grads)
+
+
+def mix(adjoint, received, weights, turn, *carried):
+    rows = SLOT_ROWS if adjoint else SENT_ROWS
     return call(
         functools.partial(mix_kernel, adjoint),
-        [slots_shape(), jax.ShapeDtypeStruct((SLOTS, CHANNELS, COEFS), bf16)],
-        [VMEM, VMEM, VMEM],
-        [SLOT_STAGE],
+        [message(rows), jax.ShapeDtypeStruct((SLOTS, CHANNELS, COEFS), bf16)],
+        [VMEM, VMEM, VMEM] + [VMEM] * len(carried),
+        [stage_of(rows)],
         6 * 10**8, 3 * 10**6, "adjoint_mix" if adjoint else "mix",
-    )(received, weights, turn)
+    )(received, weights, turn, *carried)
 
 
 def exchange(rows):
@@ -530,33 +579,35 @@
 
 def weight_gradient(coeffs, grads, turn):
     turned = jnp.einsum("sjcf,fe->sjce", coeffs, turn, preferred_element_type=f32).astype(bf16)
-    real = jnp.einsum("sjcf,sjdf->jcd", coeffs, grads, preferred_element_type=f32)
-    imag = jnp.einsum("sjcf,sjdf->jcd", turned, grads, preferred_element_type=f32)
-    return jnp.stack([real, imag], axis=1).astype(bf16)
+    both = jnp.stack([coeffs, turned], axis=2)
+    total = jnp.einsum("sjpcf,sjdf->jpcd", both, grads, preferred_element_type=f32)
+    return total.astype(bf16)
 
 
 def local(fields, cotangent, weights, degree_of):
     table = {k: jnp.asarray(v) for k, v in constants().items()}
     slots = degree_of.reshape(GROUPS, SLOTS).T.reshape(DEGREES)
     degree_col, degree_row = slots[:, None], slots[None, :]
-    scale = lax.dynamic_slice(table["weight"], (lax.axis_index("lat") * BAND,), (BAND,))
     turned_weights = jnp.swapaxes(weights, 2, 3)
-    on_bands = exchange(spread(fields[0], cotangent[0], table["forward"], scale))
-    on_bands = on_bands.reshape(GROUPS, FIRST_ROWS, 128)
-    coeffs_sent = exchange(first(on_bands, table["analysis"], degree_col))
-    filtered, coeffs = mix(False, coeffs_sent, turned_weights, table["turn"])
-    grad_sent = exchange(
+    sent, cot_two, cot_three = spread(fields[0], cotangent[0], table["forward"])
+    one = exchange(sent)
+    two = exchange(first(one, table["weighted"], degree_col, cot_two, turned_weights))
+    filtered, coeffs = mix(False, two, turned_weights, table["turn"], cot_three)
+    all_coeffs = lax.all_gather(coeffs, "batch", axis=0)
+    three = exchange(filtered)
+    as_sent = (GROUPS, SENT_ROWS, 128)
+    four = exchange(
         middle(
-            exchange(filtered), on_bands, table["analysis"], table["synthesis"],
-            degree_row, degree_col, table["inverse"], table["inverse_t"],
+            three, one.reshape(as_sent), two.reshape(as_sent), table["analysis"],
+            table["synthesis"], degree_row, degree_col, table["inverse"], table["inverse_t"],
         )
     )
-    grad_coeffs, grads = mix(True, grad_sent, weights, table["turn"])
-    all_coeffs = lax.all_gather(coeffs, "batch", axis=0)
+    grad_coeffs, grads = mix(True, four, weights, table["turn"])
     all_grads = lax.all_gather(grads, "batch", axis=0)
     grad_weights = weight_gradient(all_coeffs, all_grads, table["turn"])
-    returned = exchange(last(exchange(grad_coeffs), table["synthesis"], degree_row, table["weight_rows"]))
-    grad_fields = gather(returned, table["forward"], cotangent[0])[None]
+    five = exchange(grad_coeffs)
+    six = exchange(last(five, table["synthesis"], degree_row, table["weight_rows"]))
+    grad_fields = gather(six, table["forward"], cotangent[0], grad_weights)[None]
     return grad_fields, grad_weights
 
 

time: 225 us -> 208 us (0.924)
  waiting for transfers between devices: 70.2 us -> 50.9 us
  blocking collectives: 61.3 us -> 69.7 us
  local copies, waits for them, and re-layouts: 10 us -> 2.2 us
    all_to_all x3, waiting for transfers between devices: 70.2 us -> 50.8 us  [exchange(): lax.all_to_all(rows.reshape(GROUPS, count, 128), 'lat', split_axis=0, con...]
    all_to_all x3, blocking collectives: 61.3 us -> 69.7 us  [exchange(): lax.all_to_all(rows.reshape(GROUPS, count, 128), 'lat', split_axis=0, con...]
    unnamed x30 -> x25, local copies, waits for them, and re-layouts: 8.83 us -> 1.77 us
  transfers between devices with their start and end apart: 5 -> 5, of which waited for: 3 -> 3; matrix products, arithmetic and copies ran while one was open for 1% -> 7% of each run, Pallas kernels for 8% -> 9%
where the time goes in v3:
time: 208 us; the launch traced here: 207 us
  blocking collectives  69.7 us (34%)
  waiting for transfers between devices  50.9 us (24%)
  Pallas kernels  30.8 us (15%)
  starting transfers between devices  27.5 us (13%)
  between operations  14.2 us (7%)
  matrix products  11.8 us (6%)
  local copies, waits for them, and re-layouts  2.2 us (1%)
    all_to_all x3, blocking collectives, exchange(): lax.all_to_all(rows.reshape(GROUPS, count, 128), 'lat', split_axis=0, con...  69.7 us
    all_to_all x3, waiting for transfers between devices, exchange(): lax.all_to_all(rows.reshape(GROUPS, count, 128), 'lat', split_axis=0, con...  50.8 us
    all_to_all x3, starting transfers between devices, exchange(): lax.all_to_all(rows.reshape(GROUPS, count, 128), 'lat', split_axis=0, con...  27.3 us
    pallas_call x1, Pallas kernels, middle(): call(middle_kernel, message(SLOT_ROWS), [VMEM, ANY, ANY, ANY, ANY, VMEM,...  10.1 us
    dot_general x1, matrix products, weight_gradient(): jnp.einsum('sjpcf,sjdf->jpcd', both, grads, preferred_element_type=f32)  7.24 us
    pallas_call x1, Pallas kernels, last(): call(last_kernel, message(LAST_ROWS), [VMEM, ANY, VMEM, VMEM], [stage_of(...  6.18 us
    pallas_call x1, Pallas kernels, spread(): call(spread_kernel, [message(SENT_ROWS), message(SLOT_ROWS), message(SLOT...  4.92 us
    pallas_call x1, Pallas kernels, first(): call(first_kernel, message(SENT_ROWS), [VMEM, ANY, VMEM, VMEM, ANY], [sta...  4.86 us
  transfers between devices with their start and end apart: 5, of which 3 were waited for; matrix products, arithmetic and copies ran while one was open for 7% of the time, Pallas kernels for 9%

profile of v3, /device:TPU:6, one launch (start us, length us, event | category | flops | bytes accessed | tf_op | source)
XLA Modules:
  0.0 207.2 jit_solution(11475377458569513816)
XLA Ops:
  7.2 4.9 %spread.1 = (bf16[3072,128]{1,0:T(8,128)(2,1)}, bf16[1536,128]{1,0:T(8,128)(2,1)}, bf16[1536,128]{1,0:T(8,128)(2,1)}) custom-call(bf16[3,384,384]{2,1,0:T(8,128)(2,1)} %bitcast.47, bf16[3,384,384]{2,1,0:T(8,128)(2,1)} %bitcast.36, bf16[384,256]{1,0:T(8,128)(2,1)} %constant.19.clone.forward), custom_call_target="tpu_custom_call" | custom-call | flops 300000000 | bytes 4000000 | tf_op jit(solution)/shard_map/spread/pallas_call | solution.py:508
  12.1 0.0 copy-start.5
  12.1 16.7 %all-to-all-start = ((bf16[64,48,128]{2,1,0:T(8,128)(2,1)}), bf16[64,48,128]{2,1,0:T(8,128)(2,1)S(1)}, u32[]{:S(2)}, u32[]{:S(2)}) async-start(bf16[64,48,128]{2,1,0:T(8,128)(2,1)} %bitcast.49), calls=%async_computation | async-start | bytes 1572864 | tf_op jit(solution)/shard_map/all_to_all | solution.py:574
  28.9 0.0 all-gather.5.cloned.1.call-start
  28.9 0.1 reshape.45
  29.0 0.1 copy.34
  29.1 0.2 broadcast_in_dim_reshape.8.degree_col
  29.3 1.7 copy.35
  31.0 22.1 %all-to-all-done.one = bf16[64,48,128]{2,1,0:T(8,128)(2,1)S(1)} async-done(((bf16[64,48,128]{2,1,0:T(8,128)(2,1)}), bf16[64,48,128]{2,1,0:T(8,128)(2,1)S(1)}, u32[]{:S(2)}, u32[]{:S(2)}) %all-to-all-start) | async-done | bytes 786464 | tf_op jit(solution)/shard_map/all_to_all | solution.py:574
  53.1 4.9 %first.1 = bf16[3072,128]{1,0:T(8,128)(2,1)S(1)} custom-call(bf16[3072,128]{1,0:T(8,128)(2,1)S(1)} %bitcast.35, bf16[9216,192]{1,0:T(8,128)(2,1)} %constant.17.clone.analysis, s32[128,1]{1,0:T(8,128)S(1)} %broadcast_in_dim_reshape.8.degree_col, bf16[1536,128]{1,0:T(8,128)(2,1)S(1)} %copy-done.5, bf16[2,2,384,384]{3,2,1,0:T(8,128)(2,1)S(1)} %bitcast.32), custom_call_target="tpu_custom_call" | custom-call | flops 1000000000 | bytes 6000000 | tf_op jit(solution)/shard_map/first/pallas_call | solution.py:518
  57.9 0.0 copy-start.6
  58.0 0.0 copy-start.7
  58.0 29.8 %all_to_all.30.two = bf16[64,48,128]{2,1,0:T(8,128)(2,1)S(1)} all-to-all(bf16[64,48,128]{2,1,0:T(8,128)(2,1)S(1)} %bitcast.39), channel_id=1, replica_groups=mesh['lat'=64,'batch'=8] {'lat'}, dimensions={0} | all-to-all | bytes 1572864 | tf_op jit(solution)/shard_map/all_to_all | solution.py:574
  87.8 2.0 mix.1
  89.8 0.0 all-gather.5.cloned.1.call-update
  89.8 5.9 %all-to-all-start.2 = ((bf16[64,48,128]{2,1,0:T(8,128)(2,1)}), bf16[64,48,128]{2,1,0:T(8,128)(2,1)S(1)}, u32[]{:S(2)}, u32[]{:S(2)}) async-start(bf16[64,48,128]{2,1,0:T(8,128)(2,1)} %bitcast.8), calls=%async_computation.2 | async-start | bytes 1572864 | tf_op jit(solution)/shard_map/all_to_all | solution.py:574
  95.7 0.2 all-gather.7.cloned.1.call-start
  95.9 0.1 broadcast_in_dim_reshape.7.degree_row
  96.0 22.5 %all-to-all-done.2 = bf16[64,48,128]{2,1,0:T(8,128)(2,1)S(1)} async-done(((bf16[64,48,128]{2,1,0:T(8,128)(2,1)}), bf16[64,48,128]{2,1,0:T(8,128)(2,1)S(1)}, u32[]{:S(2)}, u32[]{:S(2)}) %all-to-all-start.2) | async-done | bytes 786464 | tf_op jit(solution)/shard_map/all_to_all | solution.py:574
  118.5 10.1 %middle.1 = bf16[1536,128]{1,0:T(8,128)(2,1)S(1)} custom-call(bf16[3072,128]{1,0:T(8,128)(2,1)S(1)} %bitcast.38, bf16[64,48,128]{2,1,0:T(8,128)(2,1)S(1)} %all-to-all-done.one, bf16[64,48,128]{2,1,0:T(8,128)(2,1)S(1)} %all_to_all.30.two, bf16[9216,192]{1,0:T(8,128)(2,1)} %constant.16.clone.analysis, bf16[12288,256]{1,0:T(8,128)(2,1)} %constant.18.clone.synthesis, ...), custom_call_target="tpu_custom_call" | custom-call | flops 3000000000 | bytes 12000000 | tf_op jit(solution)/shard_map/middle/pallas_call | solution.py:528
  128.6 0.0 copy-start.9
  128.7 20.9 %all_to_all.31 = bf16[64,24,128]{2,1,0:T(8,128)(2,1)S(1)} all-to-all(bf16[64,24,128]{2,1,0:T(8,128)(2,1)S(1)} %bitcast.41), channel_id=1, replica_groups=mesh['lat'=64,'batch'=8] {'lat'}, dimensions={0} | all-to-all | bytes 786432 | tf_op jit(solution)/shard_map/all_to_all | solution.py:574
  149.5 1.3 adjoint_mix.1
  150.9 0.0 all-gather.7.cloned.1.call-update
  150.9 19.0 %all_to_all.32 = bf16[64,24,128]{2,1,0:T(8,128)(2,1)S(1)} all-to-all(bf16[64,24,128]{2,1,0:T(8,128)(2,1)S(1)} %bitcast.43), channel_id=1, replica_groups=mesh['lat'=64,'batch'=8] {'lat'}, dimensions={0} | all-to-all | bytes 786432 | tf_op jit(solution)/shard_map/all_to_all | solution.py:574
  169.9 6.2 %last.1 = bf16[2560,128]{1,0:T(8,128)(2,1)} custom-call(bf16[1536,128]{1,0:T(8,128)(2,1)S(1)} %bitcast.42, bf16[12288,256]{1,0:T(8,128)(2,1)} %constant.18.clone.synthesis, s32[1,128]{1,0:T(1,128)S(1)} %broadcast_in_dim_reshape.7.degree_row, f32[192,1]{1,0:T(8,128)S(1)} %copy-done.9), custom_call_target="tpu_custom_call" | custom-call | flops 1000000000 | bytes 7000000 | tf_op jit(solution)/shard_map/last/pallas_call | solution.py:542
  176.1 4.7 %all-to-all-start.5 = ((bf16[64,40,128]{2,1,0:T(8,128)(2,1)}), bf16[64,40,128]{2,1,0:T(8,128)(2,1)S(1)}, u32[]{:S(2)}, u32[]{:S(2)}) async-start(bf16[64,40,128]{2,1,0:T(8,128)(2,1)} %bitcast.14), calls=%async_computation.5 | async-start | bytes 1310720 | tf_op jit(solution)/shard_map/all_to_all | solution.py:574
  180.7 0.0 all-gather.5.cloned.1.call-done
  180.8 4.6 %convert_bitcast_fusion = bf16[8,2,1,384,256]{4,3,1,0,2:T(8,128)(2,1)} fusion(bf16[8,2,384,256]{3,2,1,0:T(8,128)(2,1)} %bitcast.45, bf16[256,256,1,1]{1,0,3,2:T(8,128)(2,1)S(1)} %copy-done.10), kind=kOutput, calls=%fused_computation.4 | convolution fusion | flops 806879232 | bytes 6422528 | tf_op jit(solution)/shard_map/sjcf,fe->sjce/dot_general | solution.py:581
  185.4 7.2 %bitcast_convert_fusion.weight_grads = bf16[2,2,384,384]{3,2,1,0:T(8,128)(2,1)S(1)} fusion(bf16[8,2,384,256,1]{3,2,1,0,4:T(8,128)(2,1)} %bitcast.51, bf16[8,2,1,384,256]{4,3,1,0,2:T(8,128)(2,1)} %convert_bitcast_fusion, bf16[8,2,1,384,256]{4,3,1,0,2:T(8,128)(2,1)} %bitcast.46), kind=kOutput, calls=%fused_computation.5 | convolution fusion | flops 2419654656 | bytes 10616832 | tf_op jit(solution)/shard_map/sjpcf,sjdf->jpcd/dot_general | solution.py:583
  192.6 6.3 %all-to-all-done.5 = bf16[64,40,128]{2,1,0:T(8,128)(2,1)S(1)} async-done(((bf16[64,40,128]{2,1,0:T(8,128)(2,1)}), bf16[64,40,128]{2,1,0:T(8,128)(2,1)S(1)}, u32[]{:S(2)}, u32[]{:S(2)}) %all-to-all-start.5) | async-done | bytes 655392 | tf_op jit(solution)/shard_map/all_to_all | solution.py:574
  198.9 1.5 gather.1
  (21 shorter events, 0.0 us)
Async XLA Ops:
  7.2 21.7 %copy-start.11 = (s32[128]{0:T(128)S(1)}, s32[128]{0:T(128)}, u32[]{:S(2)}) copy-start(s32[128]{0:T(128)} %param.15) | copy-start | bytes 1540
  12.1 41.0 %copy-start.5 = (bf16[1536,128]{1,0:T(8,128)(2,1)S(1)}, bf16[1536,128]{1,0:T(8,128)(2,1)}, u32[]{:S(2)}) copy-start(bf16[1536,128]{1,0:T(8,128)(2,1)} %get-tuple-element.10.carried) | copy-start | bytes 1179652
  12.1 40.9 %all-to-all-start = ((bf16[64,48,128]{2,1,0:T(8,128)(2,1)}), bf16[64,48,128]{2,1,0:T(8,128)(2,1)S(1)}, u32[]{:S(2)}, u32[]{:S(2)}) async-start(bf16[64,48,128]{2,1,0:T(8,128)(2,1)} %bitcast.49), calls=%async_computation | async-start | bytes 1572864 | tf_op jit(solution)/shard_map/all_to_all | solution.py:574
  28.9 151.9 %all-gather.5.cloned.1.call-start = ((), (), s32[]{:S(2)}) async-start(), calls=%async_computation.6 | async-start | bytes 3538944 | tf_op jit(solution)/shard_map/all_gather | solution.py:596
  53.1 34.7 %copy-start.4 = (bf16[1536,128]{1,0:T(8,128)(2,1)S(1)}, bf16[1536,128]{1,0:T(8,128)(2,1)}, u32[]{:S(2)}) copy-start(bf16[1536,128]{1,0:T(8,128)(2,1)} %get-tuple-element.11.rest_0_) | copy-start | bytes 1179652
  53.1 34.7 %copy-start.8 = (bf16[256,256]{1,0:T(8,128)(2,1)S(1)}, bf16[256,256]{1,0:T(8,128)(2,1)}, u32[]{:S(2)}) copy-start(bf16[256,256]{1,0:T(8,128)(2,1)} %constant.22.clone.turn) | copy-start | bytes 393220
  57.9 60.6 %copy-start.6 = (bf16[384,256]{1,0:T(8,128)(2,1)S(1)}, bf16[384,256]{1,0:T(8,128)(2,1)}, u32[]{:S(2)}) copy-start(bf16[384,256]{1,0:T(8,128)(2,1)} %constant.20.clone.inverse) | copy-start | bytes 589828
  58.0 60.6 %copy-start.7 = (bf16[256,384]{1,0:T(8,128)(2,1)S(1)}, bf16[256,384]{1,0:T(8,128)(2,1)}, u32[]{:S(2)}) copy-start(bf16[256,384]{1,0:T(8,128)(2,1)} %constant.21.clone.inverse_t) | copy-start | bytes 589828
  89.8 28.7 %all-to-all-start.2 = ((bf16[64,48,128]{2,1,0:T(8,128)(2,1)}), bf16[64,48,128]{2,1,0:T(8,128)(2,1)S(1)}, u32[]{:S(2)}, u32[]{:S(2)}) async-start(bf16[64,48,128]{2,1,0:T(8,128)(2,1)} %bitcast.8), calls=%async_computation.2 | async-start | bytes 1572864 | tf_op jit(solution)/shard_map/all_to_all | solution.py:574
  95.7 89.6 %all-gather.7.cloned.1.call-start = ((), (), s32[]{:S(2)}) async-start(), calls=%async_computation.7 | async-start | bytes 3538944 | tf_op jit(solution)/shard_map/all_gather | solution.py:606
  118.5 31.0 %copy-start.1 = (bf16[2,2,384,384]{3,2,1,0:T(8,128)(2,1)S(1)}, bf16[2,2,384,384]{3,2,1,0:T(8,128)(2,1)}, u32[]{:S(2)}) copy-start(bf16[2,2,384,384]{3,2,1,0:T(8,128)(2,1)} %weights.1) | copy-start | bytes 3538948
  128.6 41.2 %copy-start.9 = (f32[192,1]{1,0:T(8,128)S(1)}, f32[192,1]{1,0:T(8,128)}, u32[]{:S(2)}) copy-start(f32[192,1]{1,0:T(8,128)} %constant.23.clone.weight_rows) | copy-start | bytes 2308
  169.9 10.9 %copy-start.10 = (bf16[256,256,1,1]{1,0,3,2:T(8,128)(2,1)S(1)}, bf16[256,256,1,1]{1,0,3,2:T(8,128)(2,1)}, u32[]{:S(2)}) copy-start(bf16[256,256,1,1]{1,0,3,2:T(8,128)(2,1)} %constant.27) | copy-start | bytes 393220
  176.1 22.8 %all-to-all-start.5 = ((bf16[64,40,128]{2,1,0:T(8,128)(2,1)}), bf16[64,40,128]{2,1,0:T(8,128)(2,1)S(1)}, u32[]{:S(2)}, u32[]{:S(2)}) async-start(bf16[64,40,128]{2,1,0:T(8,128)(2,1)} %bitcast.14), calls=%async_computation.5 | async-start | bytes 1310720 | tf_op jit(solution)/shard_map/all_to_all | solution.py:574
  185.4 13.6 %copy-start = (bf16[1,3,384,384]{3,2,1,0:T(8,128)(2,1)S(1)}, bf16[1,3,384,384]{3,2,1,0:T(8,128)(2,1)}, u32[]{:S(2)}) copy-start(bf16[1,3,384,384]{3,2,1,0:T(8,128)(2,1)} %param.13) | copy-start | bytes 2654212
  185.4 13.6 %copy-start.3 = (bf16[384,256]{1,0:T(8,128)(2,1)S(1)}, bf16[384,256]{1,0:T(8,128)(2,1)}, u32[]{:S(2)}) copy-start(bf16[384,256]{1,0:T(8,128)(2,1)} %constant.19.clone.forward) | copy-start | bytes 589828
  192.6 7.8 %copy-start.2 = (bf16[2,2,384,384]{3,2,1,0:T(8,128)(2,1)}, bf16[2,2,384,384]{3,2,1,0:T(8,128)(2,1)S(1)}, u32[]{:S(2)}) copy-start(bf16[2,2,384,384]{3,2,1,0:T(8,128)(2,1)S(1)} %bitcast_convert_fusion.weight_grads) | copy-start | bytes 3538948
Sparse Core Ops, SparseCore 0:
  89.9 25.8 all-gather.4
  151.0 24.6 all-gather.6

commit v4 on v3

--- a/solution.py
+++ b/solution.py
@@ -25,9 +25,12 @@
 COT_CUTS = (0, 12, 36, 54)
 SLOT_ROWS = SLOTS * PARTS * 2
 LAST_ROWS = 40
-REACH = [DEGREES - 16 * t for t in range(BLOCKS)]
+HALF = GROUPS // 2
+LOW = LATS // 2
+REACH = [DEGREES // 2 - 8 * t for t in range(BLOCKS)]
 STARTS = [16 * sum(REACH[:t]) for t in range(BLOCKS + 1)]
-PAIR_ROWS = 8 * LATS
+STEPS = [8 * LOW * t for t in range(BLOCKS + 1)]
+PLACES = [*range(HALF), *range(GROUPS - 1, HALF - 1, -1)]
 
 f32 = jnp.float32
 bf16 = jnp.bfloat16
@@ -72,22 +75,30 @@
 @functools.cache
 def constants():
     table, quadrature = legendre_table()
-    where = np.arange(LATS).reshape(GROUPS, BAND).T.reshape(-1)
-    table = table[:, :, where]
-
-    def by_block(values):
+    where = (np.array(PLACES)[None, :] * BAND + np.arange(BAND)[:, None]).reshape(-1)
+    low = (np.arange(HALF)[None, :] * BAND + np.arange(BAND)[:, None]).reshape(-1)
+
+    def for_analysis(values):
         values = values.astype(bf16)
         return np.concatenate(
-            [values[16 * t + k, 16 * t :] for t in range(BLOCKS) for k in range(16)], axis=0
+            [
+                np.concatenate([values[16 * t + k + 8 * g, 16 * t + odd :: 2] for g in (0, 1)], axis=1)
+                for t in range(BLOCKS)
+                for odd in (0, 1)
+                for k in range(8)
+            ],
+            axis=0,
         )
 
-    analysis, weighted = by_block(table), by_block(table * quadrature[where])
-    table = table.astype(bf16)
+    analysis = for_analysis(table[:, :, low])
+    weighted = for_analysis((table * quadrature)[:, :, low])
+    below = table[:, :, low].astype(bf16)
     synthesis = np.concatenate(
         [
-            np.concatenate([table[16 * t + k].T, table[16 * t + k + 8].T], axis=1)
+            np.concatenate([below[16 * t + k + 4 * g, odd::2].T for g in range(4)], axis=1)
             for t in range(BLOCKS)
-            for k in range(8)
+            for odd in (0, 1)
+            for k in range(4)
         ],
         axis=0,
     )
@@ -178,42 +189,75 @@
     return tiles
 
 
-def analyse(tiles, table, ready, rows_each=4):
+def order_sign(lanes):
+    return jnp.where((lanes // 2) % 2 == 0, 1.0, -1.0).astype(f32)
+
+
+def fold(x):
+    low = jnp.concatenate([x[i * GROUPS : i * GROUPS + HALF] for i in range(BAND)], axis=0)
+    high = jnp.concatenate(
+        [x[i * GROUPS + HALF : (i + 1) * GROUPS] for i in reversed(range(BAND))], axis=0
+    )
+    high = high * order_sign(lane_of(high.shape))
+    return low + high, low - high
+
+
+def unfold(even, odd):
+    low = even + odd
+    high = (even - odd) * order_sign(lane_of(low.shape))
+    pieces = []
+    for i in range(BAND):
+        pieces.append(low[i * HALF : (i + 1) * HALF])
+        pieces.append(high[(BAND - 1 - i) * HALF : (BAND - i) * HALF])
+    return jnp.concatenate(pieces, axis=0)
+
+
+def stacked(operand, groups, width):
+    order = (lane_of(operand.shape) % 32) // 2
+    none = jnp.zeros_like(operand)
+    return jnp.concatenate(
+        [jnp.where(order // width == g, operand, none) for g in range(groups)], axis=0
+    )
+
+
+def analyse(parts, table, ready):
+    folded = [[fold(x) for x in pair] for pair in parts]
+    tiles = [as_bf16(to_tiles([[x[odd] for x in pair] for pair in folded])) for odd in (0, 1)]
     sums = []
     for t in range(BLOCKS):
         ready(t)
-        operand = block_operand(tiles, t)
         reach = REACH[t]
-        order = (lane_of((reach, 256)) % 32) // 2
-        total = jnp.zeros((reach, 256), f32)
-        for k in range(0, 16, rows_each):
-            part = dot(table[pl.ds(STARTS[t] + k * reach, rows_each * reach), :], operand)
-            for n in range(rows_each):
-                total = jnp.where(order == k + n, part[n * reach : (n + 1) * reach], total)
-        if t:
-            total = jnp.concatenate([jnp.zeros((16 * t, 256), f32), total], axis=0)
-        sums.append(total)
+        order = (lane_of((reach, 256)) % 16) // 2
+        pieces = []
+        for odd in (0, 1):
+            operand = stacked(block_operand(tiles[odd], t), 2, 8)
+            rows = pl.ds(STARTS[t] + odd * 8 * reach, 8 * reach)
+            part = dot(table[rows, :], operand)
+            total = part[:reach]
+            for k in range(1, 8):
+                total = jnp.where(order == k, part[k * reach : (k + 1) * reach], total)
+            if t:
+                pieces.append(jnp.zeros((8 * t, 256), f32))
+            pieces.append(total)
+        sums.append(jnp.concatenate(pieces, axis=0))
     return merge_blocks(sums)
 
 
-def synthesise(tiles, table, ready, rows_each=2):
-    sums = []
+def synthesise(tiles, table, ready):
+    sums = ([], [])
+    order = (lane_of((LOW, 256)) % 8) // 2
     for t in range(BLOCKS):
         ready(t)
         operand = block_operand(tiles, t)
-        low = (lane_of((DEGREES, 256)) % 32) < 16
-        none = jnp.zeros_like(operand)
-        stacked = jnp.concatenate(
-            [jnp.where(low, operand, none), jnp.where(low, none, operand)], axis=0
-        )
-        order = (lane_of((LATS, 256)) % 16) // 2
-        total = jnp.zeros((LATS, 256), f32)
-        for k in range(0, 8, rows_each):
-            part = dot(table[pl.ds(t * PAIR_ROWS + k * LATS, rows_each * LATS), :], stacked)
-            for n in range(rows_each):
-                total = jnp.where(order == k + n, part[n * LATS : (n + 1) * LATS], total)
-        sums.append(total)
-    return merge_blocks(sums)
+        for odd in (0, 1):
+            rows = operand[odd * GROUPS : (odd + 1) * GROUPS]
+            part = dot(table[pl.ds(STEPS[t] + odd * 4 * LOW, 4 * LOW), :], stacked(rows, 4, 4))
+            total = part[:LOW]
+            for k in range(1, 4):
+                total = jnp.where(order == k, part[k * LOW : (k + 1) * LOW], total)
+            sums[odd].append(total)
+    even, odd = merge_blocks(sums[0]), merge_blocks(sums[1])
+    return from_tiles([tuple(unfold(x, y) for x, y in zip(e, o)) for e, o in zip(even, odd)])
 
 
 def permute_rows(matrix, tiles):
@@ -260,13 +304,14 @@
 
 
 def slot_rows_out(tiles, degree_col, carried, stage, out):
-    pick = (degree_col[...] == lane_of((DEGREES, DEGREES))).astype(f32).astype(bf16)
+    row = lane_of((DEGREES, DEGREES))
+    pick = (degree_col[...] == 2 * (row % GROUPS) + row // GROUPS).astype(f32).astype(bf16)
     put_slots(from_tiles(permute_rows(pick, as_bf16(tiles))), carried, stage, out)
 
 
 def slot_rows_in(received, degree_row, stage):
-    rows = lax.broadcasted_iota(jnp.int32, (DEGREES, DEGREES), 0)
-    pick = (rows == degree_row[...]).astype(f32).astype(bf16)
+    row = lax.broadcasted_iota(jnp.int32, (DEGREES, DEGREES), 0)
+    pick = (degree_row[...] == 2 * (row % GROUPS) + row // GROUPS).astype(f32).astype(bf16)
     return as_bf16(permute_rows(pick, as_bf16(to_tiles(get_slots(received, stage)))))
 
 
@@ -278,17 +323,18 @@
     return copies
 
 
-PAIR_STARTS = [PAIR_ROWS * t for t in range(BLOCKS + 1)]
-
-
 def cot_place(i, q, h):
     row = (i * PARTS + q) * 3 + h
     which = sum(row >= cut for cut in COT_CUTS[1:3])
     return which, row - COT_CUTS[which]
 
 
-def spread_kernel(fields, cotangent, forward, out, cot_two, cot_three, field, cot, stages, sems):
+def spread_kernel(
+    fields, cotangent, forward_source, out, cot_two, cot_three, field, cot, forward, stages, sems
+):
     copies = []
+    fetch = pltpu.make_async_copy(forward_source, forward, sems.at[2 * BAND])
+    fetch.start()
     for i in range(BAND):
         copies.append(
             (
@@ -302,6 +348,8 @@
     stage, stage_two, stage_three = stages.at[0], stages.at[1], stages.at[2]
     spots = ((stage, SPEC_ROWS, SENT_ROWS), (stage_two, 0, SLOT_ROWS), (stage_three, 0, SLOT_ROWS))
     for i in range(BAND):
+        if i == 0:
+            fetch.wait()
         copies[i][0].wait()
         spectra = dot(field[i], forward[...], TN)
         for q in range(PARTS):
@@ -349,8 +397,7 @@
         ]
         for q in range(PARTS)
     ]
-    tiles = as_bf16(to_tiles(parts))
-    sums = analyse(tiles, table, lambda t: copies[t].wait())
+    sums = analyse(parts, table, lambda t: copies[t].wait())
     slot_rows_out(sums, degree_col, carried, stage, out)
 
 
@@ -362,19 +409,21 @@
 
 
 def middle_kernel(
-    received, one, two, analysis, synthesis, degree_row, degree_col, inverse, inverse_t, out,
-    rows_one, rows_two, stage_one, stage_two, stage, table, table_s, row_sems, sems, sems_s,
+    received, one, two, analysis, synthesis, degree_row, degree_col, inverse_source, turned_source, out,
+    inverse, inverse_t, rows_one, rows_two, stage_one, stage_two, stage, table, table_s, row_sems, sems, sems_s,
 ):
-    copies_s = table_copies(synthesis, table_s, sems_s, PAIR_STARTS)
+    copies_s = table_copies(synthesis, table_s, sems_s, STEPS)
     copies = table_copies(analysis, table, sems, STARTS)
     fetches = (
         pltpu.make_async_copy(one.at[:, pl.ds(32, 16), :], rows_one, row_sems.at[0]),
         pltpu.make_async_copy(two.at[:, pl.ds(16, 32), :], rows_two, row_sems.at[1]),
+        pltpu.make_async_copy(inverse_source, inverse, row_sems.at[2]),
+        pltpu.make_async_copy(turned_source, inverse_t, row_sems.at[3]),
     )
     for copy in (*copies_s, *fetches, *copies):
         copy.start()
     tiles = slot_rows_in(received, degree_row, stage)
-    synth = from_tiles(synthesise(tiles, table_s, lambda t: copies_s[t].wait()))
+    synth = synthesise(tiles, table_s, lambda t: copies_s[t].wait())
     for fetch in fetches:
         fetch.wait()
     stage_one[...] = rows_one[...].astype(f32).reshape(GROUPS * 16, 128)
@@ -399,16 +448,16 @@
         upstream = (cotangent * gelu_slope(response)).astype(bf16)
         grad = dot(upstream, inverse[...])
         parts.append([grad[:, :128], grad[:, 128:]])
-    sums = analyse(as_bf16(to_tiles(parts)), table, lambda t: copies[t].wait())
+    sums = analyse(parts, table, lambda t: copies[t].wait())
     slot_rows_out(sums, degree_col, None, stage, out)
 
 
 def last_kernel(received, synthesis, degree_row, weight_rows, out, stage, stage_out, table_s, sems_s):
-    copies_s = table_copies(synthesis, table_s, sems_s, PAIR_STARTS)
+    copies_s = table_copies(synthesis, table_s, sems_s, STEPS)
     for copy in copies_s:
         copy.start()
     tiles = slot_rows_in(received, degree_row, stage)
-    synth = from_tiles(synthesise(tiles, table_s, lambda t: copies_s[t].wait()))
+    synth = synthesise(tiles, table_s, lambda t: copies_s[t].wait())
     for q in range(PARTS):
         for h in range(2):
             scaled = synth[q][h] * weight_rows[...]
@@ -473,7 +522,7 @@
 ANY = pl.BlockSpec(memory_space=pl.ANY)
 
 
-def call(kernel, out_shape, in_specs, scratch, flops, moved, name, limit=50):
+def call(kernel, out_shape, in_specs, scratch, flops, moved, name, limit=24):
     several = isinstance(out_shape, list)
     return pl.pallas_call(
         kernel,
@@ -496,11 +545,15 @@
 
 
 TABLE = pltpu.VMEM((STARTS[-1], LATS), bf16)
-TABLE_S = pltpu.VMEM((PAIR_STARTS[-1], 256), bf16)
+TABLE_S = pltpu.VMEM((STEPS[-1], 256), bf16)
 
 
 def sems(count):
     return pltpu.SemaphoreType.DMA((count,))
+
+
+def in_hbm(array):
+    return pltpu.with_memory_space_constraint(array, pltpu.HBM)
 
 
 def spread(fields, cotangent, forward):
@@ -508,10 +561,13 @@
     return call(
         spread_kernel,
         [message(SENT_ROWS), message(SLOT_ROWS), message(SLOT_ROWS)],
-        [ANY, ANY, VMEM],
-        [cycle, cycle, pltpu.VMEM((3, GROUPS * SENT_ROWS, 128), f32), sems(2 * BAND)],
-        3 * 10**8, 4 * 10**6, "spread", 60,
-    )(fields, cotangent, forward)
+        [ANY, ANY, ANY],
+        [
+            cycle, cycle, pltpu.VMEM((LONS, COEFS), bf16),
+            pltpu.VMEM((3, GROUPS * SENT_ROWS, 128), f32), sems(2 * BAND + 1),
+        ],
+        3 * 10**8, 4 * 10**6, "spread",
+    )(in_hbm(fields), in_hbm(cotangent), in_hbm(forward))
 
 
 def first(received, weighted, degree_col, carried, early):
@@ -521,21 +577,23 @@
         [VMEM, ANY, VMEM, VMEM, ANY],
         [stage_of(SENT_ROWS), stage_of(SENT_ROWS), TABLE, sems(BLOCKS)],
         10**9, 6 * 10**6, "first",
-    )(received, weighted, degree_col, carried, early)
+    )(received, in_hbm(weighted), degree_col, carried, early)
 
 
 def middle(received, one, two, analysis, synthesis, degree_row, degree_col, inverse, inverse_t):
     return call(
         middle_kernel,
         message(SLOT_ROWS),
-        [VMEM, ANY, ANY, ANY, ANY, VMEM, VMEM, VMEM, VMEM],
+        [VMEM, ANY, ANY, ANY, ANY, VMEM, VMEM, ANY, ANY],
         [
+            pltpu.VMEM((LONS, COEFS), bf16), pltpu.VMEM((COEFS, LONS), bf16),
             pltpu.VMEM((GROUPS, 16, 128), bf16), pltpu.VMEM((GROUPS, 32, 128), bf16),
             stage_of(16), stage_of(32), stage_of(SENT_ROWS),
-            TABLE, TABLE_S, sems(2), sems(BLOCKS), sems(BLOCKS),
+            TABLE, TABLE_S, sems(4), sems(BLOCKS), sems(BLOCKS),
         ],
         3 * 10**9, 12 * 10**6, "middle",
-    )(received, one, two, analysis, synthesis, degree_row, degree_col, inverse, inverse_t)
+    )(received, one, two, in_hbm(analysis), in_hbm(synthesis), degree_row, degree_col,
+      in_hbm(inverse), in_hbm(inverse_t))
 
 
 def last(received, synthesis, degree_row, weight_rows):
@@ -545,7 +603,7 @@
         [VMEM, ANY, VMEM, VMEM],
         [stage_of(SLOT_ROWS), stage_of(LAST_ROWS), TABLE_S, sems(BLOCKS)],
         10**9, 7 * 10**6, "last",
-    )(received, synthesis, degree_row, weight_rows)
+    )(received, in_hbm(synthesis), degree_row, weight_rows)
 
 
 def gather(received, forward, cotangent, weight_grads):
@@ -572,7 +630,8 @@
 def exchange(rows):
     count = rows.shape[0] // GROUPS
     out = lax.all_to_all(
-        rows.reshape(GROUPS, count, 128), "lat", split_axis=0, concat_axis=0, tiled=True
+        rows.reshape(GROUPS, count, 128), "lat", split_axis=0, concat_axis=0, tiled=True,
+        axis_index_groups=[PLACES],
     )
     return out.reshape(GROUPS * count, 128)
 
@@ -586,7 +645,8 @@
 
 def local(fields, cotangent, weights, degree_of):
     table = {k: jnp.asarray(v) for k, v in constants().items()}
-    slots = degree_of.reshape(GROUPS, SLOTS).T.reshape(DEGREES)
+    slots = degree_of.reshape(GROUPS, SLOTS)
+    slots = jnp.concatenate([slots[:HALF], slots[HALF:][::-1]], axis=0).T.reshape(DEGREES)
     degree_col, degree_row = slots[:, None], slots[None, :]
     turned_weights = jnp.swapaxes(weights, 2, 3)
     sent, cot_two, cot_three = spread(fields[0], cotangent[0], table["forward"])

time: 208 us -> 212 us (1.019)
  waiting for transfers between devices: 50.9 us -> 59 us
  Pallas kernels: 30.8 us -> 26.7 us
    all_to_all x3, waiting for transfers between devices: 50.8 us -> 58.9 us  [exchange(): lax.all_to_all(rows.reshape(GROUPS, count, 128), 'lat', split_axis=0, con...]
  transfers between devices with their start and end apart: 5 -> 5, of which waited for: 3 -> 3; matrix products, arithmetic and copies ran while one was open for 7% -> 7% of each run, Pallas kernels for 9% -> 7%
where the time goes in v4:
time: 212 us; the launch traced here: 211 us
  blocking collectives  70.9 us (33%)
  waiting for transfers between devices  59 us (28%)
  Pallas kernels  26.7 us (13%)
  starting transfers between devices  26.4 us (12%)
  between operations  14.2 us (7%)
  matrix products  11.8 us (6%)
  local copies, waits for them, and re-layouts  2.41 us (1%)
    all_to_all x3, blocking collectives, exchange(): lax.all_to_all(rows.reshape(GROUPS, count, 128), 'lat', split_axis=0, con...  70.9 us
    all_to_all x3, waiting for transfers between devices, exchange(): lax.all_to_all(rows.reshape(GROUPS, count, 128), 'lat', split_axis=0, con...  58.9 us
    all_to_all x3, starting transfers between devices, exchange(): lax.all_to_all(rows.reshape(GROUPS, count, 128), 'lat', split_axis=0, con...  26.1 us
    pallas_call x1, Pallas kernels, middle(): call(middle_kernel, message(SLOT_ROWS), [VMEM, ANY, ANY, ANY, ANY, VMEM,...  8.6 us
    dot_general x1, matrix products, weight_gradient(): jnp.einsum('sjpcf,sjdf->jpcd', both, grads, preferred_element_type=f32)  7.24 us
    pallas_call x1, Pallas kernels, last(): call(last_kernel, message(LAST_ROWS), [VMEM, ANY, VMEM, VMEM], [stage_of(...  5.29 us
    dot_general x1, matrix products, weight_gradient(): jnp.einsum('sjcf,fe->sjce', coeffs, turn, preferred_element_type=f32)  4.58 us
  transfers between devices with their start and end apart: 5, of which 3 were waited for; matrix products, arithmetic and copies ran while one was open for 7% of the time, Pallas kernels for 7%

profile of v4, /device:TPU:6, one launch (start us, length us, event | category | flops | bytes accessed | tf_op | source)
XLA Modules:
  0.0 211.5 jit_solution(3339505956168500048)
XLA Ops:
  7.2 3.9 %spread.1 = (bf16[3072,128]{1,0:T(8,128)(2,1)}, bf16[1536,128]{1,0:T(8,128)(2,1)S(1)}, bf16[1536,128]{1,0:T(8,128)(2,1)S(1)}) custom-call(bf16[3,384,384]{2,1,0:T(8,128)(2,1)} %bitcast.48, bf16[3,384,384]{2,1,0:T(8,128)(2,1)} %bitcast.35, bf16[384,256]{1,0:T(8,128)(2,1)} %constant.19.clone.forward_source.forward), custom_call_target="tpu_custom_call" | custom-call | flops 300000000 | bytes 4000000 | tf_op jit(solution)/shard_map/spread/pallas_call | solution.py:561
  11.1 16.6 %all-to-all-start = ((bf16[64,48,128]{2,1,0:T(8,128)(2,1)}), bf16[64,48,128]{2,1,0:T(8,128)(2,1)S(1)}, u32[]{:S(2)}, u32[]{:S(2)}) async-start(bf16[64,48,128]{2,1,0:T(8,128)(2,1)} %bitcast.2), calls=%async_computation | async-start | bytes 1572864 | tf_op jit(solution)/shard_map/all_to_all | solution.py:632
  27.7 0.0 all-gather.5.cloned.1.call-start
  27.8 0.1 fusion.7
  27.8 0.1 slice.31
  28.0 0.1 copy.35
  28.0 0.1 slice.29
  28.2 0.1 copy.34
  28.2 0.1 add_bitcast_fusion
  28.3 0.1 broadcast_in_dim_reshape.8.degree_col
  28.5 1.7 copy.36
  30.2 24.2 %all-to-all-done.one = bf16[64,48,128]{2,1,0:T(8,128)(2,1)S(1)} async-done(((bf16[64,48,128]{2,1,0:T(8,128)(2,1)}), bf16[64,48,128]{2,1,0:T(8,128)(2,1)S(1)}, u32[]{:S(2)}, u32[]{:S(2)}) %all-to-all-start) | async-done | bytes 786464 | tf_op jit(solution)/shard_map/all_to_all | solution.py:632
  54.4 4.1 %first.1 = bf16[3072,128]{1,0:T(8,128)(2,1)S(1)} custom-call(bf16[3072,128]{1,0:T(8,128)(2,1)S(1)} %bitcast.38, bf16[4608,192]{1,0:T(8,128)(2,1)} %constant.17.clone.analysis, s32[128,1]{1,0:T(8,128)S(1)} %broadcast_in_dim_reshape.8.degree_col, bf16[1536,128]{1,0:T(8,128)(2,1)S(1)} %get-tuple-element.10.carried, bf16[2,2,384,384]{3,2,1,0:T(8,128)(2,1)S(1)} %bitcast.33), custom_call_target="tpu_custom_call" | custom-call | flops 1000000000 | bytes 6000000 | tf_op jit(solution)/shard_map/first/pallas_call | solution.py:574
  58.5 29.9 %all_to_all.30.two = bf16[64,48,128]{2,1,0:T(8,128)(2,1)S(1)} all-to-all(bf16[64,48,128]{2,1,0:T(8,128)(2,1)S(1)} %bitcast.39), channel_id=1, replica_groups={{0,8,16,24,32,40,48,56,64,72,80,88,96,104,112,120,128,136,144,152,160,1..., dimensions={0} | all-to-all | bytes 1572864 | tf_op jit(solution)/shard_map/all_to_all | solution.py:632
  88.4 2.0 mix.1
  90.3 0.0 all-gather.5.cloned.1.call-update
  90.4 4.7 %all-to-all-start.2 = ((bf16[64,48,128]{2,1,0:T(8,128)(2,1)}), bf16[64,48,128]{2,1,0:T(8,128)(2,1)S(1)}, u32[]{:S(2)}, u32[]{:S(2)}) async-start(bf16[64,48,128]{2,1,0:T(8,128)(2,1)} %bitcast.8), calls=%async_computation.2 | async-start | bytes 1572864 | tf_op jit(solution)/shard_map/all_to_all | solution.py:632
  95.0 0.2 all-gather.7.cloned.1.call-start
  95.3 0.1 broadcast_in_dim_reshape.7.degree_row
  95.3 24.6 %all-to-all-done.2 = bf16[64,48,128]{2,1,0:T(8,128)(2,1)S(1)} async-done(((bf16[64,48,128]{2,1,0:T(8,128)(2,1)}), bf16[64,48,128]{2,1,0:T(8,128)(2,1)S(1)}, u32[]{:S(2)}, u32[]{:S(2)}) %all-to-all-start.2) | async-done | bytes 786464 | tf_op jit(solution)/shard_map/all_to_all | solution.py:632
  120.0 8.6 %middle.1 = bf16[1536,128]{1,0:T(8,128)(2,1)S(1)} custom-call(bf16[3072,128]{1,0:T(8,128)(2,1)S(1)} %bitcast.42, bf16[64,48,128]{2,1,0:T(8,128)(2,1)S(1)} %all-to-all-done.one, bf16[64,48,128]{2,1,0:T(8,128)(2,1)S(1)} %all_to_all.30.two, bf16[4608,192]{1,0:T(8,128)(2,1)} %constant.16.clone.analysis, bf16[6144,256]{1,0:T(8,128)(2,1)} %constant.18.clone.synthesis, ...), custom_call_target="tpu_custom_call" | custom-call | flops 3000000000 | bytes 12000000 | tf_op jit(solution)/shard_map/middle/pallas_call | solution.py:584
  128.6 20.4 %all_to_all.31 = bf16[64,24,128]{2,1,0:T(8,128)(2,1)S(1)} all-to-all(bf16[64,24,128]{2,1,0:T(8,128)(2,1)S(1)} %bitcast.44), channel_id=1, replica_groups={{0,8,16,24,32,40,48,56,64,72,80,88,96,104,112,120,128,136,144,152,160,1..., dimensions={0} | all-to-all | bytes 786432 | tf_op jit(solution)/shard_map/all_to_all | solution.py:632
  149.0 1.3 adjoint_mix.1
  150.4 0.0 all-gather.7.cloned.1.call-update
  150.4 20.6 %all_to_all.32 = bf16[64,24,128]{2,1,0:T(8,128)(2,1)S(1)} all-to-all(bf16[64,24,128]{2,1,0:T(8,128)(2,1)S(1)} %bitcast.43), channel_id=1, replica_groups={{0,8,16,24,32,40,48,56,64,72,80,88,96,104,112,120,128,136,144,152,160,1..., dimensions={0} | all-to-all | bytes 786432 | tf_op jit(solution)/shard_map/all_to_all | solution.py:632
  171.0 5.3 %last.1 = bf16[2560,128]{1,0:T(8,128)(2,1)} custom-call(bf16[1536,128]{1,0:T(8,128)(2,1)S(1)} %bitcast.41, bf16[6144,256]{1,0:T(8,128)(2,1)} %constant.18.clone.synthesis, s32[1,128]{1,0:T(1,128)S(1)} %broadcast_in_dim_reshape.7.degree_row, f32[192,1]{1,0:T(8,128)S(1)} %copy-done.5), custom_call_target="tpu_custom_call" | custom-call | flops 1000000000 | bytes 7000000 | tf_op jit(solution)/shard_map/last/pallas_call | solution.py:600
  176.3 4.9 %all-to-all-start.5 = ((bf16[64,40,128]{2,1,0:T(8,128)(2,1)}), bf16[64,40,128]{2,1,0:T(8,128)(2,1)S(1)}, u32[]{:S(2)}, u32[]{:S(2)}) async-start(bf16[64,40,128]{2,1,0:T(8,128)(2,1)} %bitcast.14), calls=%async_computation.5 | async-start | bytes 1310720 | tf_op jit(solution)/shard_map/all_to_all | solution.py:632
  181.2 0.0 all-gather.5.cloned.1.call-done
  181.3 4.6 %convert_bitcast_fusion = bf16[8,2,1,384,256]{4,3,1,0,2:T(8,128)(2,1)} fusion(bf16[8,2,384,256]{3,2,1,0:T(8,128)(2,1)} %bitcast.46, bf16[256,256,1,1]{1,0,3,2:T(8,128)(2,1)S(1)} %copy-done.6), kind=kOutput, calls=%fused_computation.4 | convolution fusion | flops 806879232 | bytes 6422528 | tf_op jit(solution)/shard_map/sjcf,fe->sjce/dot_general | solution.py:640
  185.8 7.2 %bitcast_convert_fusion.weight_grads = bf16[2,2,384,384]{3,2,1,0:T(8,128)(2,1)S(1)} fusion(bf16[8,2,384,256,1]{3,2,1,0,4:T(8,128)(2,1)} %bitcast.50, bf16[8,2,1,384,256]{4,3,1,0,2:T(8,128)(2,1)} %convert_bitcast_fusion, bf16[8,2,1,384,256]{4,3,1,0,2:T(8,128)(2,1)} %bitcast.47), kind=kOutput, calls=%fused_computation.5 | convolution fusion | flops 2419654656 | bytes 10616832 | tf_op jit(solution)/shard_map/sjpcf,sjdf->jpcd/dot_general | solution.py:642
  193.1 10.0 %all-to-all-done.5 = bf16[64,40,128]{2,1,0:T(8,128)(2,1)S(1)} async-done(((bf16[64,40,128]{2,1,0:T(8,128)(2,1)}), bf16[64,40,128]{2,1,0:T(8,128)(2,1)S(1)}, u32[]{:S(2)}, u32[]{:S(2)}) %all-to-all-start.5) | async-done | bytes 655392 | tf_op jit(solution)/shard_map/all_to_all | solution.py:632
  203.2 1.5 gather.1
  (18 shorter events, 0.0 us)
Async XLA Ops:
  7.2 20.6 %copy-start.7 = (s32[128]{0:T(128)S(1)}, s32[128]{0:T(128)}, u32[]{:S(2)}) copy-start(s32[128]{0:T(128)} %param.15) | copy-start | bytes 1540
  11.1 43.3 %all-to-all-start = ((bf16[64,48,128]{2,1,0:T(8,128)(2,1)}), bf16[64,48,128]{2,1,0:T(8,128)(2,1)S(1)}, u32[]{:S(2)}, u32[]{:S(2)}) async-start(bf16[64,48,128]{2,1,0:T(8,128)(2,1)} %bitcast.2), calls=%async_computation | async-start | bytes 1572864 | tf_op jit(solution)/shard_map/all_to_all | solution.py:632
  27.7 153.5 %all-gather.5.cloned.1.call-start = ((), (), s32[]{:S(2)}) async-start(), calls=%async_computation.6 | async-start | bytes 3538944 | tf_op jit(solution)/shard_map/all_gather | solution.py:656
  54.4 34.0 %copy-start.4 = (bf16[256,256]{1,0:T(8,128)(2,1)S(1)}, bf16[256,256]{1,0:T(8,128)(2,1)}, u32[]{:S(2)}) copy-start(bf16[256,256]{1,0:T(8,128)(2,1)} %constant.22.clone.turn) | copy-start | bytes 393220
  90.4 29.6 %all-to-all-start.2 = ((bf16[64,48,128]{2,1,0:T(8,128)(2,1)}), bf16[64,48,128]{2,1,0:T(8,128)(2,1)S(1)}, u32[]{:S(2)}, u32[]{:S(2)}) async-start(bf16[64,48,128]{2,1,0:T(8,128)(2,1)} %bitcast.8), calls=%async_computation.2 | async-start | bytes 1572864 | tf_op jit(solution)/shard_map/all_to_all | solution.py:632
  95.0 90.8 %all-gather.7.cloned.1.call-start = ((), (), s32[]{:S(2)}) async-start(), calls=%async_computation.7 | async-start | bytes 3538944 | tf_op jit(solution)/shard_map/all_gather | solution.py:666
  120.0 29.0 %copy-start.1 = (bf16[2,2,384,384]{3,2,1,0:T(8,128)(2,1)S(1)}, bf16[2,2,384,384]{3,2,1,0:T(8,128)(2,1)}, u32[]{:S(2)}) copy-start(bf16[2,2,384,384]{3,2,1,0:T(8,128)(2,1)} %weights.1) | copy-start | bytes 3538948
  128.6 42.4 %copy-start.5 = (f32[192,1]{1,0:T(8,128)S(1)}, f32[192,1]{1,0:T(8,128)}, u32[]{:S(2)}) copy-start(f32[192,1]{1,0:T(8,128)} %constant.23.clone.weight_rows) | copy-start | bytes 2308
  150.4 30.9 %copy-start.6 = (bf16[256,256,1,1]{1,0,3,2:T(8,128)(2,1)S(1)}, bf16[256,256,1,1]{1,0,3,2:T(8,128)(2,1)}, u32[]{:S(2)}) copy-start(bf16[256,256,1,1]{1,0,3,2:T(8,128)(2,1)} %constant.27) | copy-start | bytes 393220
  176.3 26.8 %all-to-all-start.5 = ((bf16[64,40,128]{2,1,0:T(8,128)(2,1)}), bf16[64,40,128]{2,1,0:T(8,128)(2,1)S(1)}, u32[]{:S(2)}, u32[]{:S(2)}) async-start(bf16[64,40,128]{2,1,0:T(8,128)(2,1)} %bitcast.14), calls=%async_computation.5 | async-start | bytes 1310720 | tf_op jit(solution)/shard_map/all_to_all | solution.py:632
  185.8 17.3 %copy-start = (bf16[1,3,384,384]{3,2,1,0:T(8,128)(2,1)S(1)}, bf16[1,3,384,384]{3,2,1,0:T(8,128)(2,1)}, u32[]{:S(2)}) copy-start(bf16[1,3,384,384]{3,2,1,0:T(8,128)(2,1)} %param.13) | copy-start | bytes 2654212
  185.8 17.3 %copy-start.3 = (bf16[384,256]{1,0:T(8,128)(2,1)S(1)}, bf16[384,256]{1,0:T(8,128)(2,1)}, u32[]{:S(2)}) copy-start(bf16[384,256]{1,0:T(8,128)(2,1)} %constant.19.clone.forward_source.forward) | copy-start | bytes 589828
  193.1 11.5 %copy-start.2 = (bf16[2,2,384,384]{3,2,1,0:T(8,128)(2,1)}, bf16[2,2,384,384]{3,2,1,0:T(8,128)(2,1)S(1)}, u32[]{:S(2)}) copy-start(bf16[2,2,384,384]{3,2,1,0:T(8,128)(2,1)S(1)} %bitcast_convert_fusion.weight_grads) | copy-start | bytes 3538948
Sparse Core Ops, SparseCore 0:
  90.5 23.7 all-gather.4
  150.5 23.4 all-gather.6

commit v5 on v4

--- a/solution.py
+++ b/solution.py
@@ -25,12 +25,12 @@
 COT_CUTS = (0, 12, 36, 54)
 SLOT_ROWS = SLOTS * PARTS * 2
 LAST_ROWS = 40
+PIECES = 4
 HALF = GROUPS // 2
 LOW = LATS // 2
 REACH = [DEGREES // 2 - 8 * t for t in range(BLOCKS)]
 STARTS = [16 * sum(REACH[:t]) for t in range(BLOCKS + 1)]
 STEPS = [8 * LOW * t for t in range(BLOCKS + 1)]
-PLACES = [*range(HALF), *range(GROUPS - 1, HALF - 1, -1)]
 
 f32 = jnp.float32
 bf16 = jnp.bfloat16
@@ -75,7 +75,6 @@
 @functools.cache
 def constants():
     table, quadrature = legendre_table()
-    where = (np.array(PLACES)[None, :] * BAND + np.arange(BAND)[:, None]).reshape(-1)
     low = (np.arange(HALF)[None, :] * BAND + np.arange(BAND)[:, None]).reshape(-1)
 
     def for_analysis(values):
@@ -115,7 +114,8 @@
         inverse=inverse,
         inverse_t=np.ascontiguousarray(inverse.T),
         turn=turn.astype(bf16),
-        weight_rows=quadrature[where].astype(np.float32)[:, None],
+        flip=np.eye(LOW)[::-1].astype(bf16),
+        weight_rows=quadrature[low].astype(np.float32)[:, None],
     )
 
 
@@ -193,23 +193,28 @@
     return jnp.where((lanes // 2) % 2 == 0, 1.0, -1.0).astype(f32)
 
 
-def fold(x):
+def fold(pair, flip):
+    x = jnp.concatenate(pair, axis=1)
     low = jnp.concatenate([x[i * GROUPS : i * GROUPS + HALF] for i in range(BAND)], axis=0)
-    high = jnp.concatenate(
-        [x[i * GROUPS + HALF : (i + 1) * GROUPS] for i in reversed(range(BAND))], axis=0
-    )
-    high = high * order_sign(lane_of(high.shape))
-    return low + high, low - high
-
-
-def unfold(even, odd):
+    high = jnp.concatenate([x[i * GROUPS + HALF : (i + 1) * GROUPS] for i in range(BAND)], axis=0)
+    high = dot(flip, high.astype(bf16)) * order_sign(lane_of(high.shape))
+    both = (low.astype(bf16).astype(f32) + high, low.astype(bf16).astype(f32) - high)
+    return [[x[:, :128], x[:, 128:]] for x in both]
+
+
+def unfold(even, odd, flip, weight):
+    even, odd = jnp.concatenate(even, axis=1), jnp.concatenate(odd, axis=1)
     low = even + odd
     high = (even - odd) * order_sign(lane_of(low.shape))
+    if weight is not None:
+        low, high = low * weight, high * weight
+    high = dot(flip, high.astype(bf16))
     pieces = []
     for i in range(BAND):
-        pieces.append(low[i * HALF : (i + 1) * HALF])
-        pieces.append(high[(BAND - 1 - i) * HALF : (BAND - i) * HALF])
-    return jnp.concatenate(pieces, axis=0)
+        rows = slice(i * HALF, (i + 1) * HALF)
+        pieces += [low[rows], high[rows]]
+    whole = jnp.concatenate(pieces, axis=0)
+    return tuple(whole[:, 128 * n : 128 * (n + 1)] for n in range(3))
 
 
 def stacked(operand, groups, width):
@@ -220,9 +225,9 @@
     )
 
 
-def analyse(parts, table, ready):
-    folded = [[fold(x) for x in pair] for pair in parts]
-    tiles = [as_bf16(to_tiles([[x[odd] for x in pair] for pair in folded])) for odd in (0, 1)]
+def analyse(parts, flip, table, ready):
+    folded = [fold(pair, flip) for pair in parts]
+    tiles = [as_bf16(to_tiles([x[odd] for x in folded])) for odd in (0, 1)]
     sums = []
     for t in range(BLOCKS):
         ready(t)
@@ -243,7 +248,7 @@
     return merge_blocks(sums)
 
 
-def synthesise(tiles, table, ready):
+def synthesise(tiles, flip, weight, table, ready):
     sums = ([], [])
     order = (lane_of((LOW, 256)) % 8) // 2
     for t in range(BLOCKS):
@@ -257,7 +262,7 @@
                 total = jnp.where(order == k, part[k * LOW : (k + 1) * LOW], total)
             sums[odd].append(total)
     even, odd = merge_blocks(sums[0]), merge_blocks(sums[1])
-    return from_tiles([tuple(unfold(x, y) for x, y in zip(e, o)) for e, o in zip(even, odd)])
+    return from_tiles([unfold(e, o, flip, weight) for e, o in zip(even, odd)])
 
 
 def permute_rows(matrix, tiles):
@@ -378,7 +383,7 @@
 
 
 def first_kernel(
-    received, analysis, degree_col, carried, early, out, stage_in, stage, table, sems
+    received, analysis, degree_col, flip, carried, early, out, stage_in, stage, table, sems
 ):
     copies = table_copies(analysis, table, sems, STARTS)
     for copy in copies:
@@ -397,7 +402,7 @@
         ]
         for q in range(PARTS)
     ]
-    sums = analyse(parts, table, lambda t: copies[t].wait())
+    sums = analyse(parts, flip[...], table, lambda t: copies[t].wait())
     slot_rows_out(sums, degree_col, carried, stage, out)
 
 
@@ -409,7 +414,7 @@
 
 
 def middle_kernel(
-    received, one, two, analysis, synthesis, degree_row, degree_col, inverse_source, turned_source, out,
+    received, one, two, analysis, synthesis, degree_row, degree_col, flip, inverse_source, turned_source, early, also, out,
     inverse, inverse_t, rows_one, rows_two, stage_one, stage_two, stage, table, table_s, row_sems, sems, sems_s,
 ):
     copies_s = table_copies(synthesis, table_s, sems_s, STEPS)
@@ -423,7 +428,7 @@
     for copy in (*copies_s, *fetches, *copies):
         copy.start()
     tiles = slot_rows_in(received, degree_row, stage)
-    synth = synthesise(tiles, table_s, lambda t: copies_s[t].wait())
+    synth = synthesise(tiles, flip[...], None, table_s, lambda t: copies_s[t].wait())
     for fetch in fetches:
         fetch.wait()
     stage_one[...] = rows_one[...].astype(f32).reshape(GROUPS * 16, 128)
@@ -448,19 +453,21 @@
         upstream = (cotangent * gelu_slope(response)).astype(bf16)
         grad = dot(upstream, inverse[...])
         parts.append([grad[:, :128], grad[:, 128:]])
-    sums = analyse(parts, table, lambda t: copies[t].wait())
+    sums = analyse(parts, flip[...], table, lambda t: copies[t].wait())
     slot_rows_out(sums, degree_col, None, stage, out)
 
 
-def last_kernel(received, synthesis, degree_row, weight_rows, out, stage, stage_out, table_s, sems_s):
+def last_kernel(received, synthesis, degree_row, weight_rows, flip, early, also, out, stage, stage_out, table_s, sems_s):
     copies_s = table_copies(synthesis, table_s, sems_s, STEPS)
     for copy in copies_s:
         copy.start()
     tiles = slot_rows_in(received, degree_row, stage)
-    synth = synthesise(tiles, table_s, lambda t: copies_s[t].wait())
+    synth = synthesise(
+        tiles, flip[...], weight_rows[...], table_s, lambda t: copies_s[t].wait()
+    )
     for q in range(PARTS):
         for h in range(2):
-            scaled = synth[q][h] * weight_rows[...]
+            scaled = synth[q][h]
             for i in range(BAND):
                 at = (i * PARTS + q) * 2 + h
                 stage_out[pl.ds(at, GROUPS, stride=LAST_ROWS), :] = scaled[
@@ -490,7 +497,7 @@
 
 
 def mix_kernel(adjoint, received, weights, turn, *rest):
-    carried, out, kept, stage = (None, *rest) if adjoint else rest
+    carried, out, kept, stage = (None, *rest[2:]) if adjoint else rest
     parts = get_slots(received, stage)
     results = []
     for j in range(SLOTS):
@@ -570,21 +577,23 @@
     )(in_hbm(fields), in_hbm(cotangent), in_hbm(forward))
 
 
-def first(received, weighted, degree_col, carried, early):
+def first(received, weighted, degree_col, flip, carried, early):
     return call(
         first_kernel,
         message(SENT_ROWS),
-        [VMEM, ANY, VMEM, VMEM, ANY],
+        [VMEM, ANY, VMEM, VMEM, VMEM, ANY],
         [stage_of(SENT_ROWS), stage_of(SENT_ROWS), TABLE, sems(BLOCKS)],
         10**9, 6 * 10**6, "first",
-    )(received, in_hbm(weighted), degree_col, carried, early)
-
-
-def middle(received, one, two, analysis, synthesis, degree_row, degree_col, inverse, inverse_t):
+    )(received, in_hbm(weighted), degree_col, flip, carried, early)
+
+
+def middle(
+    received, one, two, analysis, synthesis, degree_row, degree_col, flip, inverse, inverse_t, early, also
+):
     return call(
         middle_kernel,
         message(SLOT_ROWS),
-        [VMEM, ANY, ANY, ANY, ANY, VMEM, VMEM, ANY, ANY],
+        [VMEM, ANY, ANY, ANY, ANY, VMEM, VMEM, VMEM, ANY, ANY, ANY, ANY],
         [
             pltpu.VMEM((LONS, COEFS), bf16), pltpu.VMEM((COEFS, LONS), bf16),
             pltpu.VMEM((GROUPS, 16, 128), bf16), pltpu.VMEM((GROUPS, 32, 128), bf16),
@@ -592,18 +601,18 @@
             TABLE, TABLE_S, sems(4), sems(BLOCKS), sems(BLOCKS),
         ],
         3 * 10**9, 12 * 10**6, "middle",
-    )(received, one, two, in_hbm(analysis), in_hbm(synthesis), degree_row, degree_col,
-      in_hbm(inverse), in_hbm(inverse_t))
-
-
-def last(received, synthesis, degree_row, weight_rows):
+    )(received, in_hbm(one), in_hbm(two), in_hbm(analysis), in_hbm(synthesis), degree_row, degree_col, flip,
+      in_hbm(inverse), in_hbm(inverse_t), in_hbm(early), in_hbm(also))
+
+
+def last(received, synthesis, degree_row, weight_rows, flip, early, also):
     return call(
         last_kernel,
         message(LAST_ROWS),
-        [VMEM, ANY, VMEM, VMEM],
+        [VMEM, ANY, VMEM, VMEM, VMEM, ANY, ANY],
         [stage_of(SLOT_ROWS), stage_of(LAST_ROWS), TABLE_S, sems(BLOCKS)],
         10**9, 7 * 10**6, "last",
-    )(received, in_hbm(synthesis), degree_row, weight_rows)
+    )(received, in_hbm(synthesis), degree_row, weight_rows, flip, in_hbm(early), in_hbm(also))
 
 
 def gather(received, forward, cotangent, weight_grads):
@@ -621,7 +630,7 @@
     return call(
         functools.partial(mix_kernel, adjoint),
         [message(rows), jax.ShapeDtypeStruct((SLOTS, CHANNELS, COEFS), bf16)],
-        [VMEM, VMEM, VMEM] + [VMEM] * len(carried),
+        [VMEM, VMEM, VMEM] + [ANY if adjoint else VMEM] * len(carried),
         [stage_of(rows)],
         6 * 10**8, 3 * 10**6, "adjoint_mix" if adjoint else "mix",
     )(received, weights, turn, *carried)
@@ -631,42 +640,71 @@
     count = rows.shape[0] // GROUPS
     out = lax.all_to_all(
         rows.reshape(GROUPS, count, 128), "lat", split_axis=0, concat_axis=0, tiled=True,
-        axis_index_groups=[PLACES],
     )
     return out.reshape(GROUPS * count, 128)
 
 
+def gradient_kernel(*refs):
+    coeffs, grads, turn, out = refs[:PIECES], refs[PIECES:-2], refs[-2], refs[-1]
+
+    def rows_of(pieces, j):
+        return jnp.concatenate(
+            [jnp.concatenate([p[s, j] for s in range(p.shape[0])], axis=1) for p in pieces], axis=0
+        )
+
+    for j in range(SLOTS):
+        right = rows_of(grads, j)
+        left = rows_of(coeffs, j)
+        turned = [
+            dot(left[:, COEFS * s : COEFS * (s + 1)], turn[...]).astype(bf16)
+            for s in range(coeffs[0].shape[0])
+        ]
+        out[j, 0] = dot(left, right, NT).astype(bf16)
+        out[j, 1] = dot(jnp.concatenate(turned, axis=1), right, NT).astype(bf16)
+
+
+def gather_pieces(x):
+    return [lax.all_gather(p, "batch", axis=0) for p in jnp.split(x, PIECES, axis=1)]
+
+
 def weight_gradient(coeffs, grads, turn):
-    turned = jnp.einsum("sjcf,fe->sjce", coeffs, turn, preferred_element_type=f32).astype(bf16)
-    both = jnp.stack([coeffs, turned], axis=2)
-    total = jnp.einsum("sjpcf,sjdf->jpcd", both, grads, preferred_element_type=f32)
-    return total.astype(bf16)
+    return call(
+        gradient_kernel,
+        jax.ShapeDtypeStruct((SLOTS, 2, CHANNELS, CHANNELS), bf16),
+        [VMEM] * (2 * PIECES + 1),
+        [],
+        5 * 10**9, 8 * 10**6, "weight_gradient",
+    )(*coeffs, *grads, turn)
 
 
 def local(fields, cotangent, weights, degree_of):
     table = {k: jnp.asarray(v) for k, v in constants().items()}
-    slots = degree_of.reshape(GROUPS, SLOTS)
-    slots = jnp.concatenate([slots[:HALF], slots[HALF:][::-1]], axis=0).T.reshape(DEGREES)
+    slots = degree_of.reshape(GROUPS, SLOTS).T.reshape(DEGREES)
     degree_col, degree_row = slots[:, None], slots[None, :]
     turned_weights = jnp.swapaxes(weights, 2, 3)
     sent, cot_two, cot_three = spread(fields[0], cotangent[0], table["forward"])
     one = exchange(sent)
-    two = exchange(first(one, table["weighted"], degree_col, cot_two, turned_weights))
+    two = exchange(first(one, table["weighted"], degree_col, table["flip"], cot_two, turned_weights))
     filtered, coeffs = mix(False, two, turned_weights, table["turn"], cot_three)
-    all_coeffs = lax.all_gather(coeffs, "batch", axis=0)
+    all_coeffs = gather_pieces(coeffs)
     three = exchange(filtered)
     as_sent = (GROUPS, SENT_ROWS, 128)
     four = exchange(
         middle(
             three, one.reshape(as_sent), two.reshape(as_sent), table["analysis"],
-            table["synthesis"], degree_row, degree_col, table["inverse"], table["inverse_t"],
+            table["synthesis"], degree_row, degree_col, table["flip"],
+            table["inverse"], table["inverse_t"], *all_coeffs[:2],
         )
     )
-    grad_coeffs, grads = mix(True, four, weights, table["turn"])
-    all_grads = lax.all_gather(grads, "batch", axis=0)
+    grad_coeffs, grads = mix(True, four, weights, table["turn"], *map(in_hbm, all_coeffs[2:]))
+    all_grads = gather_pieces(grads)
     grad_weights = weight_gradient(all_coeffs, all_grads, table["turn"])
     five = exchange(grad_coeffs)
-    six = exchange(last(five, table["synthesis"], degree_row, table["weight_rows"]))
+    six = exchange(
+        last(
+            five, table["synthesis"], degree_row, table["weight_rows"], table["flip"], *all_grads[:2]
+        )
+    )
     grad_fields = gather(six, table["forward"], cotangent[0], grad_weights)[None]
     return grad_fields, grad_weights
 

time: 212 us -> 277 us (1.31)
  blocking collectives: 70.9 us -> 144 us
  waiting for transfers between devices: 59 us -> 23 us
  starting transfers between devices: 26.4 us -> 61.2 us
  between operations: 14.2 us -> 0.87 us
  matrix products: 11.8 us -> 0 us
  local copies, waits for them, and re-layouts: 2.41 us -> 12.3 us
  Pallas kernels: 26.7 us -> 33.7 us
    all_gather x0 -> x8, blocking collectives: none -> 114 us  [gather_pieces(): lax.all_gather(p, 'batch', axis=0)]
    all_to_all x3 -> x1, blocking collectives: 70.9 us -> 29.7 us  [exchange(): lax.all_to_all(rows.reshape(GROUPS, count, 128), 'lat', split_axis=0, con...]
    all_to_all x3 -> x5, waiting for transfers between devices: 58.9 us -> 23 us  [exchange(): lax.all_to_all(rows.reshape(GROUPS, count, 128), 'lat', split_axis=0, con...]
    all_to_all x3 -> x5, starting transfers between devices: 26.1 us -> 61.2 us  [exchange(): lax.all_to_all(rows.reshape(GROUPS, count, 128), 'lat', split_axis=0, con...]
    dot_general x2 -> x0, matrix products: 11.8 us -> none  [the longest x1 7.24 us: weight_gradient(): jnp.einsum('sjpcf,sjdf->jpcd', both, grads, preferred_element_type=f32)]
    unnamed x17 -> x47, local copies, waits for them, and re-layouts: 1.74 us -> 10.8 us
    pallas_call x2 -> x3, Pallas kernels: 9.34 us -> 14.6 us  [the longest x1 5.24 us: weight_gradient(): call(gradient_kernel, jax.ShapeDtypeStruct((SLOTS, 2, CHANNELS, CHANNELS)...]
  transfers between devices with their start and end apart: 5 -> 5, of which waited for: 3 -> 1; matrix products, arithmetic and copies ran while one was open for 7% -> 1% of each run, Pallas kernels for 7% -> 2%
where the time goes in v5:
time: 277 us; the launch traced here: 275 us
  blocking collectives  144 us (52%)
  starting transfers between devices  61.2 us (22%)
  Pallas kernels  33.7 us (12%)
  waiting for transfers between devices  23 us (8%)
  local copies, waits for them, and re-layouts  12.3 us (4%)
    all_gather x8, blocking collectives, gather_pieces(): lax.all_gather(p, 'batch', axis=0)  114 us
    all_to_all x5, starting transfers between devices, exchange(): lax.all_to_all(rows.reshape(GROUPS, count, 128), 'lat', split_axis=0, con...  61.2 us
    all_to_all x1, blocking collectives, exchange(): lax.all_to_all(rows.reshape(GROUPS, count, 128), 'lat', split_axis=0, con...  29.7 us
    all_to_all x5, waiting for transfers between devices, exchange(): lax.all_to_all(rows.reshape(GROUPS, count, 128), 'lat', split_axis=0, con...  23 us
    unnamed x47, local copies, waits for them, and re-layouts  10.8 us
    pallas_call x1, Pallas kernels, middle(): call(middle_kernel, message(SLOT_ROWS), [VMEM, ANY, ANY, ANY, ANY, VMEM,...  9.85 us
  transfers between devices with their start and end apart: 5, of which 1 were waited for; matrix products, arithmetic and copies ran while one was open for 1% of the time, Pallas kernels for 2%

profile of v5, /device:TPU:6, one launch (start us, length us, event | category | flops | bytes accessed | tf_op | source)
XLA Modules:
  0.0 274.7 jit_solution(264892066710331040)
XLA Ops:
  0.6 4.0 %spread.1 = (bf16[3072,128]{1,0:T(8,128)(2,1)}, bf16[1536,128]{1,0:T(8,128)(2,1)S(1)}, bf16[1536,128]{1,0:T(8,128)(2,1)S(1)}) custom-call(bf16[3,384,384]{2,1,0:T(8,128)(2,1)} %bitcast.50, bf16[3,384,384]{2,1,0:T(8,128)(2,1)} %bitcast.27, bf16[384,256]{1,0:T(8,128)(2,1)} %constant.21.clone.forward_source.forward), custom_call_target="tpu_custom_call" | custom-call | flops 300000000 | bytes 4000000 | tf_op jit(solution)/shard_map/spread/pallas_call | solution.py:568
  6.2 16.7 %all-to-all-start = ((bf16[64,48,128]{2,1,0:T(8,128)(2,1)}), bf16[64,48,128]{2,1,0:T(8,128)(2,1)S(1)}, u32[]{:S(2)}, u32[]{:S(2)}) async-start(bf16[64,48,128]{2,1,0:T(8,128)(2,1)} %bitcast.2), calls=%async_computation | async-start | bytes 1572864 | tf_op jit(solution)/shard_map/all_to_all | solution.py:641
  23.3 0.8 copy.26
  24.1 23.0 %all-to-all-done.one = bf16[64,48,128]{2,1,0:T(8,128)(2,1)S(1)} async-done(((bf16[64,48,128]{2,1,0:T(8,128)(2,1)}), bf16[64,48,128]{2,1,0:T(8,128)(2,1)S(1)}, u32[]{:S(2)}, u32[]{:S(2)}) %all-to-all-start) | async-done | bytes 786464 | tf_op jit(solution)/shard_map/all_to_all | solution.py:641
  47.1 1.3 copy-done.19
  48.4 4.4 %first.1 = bf16[3072,128]{1,0:T(8,128)(2,1)S(1)} custom-call(bf16[3072,128]{1,0:T(8,128)(2,1)S(1)} %bitcast.38, bf16[4608,192]{1,0:T(8,128)(2,1)} %constant.19.clone.analysis, s32[128,1]{1,0:T(8,128)S(1)} %broadcast_in_dim_reshape.8.degree_col, bf16[96,96]{1,0:T(8,128)(2,1)S(1)} %copy-done.20, bf16[1536,128]{1,0:T(8,128)(2,1)S(1)} %copy-done.19, ...), custom_call_target="tpu_custom_call" | custom-call | flops 1000000000 | bytes 6000000 | tf_op jit(solution)/shard_map/first/pallas_call | solution.py:581
  52.7 29.7 %all_to_all.30.two = bf16[64,48,128]{2,1,0:T(8,128)(2,1)S(1)} all-to-all(bf16[64,48,128]{2,1,0:T(8,128)(2,1)S(1)} %bitcast.39), channel_id=1, replica_groups=mesh['lat'=64,'batch'=8] {'lat'}, dimensions={0} | all-to-all | bytes 1572864 | tf_op jit(solution)/shard_map/all_to_all | solution.py:641
  82.4 1.1 mix.1
  83.6 0.9 copy-done.11
  85.2 5.9 %all-to-all-start.2 = ((bf16[64,48,128]{2,1,0:T(8,128)(2,1)}), bf16[64,48,128]{2,1,0:T(8,128)(2,1)S(1)}, u32[]{:S(2)}, u32[]{:S(2)}) async-start(bf16[64,48,128]{2,1,0:T(8,128)(2,1)} %bitcast.47), calls=%async_computation.2 | async-start | bytes 1572864 | tf_op jit(solution)/shard_map/all_to_all | solution.py:641
  91.2 1.1 fusion.1
  92.2 14.5 %all-gather.1 = bf16[16,96,256]{2,1,0:T(8,128)(2,1)} all-gather(bf16[2,96,256]{2,1,0:T(8,128)(2,1)S(1)} %get-tuple-element.22), channel_id=3, replica_groups=mesh['lat'=64,'batch'=8] {'batch'}, dimensions={0}, use_global_device_ids=true | all-gather | bytes 884736 | tf_op jit(solution)/shard_map/all_gather | solution.py:667
  106.7 14.6 %all-gather = bf16[16,96,256]{2,1,0:T(8,128)(2,1)} all-gather(bf16[2,96,256]{2,1,0:T(8,128)(2,1)S(1)} %get-tuple-element.23), channel_id=2, replica_groups=mesh['lat'=64,'batch'=8] {'batch'}, dimensions={0}, use_global_device_ids=true | all-gather | bytes 884736 | tf_op jit(solution)/shard_map/all_gather | solution.py:667
  121.3 9.8 %middle.1 = bf16[1536,128]{1,0:T(8,128)(2,1)} custom-call(bf16[3072,128]{1,0:T(8,128)(2,1)S(1)} %bitcast.46, bf16[64,48,128]{2,1,0:T(8,128)(2,1)} %copy-done.7, bf16[64,48,128]{2,1,0:T(8,128)(2,1)} %copy-done.2, bf16[4608,192]{1,0:T(8,128)(2,1)} %constant.18.clone.analysis, bf16[6144,256]{1,0:T(8,128)(2,1)} %constant.20.clone.synthesis, ...), custom_call_target="tpu_custom_call" | custom-call | flops 3000000000 | bytes 12000000 | tf_op jit(solution)/shard_map/middle/pallas_call | solution.py:593
  131.2 12.7 %all-to-all-start.3 = ((bf16[64,24,128]{2,1,0:T(8,128)(2,1)}), bf16[64,24,128]{2,1,0:T(8,128)(2,1)S(1)}, u32[]{:S(2)}, u32[]{:S(2)}) async-start(bf16[64,24,128]{2,1,0:T(8,128)(2,1)} %bitcast.12), calls=%async_computation.3 | async-start | bytes 786432 | tf_op jit(solution)/shard_map/all_to_all | solution.py:641
  143.9 14.5 %all-gather.3 = bf16[16,96,256]{2,1,0:T(8,128)(2,1)} all-gather(bf16[2,96,256]{2,1,0:T(8,128)(2,1)S(1)} %get-tuple-element.20), channel_id=5, replica_groups=mesh['lat'=64,'batch'=8] {'batch'}, dimensions={0}, use_global_device_ids=true | all-gather | bytes 884736 | tf_op jit(solution)/shard_map/all_gather | solution.py:667
  158.4 14.4 %all-gather.2 = bf16[16,96,256]{2,1,0:T(8,128)(2,1)} all-gather(bf16[2,96,256]{2,1,0:T(8,128)(2,1)S(1)} %get-tuple-element.21), channel_id=4, replica_groups=mesh['lat'=64,'batch'=8] {'batch'}, dimensions={0}, use_global_device_ids=true | all-gather | bytes 884736 | tf_op jit(solution)/shard_map/all_gather | solution.py:667
  172.8 1.6 adjoint_mix.1
  174.4 12.8 %all-to-all-start.4 = ((bf16[64,24,128]{2,1,0:T(8,128)(2,1)}), bf16[64,24,128]{2,1,0:T(8,128)(2,1)S(1)}, u32[]{:S(2)}, u32[]{:S(2)}) async-start(bf16[64,24,128]{2,1,0:T(8,128)(2,1)} %bitcast.16), calls=%async_computation.4 | async-start | bytes 786432 | tf_op jit(solution)/shard_map/all_to_all | solution.py:641
  187.3 14.5 %all-gather.5 = bf16[16,96,256]{2,1,0:T(8,128)(2,1)} all-gather(bf16[2,96,256]{2,1,0:T(8,128)(2,1)S(1)} %get-tuple-element.18), channel_id=7, replica_groups=mesh['lat'=64,'batch'=8] {'batch'}, dimensions={0}, use_global_device_ids=true | all-gather | bytes 884736 | tf_op jit(solution)/shard_map/all_gather | solution.py:667
  201.8 14.7 %all-gather.4 = bf16[16,96,256]{2,1,0:T(8,128)(2,1)} all-gather(bf16[2,96,256]{2,1,0:T(8,128)(2,1)S(1)} %get-tuple-element.19), channel_id=6, replica_groups=mesh['lat'=64,'batch'=8] {'batch'}, dimensions={0}, use_global_device_ids=true | all-gather | bytes 884736 | tf_op jit(solution)/shard_map/all_gather | solution.py:667
  216.5 5.0 %last.1 = bf16[2560,128]{1,0:T(8,128)(2,1)} custom-call(bf16[1536,128]{1,0:T(8,128)(2,1)S(1)} %bitcast.40, bf16[6144,256]{1,0:T(8,128)(2,1)} %constant.20.clone.synthesis, s32[1,128]{1,0:T(1,128)S(1)} %broadcast_in_dim_reshape.7.degree_row, f32[96,1]{1,0:T(8,128)S(1)} %copy-done.21, bf16[96,96]{1,0:T(8,128)(2,1)S(1)} %copy-done.20, ...), custom_call_target="tpu_custom_call" | custom-call | flops 1000000000 | bytes 7000000 | tf_op jit(solution)/shard_map/last/pallas_call | solution.py:609
  221.4 13.1 %all-to-all-start.5 = ((bf16[64,40,128]{2,1,0:T(8,128)(2,1)}), bf16[64,40,128]{2,1,0:T(8,128)(2,1)}, u32[]{:S(2)}, u32[]{:S(2)}) async-start(bf16[64,40,128]{2,1,0:T(8,128)(2,1)} %bitcast.20), calls=%async_computation.5 | async-start | bytes 1310720 | tf_op jit(solution)/shard_map/all_to_all | solution.py:641
  234.5 13.4 %all-gather.7 = bf16[16,96,256]{2,1,0:T(8,128)(2,1)S(1)} all-gather(bf16[2,96,256]{2,1,0:T(8,128)(2,1)S(1)} %get-tuple-element.16), channel_id=9, replica_groups=mesh['lat'=64,'batch'=8] {'batch'}, dimensions={0}, use_global_device_ids=true | all-gather | bytes 884736 | tf_op jit(solution)/shard_map/all_gather | solution.py:667
  247.9 13.4 %all-gather.6 = bf16[16,96,256]{2,1,0:T(8,128)(2,1)S(1)} all-gather(bf16[2,96,256]{2,1,0:T(8,128)(2,1)S(1)} %get-tuple-element.17), channel_id=8, replica_groups=mesh['lat'=64,'batch'=8] {'batch'}, dimensions={0}, use_global_device_ids=true | all-gather | bytes 884736 | tf_op jit(solution)/shard_map/all_gather | solution.py:667
  261.3 1.1 copy-done.6
  262.4 1.1 copy-done.9
  263.6 1.1 copy-done.10
  264.7 0.9 copy-done.14
  265.6 5.2 %weight_gradient.1.weight_grads = bf16[2,2,384,384]{3,2,1,0:T(8,128)(2,1)} custom-call(bf16[8,2,96,256]{3,2,1,0:T(8,128)(2,1)S(1)} %bitcast.45, bf16[8,2,96,256]{3,2,1,0:T(8,128)(2,1)S(1)} %bitcast.43, bf16[8,2,96,256]{3,2,1,0:T(8,128)(2,1)S(1)} %bitcast.37, bf16[8,2,96,256]{3,2,1,0:T(8,128)(2,1)S(1)} %bitcast.35, bf16[8,2,96,256]{3,2,1,0:T(8,128)(2,1)S(1)} %bitcast.33, ...), custom_call_target="tpu_custom_call" | custom-call | flops 5000000000 | bytes 8000000 | tf_op jit(solution)/shard_map/weight_gradient/pallas_call | solution.py:671
  270.9 1.3 copy-done.8
  272.1 2.5 gather.1
  (48 shorter events, 2.8 us)
Async XLA Ops:
  0.6 22.3 %copy-start.22 = (s32[128]{0:T(128)S(1)}, s32[128]{0:T(128)}, u32[]{:S(2)}) copy-start(s32[128]{0:T(128)} %param.16) | copy-start | bytes 1540
  0.6 22.6 %copy-start = (bf16[2,2,384,384]{3,2,1,0:T(8,128)(2,1)S(1)}, bf16[2,2,384,384]{3,2,1,0:T(8,128)(2,1)}, u32[]{:S(2)}) copy-start(bf16[2,2,384,384]{3,2,1,0:T(8,128)(2,1)} %weights.1) | copy-start | bytes 3538948
  4.7 0.7 copy-start.15
  5.4 0.7 copy-start.18
  6.2 40.9 %copy-start.20 = (bf16[96,96]{1,0:T(8,128)(2,1)S(1)}, bf16[96,96]{1,0:T(8,128)(2,1)}, u32[]{:S(2)}) copy-start(bf16[96,96]{1,0:T(8,128)(2,1)} %constant.25.clone.flip) | copy-start | bytes 55300
  6.2 40.9 %all-to-all-start = ((bf16[64,48,128]{2,1,0:T(8,128)(2,1)}), bf16[64,48,128]{2,1,0:T(8,128)(2,1)S(1)}, u32[]{:S(2)}, u32[]{:S(2)}) async-start(bf16[64,48,128]{2,1,0:T(8,128)(2,1)} %bitcast.2), calls=%async_computation | async-start | bytes 1572864 | tf_op jit(solution)/shard_map/all_to_all | solution.py:641
  47.1 5.6 %copy-start.7 = (bf16[64,48,128]{2,1,0:T(8,128)(2,1)}, bf16[64,48,128]{2,1,0:T(8,128)(2,1)S(1)}, u32[]{:S(2)}) copy-start(bf16[64,48,128]{2,1,0:T(8,128)(2,1)S(1)} %all-to-all-done.one) | copy-start | bytes 2359300
  47.1 1.3 copy-start.19
  48.4 34.1 %copy-start.13 = (bf16[256,256]{1,0:T(8,128)(2,1)S(1)}, bf16[256,256]{1,0:T(8,128)(2,1)}, u32[]{:S(2)}) copy-start(bf16[256,256]{1,0:T(8,128)(2,1)} %constant.24.clone.turn.refs_8_) | copy-start | bytes 393220
  48.4 34.1 %copy-start.16 = (bf16[1536,128]{1,0:T(8,128)(2,1)S(1)}, bf16[1536,128]{1,0:T(8,128)(2,1)}, u32[]{:S(2)}) copy-start(bf16[1536,128]{1,0:T(8,128)(2,1)} %copy-done.15) | copy-start | bytes 1179652
  82.4 9.8 %copy-start.2 = (bf16[64,48,128]{2,1,0:T(8,128)(2,1)}, bf16[64,48,128]{2,1,0:T(8,128)(2,1)S(1)}, u32[]{:S(2)}) copy-start(bf16[64,48,128]{2,1,0:T(8,128)(2,1)S(1)} %all_to_all.30.two) | copy-start | bytes 2359300
  83.5 0.9 copy-start.11
  84.4 0.7 copy-start.17
  85.2 36.2 %all-to-all-start.2 = ((bf16[64,48,128]{2,1,0:T(8,128)(2,1)}), bf16[64,48,128]{2,1,0:T(8,128)(2,1)S(1)}, u32[]{:S(2)}, u32[]{:S(2)}) async-start(bf16[64,48,128]{2,1,0:T(8,128)(2,1)} %bitcast.47), calls=%async_computation.2 | async-start | bytes 1572864 | tf_op jit(solution)/shard_map/all_to_all | solution.py:641
  131.2 41.6 %all-to-all-start.3 = ((bf16[64,24,128]{2,1,0:T(8,128)(2,1)}), bf16[64,24,128]{2,1,0:T(8,128)(2,1)S(1)}, u32[]{:S(2)}, u32[]{:S(2)}) async-start(bf16[64,24,128]{2,1,0:T(8,128)(2,1)} %bitcast.12), calls=%async_computation.3 | async-start | bytes 786432 | tf_op jit(solution)/shard_map/all_to_all | solution.py:641
  174.4 42.0 %copy-start.21 = (f32[96,1]{1,0:T(8,128)S(1)}, f32[96,1]{1,0:T(8,128)}, u32[]{:S(2)}) copy-start(f32[96,1]{1,0:T(8,128)} %constant.26.clone.weight_rows) | copy-start | bytes 1156
  174.4 42.0 %all-to-all-start.4 = ((bf16[64,24,128]{2,1,0:T(8,128)(2,1)}), bf16[64,24,128]{2,1,0:T(8,128)(2,1)S(1)}, u32[]{:S(2)}, u32[]{:S(2)}) async-start(bf16[64,24,128]{2,1,0:T(8,128)(2,1)} %bitcast.16), calls=%async_computation.4 | async-start | bytes 786432 | tf_op jit(solution)/shard_map/all_to_all | solution.py:641
  221.4 39.9 %copy-start.3 = (bf16[16,96,256]{2,1,0:T(8,128)(2,1)S(1)}, bf16[16,96,256]{2,1,0:T(8,128)(2,1)}, u32[]{:S(2)}) copy-start(bf16[16,96,256]{2,1,0:T(8,128)(2,1)} %all-gather.5) | copy-start | bytes 2359300
  221.4 39.9 %copy-start.4 = (bf16[16,96,256]{2,1,0:T(8,128)(2,1)S(1)}, bf16[16,96,256]{2,1,0:T(8,128)(2,1)}, u32[]{:S(2)}) copy-start(bf16[16,96,256]{2,1,0:T(8,128)(2,1)} %all-gather.4) | copy-start | bytes 2359300
  221.4 39.9 %copy-start.5 = (bf16[16,96,256]{2,1,0:T(8,128)(2,1)S(1)}, bf16[16,96,256]{2,1,0:T(8,128)(2,1)}, u32[]{:S(2)}) copy-start(bf16[16,96,256]{2,1,0:T(8,128)(2,1)} %all-gather.3) | copy-start | bytes 2359300
  221.4 49.4 %all-to-all-start.5 = ((bf16[64,40,128]{2,1,0:T(8,128)(2,1)}), bf16[64,40,128]{2,1,0:T(8,128)(2,1)}, u32[]{:S(2)}, u32[]{:S(2)}) async-start(bf16[64,40,128]{2,1,0:T(8,128)(2,1)} %bitcast.20), calls=%async_computation.5 | async-start | bytes 1310720 | tf_op jit(solution)/shard_map/all_to_all | solution.py:641
  261.3 1.1 copy-start.6
  262.4 1.1 copy-start.9
  263.6 1.1 copy-start.10
  264.7 0.9 copy-start.14
  265.6 5.2 %copy-start.1 = (bf16[1,3,384,384]{3,2,1,0:T(8,128)(2,1)S(1)}, bf16[1,3,384,384]{3,2,1,0:T(8,128)(2,1)}, u32[]{:S(2)}) copy-start(bf16[1,3,384,384]{3,2,1,0:T(8,128)(2,1)} %param.14) | copy-start | bytes 2654212
  265.6 5.2 %copy-start.12 = (bf16[384,256]{1,0:T(8,128)(2,1)S(1)}, bf16[384,256]{1,0:T(8,128)(2,1)}, u32[]{:S(2)}) copy-start(bf16[384,256]{1,0:T(8,128)(2,1)} %constant.21.clone.forward_source.forward) | copy-start | bytes 589828
  270.9 1.3 copy-start.8

commit v6 on v5

--- a/solution.py
+++ b/solution.py
@@ -25,7 +25,6 @@
 COT_CUTS = (0, 12, 36, 54)
 SLOT_ROWS = SLOTS * PARTS * 2
 LAST_ROWS = 40
-PIECES = 4
 HALF = GROUPS // 2
 LOW = LATS // 2
 REACH = [DEGREES // 2 - 8 * t for t in range(BLOCKS)]
@@ -414,7 +413,7 @@
 
 
 def middle_kernel(
-    received, one, two, analysis, synthesis, degree_row, degree_col, flip, inverse_source, turned_source, early, also, out,
+    received, one, two, analysis, synthesis, degree_row, degree_col, flip, inverse_source, turned_source, out,
     inverse, inverse_t, rows_one, rows_two, stage_one, stage_two, stage, table, table_s, row_sems, sems, sems_s,
 ):
     copies_s = table_copies(synthesis, table_s, sems_s, STEPS)
@@ -457,7 +456,7 @@
     slot_rows_out(sums, degree_col, None, stage, out)
 
 
-def last_kernel(received, synthesis, degree_row, weight_rows, flip, early, also, out, stage, stage_out, table_s, sems_s):
+def last_kernel(received, synthesis, degree_row, weight_rows, flip, out, stage, stage_out, table_s, sems_s):
     copies_s = table_copies(synthesis, table_s, sems_s, STEPS)
     for copy in copies_s:
         copy.start()
@@ -497,7 +496,7 @@
 
 
 def mix_kernel(adjoint, received, weights, turn, *rest):
-    carried, out, kept, stage = (None, *rest[2:]) if adjoint else rest
+    carried, out, kept, stage = (None, *rest) if adjoint else rest
     parts = get_slots(received, stage)
     results = []
     for j in range(SLOTS):
@@ -588,12 +587,12 @@
 
 
 def middle(
-    received, one, two, analysis, synthesis, degree_row, degree_col, flip, inverse, inverse_t, early, also
+    received, one, two, analysis, synthesis, degree_row, degree_col, flip, inverse, inverse_t
 ):
     return call(
         middle_kernel,
         message(SLOT_ROWS),
-        [VMEM, ANY, ANY, ANY, ANY, VMEM, VMEM, VMEM, ANY, ANY, ANY, ANY],
+        [VMEM, ANY, ANY, ANY, ANY, VMEM, VMEM, VMEM, ANY, ANY],
         [
             pltpu.VMEM((LONS, COEFS), bf16), pltpu.VMEM((COEFS, LONS), bf16),
             pltpu.VMEM((GROUPS, 16, 128), bf16), pltpu.VMEM((GROUPS, 32, 128), bf16),
@@ -601,18 +600,18 @@
             TABLE, TABLE_S, sems(4), sems(BLOCKS), sems(BLOCKS),
         ],
         3 * 10**9, 12 * 10**6, "middle",
-    )(received, in_hbm(one), in_hbm(two), in_hbm(analysis), in_hbm(synthesis), degree_row, degree_col, flip,
-      in_hbm(inverse), in_hbm(inverse_t), in_hbm(early), in_hbm(also))
-
-
-def last(received, synthesis, degree_row, weight_rows, flip, early, also):
+    )(received, one, two, in_hbm(analysis), in_hbm(synthesis), degree_row, degree_col, flip,
+      in_hbm(inverse), in_hbm(inverse_t))
+
+
+def last(received, synthesis, degree_row, weight_rows, flip):
     return call(
         last_kernel,
         message(LAST_ROWS),
-        [VMEM, ANY, VMEM, VMEM, VMEM, ANY, ANY],
+        [VMEM, ANY, VMEM, VMEM, VMEM],
         [stage_of(SLOT_ROWS), stage_of(LAST_ROWS), TABLE_S, sems(BLOCKS)],
         10**9, 7 * 10**6, "last",
-    )(received, in_hbm(synthesis), degree_row, weight_rows, flip, in_hbm(early), in_hbm(also))
+    )(received, in_hbm(synthesis), degree_row, weight_rows, flip)
 
 
 def gather(received, forward, cotangent, weight_grads):
@@ -622,7 +621,7 @@
         [VMEM, VMEM, VMEM, ANY],
         [stage_of(LAST_ROWS)],
         3 * 10**8, 3 * 10**6, "gather",
-    )(received, forward, cotangent, weight_grads)
+    )(received, forward, cotangent, in_hbm(weight_grads))
 
 
 def mix(adjoint, received, weights, turn, *carried):
@@ -630,7 +629,7 @@
     return call(
         functools.partial(mix_kernel, adjoint),
         [message(rows), jax.ShapeDtypeStruct((SLOTS, CHANNELS, COEFS), bf16)],
-        [VMEM, VMEM, VMEM] + [ANY if adjoint else VMEM] * len(carried),
+        [VMEM, VMEM, VMEM] + [VMEM] * len(carried),
         [stage_of(rows)],
         6 * 10**8, 3 * 10**6, "adjoint_mix" if adjoint else "mix",
     )(received, weights, turn, *carried)
@@ -644,37 +643,38 @@
     return out.reshape(GROUPS * count, 128)
 
 
-def gradient_kernel(*refs):
-    coeffs, grads, turn, out = refs[:PIECES], refs[PIECES:-2], refs[-2], refs[-1]
-
-    def rows_of(pieces, j):
-        return jnp.concatenate(
-            [jnp.concatenate([p[s, j] for s in range(p.shape[0])], axis=1) for p in pieces], axis=0
+def gradient_kernel(coeffs_source, grads_source, turn, out, coeffs, grads, sems):
+    copies = []
+    for j in range(SLOTS):
+        copies.append(
+            [
+                pltpu.make_async_copy(source.at[:, j], held.at[:, j], sems.at[2 * j + n])
+                for n, (source, held) in enumerate(((coeffs_source, coeffs), (grads_source, grads)))
+            ]
         )
-
+    for pair in copies:
+        for copy in pair:
+            copy.start()
+    samples = range(coeffs.shape[0])
     for j in range(SLOTS):
-        right = rows_of(grads, j)
-        left = rows_of(coeffs, j)
-        turned = [
-            dot(left[:, COEFS * s : COEFS * (s + 1)], turn[...]).astype(bf16)
-            for s in range(coeffs[0].shape[0])
-        ]
-        out[j, 0] = dot(left, right, NT).astype(bf16)
+        copies[j][0].wait()
+        left = [coeffs[s, j] for s in samples]
+        turned = [dot(x, turn[...]).astype(bf16) for x in left]
+        copies[j][1].wait()
+        right = jnp.concatenate([grads[s, j] for s in samples], axis=1)
+        out[j, 0] = dot(jnp.concatenate(left, axis=1), right, NT).astype(bf16)
         out[j, 1] = dot(jnp.concatenate(turned, axis=1), right, NT).astype(bf16)
 
 
-def gather_pieces(x):
-    return [lax.all_gather(p, "batch", axis=0) for p in jnp.split(x, PIECES, axis=1)]
-
-
 def weight_gradient(coeffs, grads, turn):
+    held = pltpu.VMEM(coeffs.shape, bf16)
     return call(
         gradient_kernel,
         jax.ShapeDtypeStruct((SLOTS, 2, CHANNELS, CHANNELS), bf16),
-        [VMEM] * (2 * PIECES + 1),
-        [],
+        [ANY, ANY, VMEM],
+        [held, held, sems(2 * SLOTS)],
         5 * 10**9, 8 * 10**6, "weight_gradient",
-    )(*coeffs, *grads, turn)
+    )(in_hbm(coeffs), in_hbm(grads), turn)
 
 
 def local(fields, cotangent, weights, degree_of):
@@ -686,25 +686,21 @@
     one = exchange(sent)
     two = exchange(first(one, table["weighted"], degree_col, table["flip"], cot_two, turned_weights))
     filtered, coeffs = mix(False, two, turned_weights, table["turn"], cot_three)
-    all_coeffs = gather_pieces(coeffs)
+    all_coeffs = lax.all_gather(coeffs, "batch", axis=0)
     three = exchange(filtered)
     as_sent = (GROUPS, SENT_ROWS, 128)
     four = exchange(
         middle(
             three, one.reshape(as_sent), two.reshape(as_sent), table["analysis"],
             table["synthesis"], degree_row, degree_col, table["flip"],
-            table["inverse"], table["inverse_t"], *all_coeffs[:2],
+            table["inverse"], table["inverse_t"],
         )
     )
-    grad_coeffs, grads = mix(True, four, weights, table["turn"], *map(in_hbm, all_coeffs[2:]))
-    all_grads = gather_pieces(grads)
+    grad_coeffs, grads = mix(True, four, weights, table["turn"])
+    all_grads = lax.all_gather(grads, "batch", axis=0)
     grad_weights = weight_gradient(all_coeffs, all_grads, table["turn"])
     five = exchange(grad_coeffs)
-    six = exchange(
-        last(
-            five, table["synthesis"], degree_row, table["weight_rows"], table["flip"], *all_grads[:2]
-        )
-    )
+    six = exchange(last(five, table["synthesis"], degree_row, table["weight_rows"], table["flip"]))
     grad_fields = gather(six, table["forward"], cotangent[0], grad_weights)[None]
     return grad_fields, grad_weights
 

time: 277 us -> 204 us (0.74)
  blocking collectives: 144 us -> 69.6 us
  starting transfers between devices: 61.2 us -> 27.6 us
  waiting for transfers between devices: 23 us -> 55.4 us
  between operations: 0.87 us -> 14.2 us
  local copies, waits for them, and re-layouts: 12.3 us -> 2.18 us
    all_gather x8 -> x0, blocking collectives: 114 us -> none  [gather_pieces(): lax.all_gather(p, 'batch', axis=0)]
    all_to_all x1 -> x3, blocking collectives: 29.7 us -> 69.6 us  [exchange(): lax.all_to_all(rows.reshape(GROUPS, count, 128), 'lat', split_axis=0, con...]
    all_to_all x5 -> x3, starting transfers between devices: 61.2 us -> 27.4 us  [exchange(): lax.all_to_all(rows.reshape(GROUPS, count, 128), 'lat', split_axis=0, con...]
    all_to_all x5 -> x3, waiting for transfers between devices: 23 us -> 55.3 us  [exchange(): lax.all_to_all(rows.reshape(GROUPS, count, 128), 'lat', split_axis=0, con...]
    unnamed x47 -> x15, local copies, waits for them, and re-layouts: 10.8 us -> 1.75 us
  transfers between devices with their start and end apart: 5 -> 5, of which waited for: 1 -> 3; matrix products, arithmetic and copies ran while one was open for 1% -> 1% of each run, Pallas kernels for 2% -> 11%
where the time goes in v6:
time: 204 us; the launch traced here: 203 us
  blocking collectives  69.6 us (34%)
  waiting for transfers between devices  55.4 us (27%)
  Pallas kernels  34 us (17%)
  starting transfers between devices  27.6 us (14%)
  between operations  14.2 us (7%)
  local copies, waits for them, and re-layouts  2.18 us (1%)
    all_to_all x3, blocking collectives, exchange(): lax.all_to_all(rows.reshape(GROUPS, count, 128), 'lat', split_axis=0, con...  69.6 us
    all_to_all x3, waiting for transfers between devices, exchange(): lax.all_to_all(rows.reshape(GROUPS, count, 128), 'lat', split_axis=0, con...  55.3 us
    all_to_all x3, starting transfers between devices, exchange(): lax.all_to_all(rows.reshape(GROUPS, count, 128), 'lat', split_axis=0, con...  27.4 us
    pallas_call x1, Pallas kernels, middle(): call(middle_kernel, message(SLOT_ROWS), [VMEM, ANY, ANY, ANY, ANY, VMEM,...  8.67 us
    pallas_call x1, Pallas kernels, weight_gradient(): call(gradient_kernel, jax.ShapeDtypeStruct((SLOTS, 2, CHANNELS, CHANNELS)...  7.38 us
    pallas_call x1, Pallas kernels, last(): call(last_kernel, message(LAST_ROWS), [VMEM, ANY, VMEM, VMEM, VMEM], [sta...  4.96 us
    pallas_call x1, Pallas kernels, first(): call(first_kernel, message(SENT_ROWS), [VMEM, ANY, VMEM, VMEM, VMEM, ANY]...  4.36 us
  transfers between devices with their start and end apart: 5, of which 3 were waited for; matrix products, arithmetic and copies ran while one was open for 1% of the time, Pallas kernels for 11%

profile of v6, /device:TPU:6, one launch (start us, length us, event | category | flops | bytes accessed | tf_op | source)
XLA Modules:
  0.0 203.1 jit_solution(9301321511435708101)
XLA Ops:
  7.2 3.9 %spread.1 = (bf16[3072,128]{1,0:T(8,128)(2,1)}, bf16[1536,128]{1,0:T(8,128)(2,1)S(1)}, bf16[1536,128]{1,0:T(8,128)(2,1)S(1)}) custom-call(bf16[3,384,384]{2,1,0:T(8,128)(2,1)} %bitcast.32, bf16[3,384,384]{2,1,0:T(8,128)(2,1)} %bitcast.21, bf16[384,256]{1,0:T(8,128)(2,1)} %constant.21.clone.forward_source.forward), custom_call_target="tpu_custom_call" | custom-call | flops 300000000 | bytes 4000000 | tf_op jit(solution)/shard_map/spread/pallas_call | solution.py:567
  11.1 0.0 copy-start.4
  11.1 16.6 %all-to-all-start = ((bf16[64,48,128]{2,1,0:T(8,128)(2,1)}), bf16[64,48,128]{2,1,0:T(8,128)(2,1)S(1)}, u32[]{:S(2)}, u32[]{:S(2)}) async-start(bf16[64,48,128]{2,1,0:T(8,128)(2,1)} %bitcast.2), calls=%async_computation | async-start | bytes 1572864 | tf_op jit(solution)/shard_map/all_to_all | solution.py:640
  27.7 0.0 all-gather.5.cloned.1.call-start
  27.8 0.1 reshape.45
  27.9 0.1 copy.25
  28.0 0.2 broadcast_in_dim_reshape.8.degree_col
  28.2 1.7 copy.26
  29.9 22.1 %all-to-all-done.one = bf16[64,48,128]{2,1,0:T(8,128)(2,1)S(1)} async-done(((bf16[64,48,128]{2,1,0:T(8,128)(2,1)}), bf16[64,48,128]{2,1,0:T(8,128)(2,1)S(1)}, u32[]{:S(2)}, u32[]{:S(2)}) %all-to-all-start) | async-done | bytes 786464 | tf_op jit(solution)/shard_map/all_to_all | solution.py:640
  51.9 4.4 %first.1 = bf16[3072,128]{1,0:T(8,128)(2,1)S(1)} custom-call(bf16[3072,128]{1,0:T(8,128)(2,1)S(1)} %bitcast.24, bf16[4608,192]{1,0:T(8,128)(2,1)} %constant.19.clone.analysis, s32[128,1]{1,0:T(8,128)S(1)} %broadcast_in_dim_reshape.8.degree_col, bf16[96,96]{1,0:T(8,128)(2,1)S(1)} %copy-done.4, bf16[1536,128]{1,0:T(8,128)(2,1)S(1)} %get-tuple-element.10.carried, ...), custom_call_target="tpu_custom_call" | custom-call | flops 1000000000 | bytes 6000000 | tf_op jit(solution)/shard_map/first/pallas_call | solution.py:580
  56.3 29.7 %all_to_all.30.two = bf16[64,48,128]{2,1,0:T(8,128)(2,1)S(1)} all-to-all(bf16[64,48,128]{2,1,0:T(8,128)(2,1)S(1)} %bitcast.25), channel_id=1, replica_groups=mesh['lat'=64,'batch'=8] {'lat'}, dimensions={0} | all-to-all | bytes 1572864 | tf_op jit(solution)/shard_map/all_to_all | solution.py:640
  86.0 2.0 mix.1
  88.0 0.0 all-gather.5.cloned.1.call-update
  88.0 5.9 %all-to-all-start.2 = ((bf16[64,48,128]{2,1,0:T(8,128)(2,1)}), bf16[64,48,128]{2,1,0:T(8,128)(2,1)S(1)}, u32[]{:S(2)}, u32[]{:S(2)}) async-start(bf16[64,48,128]{2,1,0:T(8,128)(2,1)} %bitcast.8), calls=%async_computation.2 | async-start | bytes 1572864 | tf_op jit(solution)/shard_map/all_to_all | solution.py:640
  93.9 0.2 all-gather.7.cloned.1.call-start
  94.2 0.1 broadcast_in_dim_reshape.7.degree_row
  94.2 22.5 %all-to-all-done.2 = bf16[64,48,128]{2,1,0:T(8,128)(2,1)S(1)} async-done(((bf16[64,48,128]{2,1,0:T(8,128)(2,1)}), bf16[64,48,128]{2,1,0:T(8,128)(2,1)S(1)}, u32[]{:S(2)}, u32[]{:S(2)}) %all-to-all-start.2) | async-done | bytes 786464 | tf_op jit(solution)/shard_map/all_to_all | solution.py:640
  116.8 8.7 %middle.1 = bf16[1536,128]{1,0:T(8,128)(2,1)S(1)} custom-call(bf16[3072,128]{1,0:T(8,128)(2,1)S(1)} %bitcast.28, bf16[64,48,128]{2,1,0:T(8,128)(2,1)S(1)} %all-to-all-done.one, bf16[64,48,128]{2,1,0:T(8,128)(2,1)S(1)} %all_to_all.30.two, bf16[4608,192]{1,0:T(8,128)(2,1)} %constant.18.clone.analysis, bf16[6144,256]{1,0:T(8,128)(2,1)} %constant.20.clone.synthesis, ...), custom_call_target="tpu_custom_call" | custom-call | flops 3000000000 | bytes 12000000 | tf_op jit(solution)/shard_map/middle/pallas_call | solution.py:592
  125.5 0.0 copy-start.5
  125.5 20.9 %all_to_all.31 = bf16[64,24,128]{2,1,0:T(8,128)(2,1)S(1)} all-to-all(bf16[64,24,128]{2,1,0:T(8,128)(2,1)S(1)} %bitcast.30), channel_id=1, replica_groups=mesh['lat'=64,'batch'=8] {'lat'}, dimensions={0} | all-to-all | bytes 786432 | tf_op jit(solution)/shard_map/all_to_all | solution.py:640
  146.4 1.3 adjoint_mix.1
  147.7 0.0 all-gather.7.cloned.1.call-update
  147.7 19.0 %all_to_all.32 = bf16[64,24,128]{2,1,0:T(8,128)(2,1)S(1)} all-to-all(bf16[64,24,128]{2,1,0:T(8,128)(2,1)S(1)} %bitcast.29), channel_id=1, replica_groups=mesh['lat'=64,'batch'=8] {'lat'}, dimensions={0} | all-to-all | bytes 786432 | tf_op jit(solution)/shard_map/all_to_all | solution.py:640
  166.8 5.0 %last.1 = bf16[2560,128]{1,0:T(8,128)(2,1)} custom-call(bf16[1536,128]{1,0:T(8,128)(2,1)S(1)} %bitcast.27, bf16[6144,256]{1,0:T(8,128)(2,1)} %constant.20.clone.synthesis, s32[1,128]{1,0:T(1,128)S(1)} %broadcast_in_dim_reshape.7.degree_row, f32[96,1]{1,0:T(8,128)S(1)} %copy-done.5, bf16[96,96]{1,0:T(8,128)(2,1)S(1)} %copy-done.4), custom_call_target="tpu_custom_call" | custom-call | flops 1000000000 | bytes 7000000 | tf_op jit(solution)/shard_map/last/pallas_call | solution.py:608
  171.7 4.9 %all-to-all-start.5 = ((bf16[64,40,128]{2,1,0:T(8,128)(2,1)}), bf16[64,40,128]{2,1,0:T(8,128)(2,1)S(1)}, u32[]{:S(2)}, u32[]{:S(2)}) async-start(bf16[64,40,128]{2,1,0:T(8,128)(2,1)} %bitcast.14), calls=%async_computation.5 | async-start | bytes 1310720 | tf_op jit(solution)/shard_map/all_to_all | solution.py:640
  176.6 0.0 all-gather.5.cloned.1.call-done
  176.6 0.0 all-gather.7.cloned.1.call-done
  176.7 0.0 copy-start
  176.7 0.0 copy-start.2
  176.7 7.4 %weight_gradient.1.weight_grads = bf16[2,2,384,384]{3,2,1,0:T(8,128)(2,1)} custom-call(bf16[8,2,384,256]{3,2,1,0:T(8,128)(2,1)} %bitcast.35, bf16[8,2,384,256]{3,2,1,0:T(8,128)(2,1)} %bitcast.36, bf16[256,256]{1,0:T(8,128)(2,1)S(1)} %copy-done.3), custom_call_target="tpu_custom_call" | custom-call | flops 5000000000 | bytes 8000000 | tf_op jit(solution)/shard_map/weight_gradient/pallas_call | solution.py:671
  184.1 10.7 %all-to-all-done.5 = bf16[64,40,128]{2,1,0:T(8,128)(2,1)S(1)} async-done(((bf16[64,40,128]{2,1,0:T(8,128)(2,1)}), bf16[64,40,128]{2,1,0:T(8,128)(2,1)S(1)}, u32[]{:S(2)}, u32[]{:S(2)}) %all-to-all-start.5) | async-done | bytes 655392 | tf_op jit(solution)/shard_map/all_to_all | solution.py:640
  194.8 1.5 gather.1
  (10 shorter events, 0.0 us)
Async XLA Ops:
  7.2 20.6 %copy-start.6 = (s32[128]{0:T(128)S(1)}, s32[128]{0:T(128)}, u32[]{:S(2)}) copy-start(s32[128]{0:T(128)} %param.16) | copy-start | bytes 1540
  11.1 40.8 %copy-start.4 = (bf16[96,96]{1,0:T(8,128)(2,1)S(1)}, bf16[96,96]{1,0:T(8,128)(2,1)}, u32[]{:S(2)}) copy-start(bf16[96,96]{1,0:T(8,128)(2,1)} %constant.25.clone.flip) | copy-start | bytes 55300
  11.1 40.8 %all-to-all-start = ((bf16[64,48,128]{2,1,0:T(8,128)(2,1)}), bf16[64,48,128]{2,1,0:T(8,128)(2,1)S(1)}, u32[]{:S(2)}, u32[]{:S(2)}) async-start(bf16[64,48,128]{2,1,0:T(8,128)(2,1)} %bitcast.2), calls=%async_computation | async-start | bytes 1572864 | tf_op jit(solution)/shard_map/all_to_all | solution.py:640
  27.7 148.9 %all-gather.5.cloned.1.call-start = ((), (), s32[]{:S(2)}) async-start(), calls=%async_computation.6 | async-start | bytes 3538944 | tf_op jit(solution)/shard_map/all_gather | solution.py:689
  51.9 34.1 %copy-start.3 = (bf16[256,256]{1,0:T(8,128)(2,1)S(1)}, bf16[256,256]{1,0:T(8,128)(2,1)}, u32[]{:S(2)}) copy-start(bf16[256,256]{1,0:T(8,128)(2,1)} %constant.24.clone.turn) | copy-start | bytes 393220
  88.0 28.8 %all-to-all-start.2 = ((bf16[64,48,128]{2,1,0:T(8,128)(2,1)}), bf16[64,48,128]{2,1,0:T(8,128)(2,1)S(1)}, u32[]{:S(2)}, u32[]{:S(2)}) async-start(bf16[64,48,128]{2,1,0:T(8,128)(2,1)} %bitcast.8), calls=%async_computation.2 | async-start | bytes 1572864 | tf_op jit(solution)/shard_map/all_to_all | solution.py:640
  93.9 82.7 %all-gather.7.cloned.1.call-start = ((), (), s32[]{:S(2)}) async-start(), calls=%async_computation.7 | async-start | bytes 3538944 | tf_op jit(solution)/shard_map/all_gather | solution.py:700
  116.8 29.6 %copy-start.1 = (bf16[2,2,384,384]{3,2,1,0:T(8,128)(2,1)S(1)}, bf16[2,2,384,384]{3,2,1,0:T(8,128)(2,1)}, u32[]{:S(2)}) copy-start(bf16[2,2,384,384]{3,2,1,0:T(8,128)(2,1)} %weights.1) | copy-start | bytes 3538948
  125.5 41.3 %copy-start.5 = (f32[96,1]{1,0:T(8,128)S(1)}, f32[96,1]{1,0:T(8,128)}, u32[]{:S(2)}) copy-start(f32[96,1]{1,0:T(8,128)} %constant.26.clone.weight_rows) | copy-start | bytes 1156
  171.7 23.0 %all-to-all-start.5 = ((bf16[64,40,128]{2,1,0:T(8,128)(2,1)}), bf16[64,40,128]{2,1,0:T(8,128)(2,1)S(1)}, u32[]{:S(2)}, u32[]{:S(2)}) async-start(bf16[64,40,128]{2,1,0:T(8,128)(2,1)} %bitcast.14), calls=%async_computation.5 | async-start | bytes 1310720 | tf_op jit(solution)/shard_map/all_to_all | solution.py:640
  176.7 18.1 %copy-start = (bf16[1,3,384,384]{3,2,1,0:T(8,128)(2,1)S(1)}, bf16[1,3,384,384]{3,2,1,0:T(8,128)(2,1)}, u32[]{:S(2)}) copy-start(bf16[1,3,384,384]{3,2,1,0:T(8,128)(2,1)} %param.14) | copy-start | bytes 2654212
  176.7 18.1 %copy-start.2 = (bf16[384,256]{1,0:T(8,128)(2,1)S(1)}, bf16[384,256]{1,0:T(8,128)(2,1)}, u32[]{:S(2)}) copy-start(bf16[384,256]{1,0:T(8,128)(2,1)} %constant.21.clone.forward_source.forward) | copy-start | bytes 589828
Sparse Core Ops, SparseCore 0:
  88.1 25.8 all-gather.4
  147.8 24.5 all-gather.6

commit v7 on v6

--- a/solution.py
+++ b/solution.py
@@ -90,16 +90,21 @@
 
     analysis = for_analysis(table[:, :, low])
     weighted = for_analysis((table * quadrature)[:, :, low])
-    below = table[:, :, low].astype(bf16)
-    synthesis = np.concatenate(
-        [
-            np.concatenate([below[16 * t + k + 4 * g, odd::2].T for g in range(4)], axis=1)
-            for t in range(BLOCKS)
-            for odd in (0, 1)
-            for k in range(4)
-        ],
-        axis=0,
-    )
+
+    def for_synthesis(values):
+        values = values.astype(bf16)
+        return np.concatenate(
+            [
+                np.concatenate([values[16 * t + k + 4 * g, odd::2].T for g in range(4)], axis=1)
+                for t in range(BLOCKS)
+                for odd in (0, 1)
+                for k in range(4)
+            ],
+            axis=0,
+        )
+
+    synthesis = for_synthesis(table[:, :, low])
+    weighted_synthesis = for_synthesis((table * quadrature)[:, :, low])
     forward, inverse = fourier_tables()
     turn = np.zeros((COEFS, COEFS), np.float32)
     even = np.arange(0, COEFS, 2)
@@ -109,12 +114,11 @@
         analysis=analysis,
         weighted=weighted,
         synthesis=synthesis,
+        weighted_synthesis=weighted_synthesis,
         forward=forward,
         inverse=inverse,
         inverse_t=np.ascontiguousarray(inverse.T),
         turn=turn.astype(bf16),
-        flip=np.eye(LOW)[::-1].astype(bf16),
-        weight_rows=quadrature[low].astype(np.float32)[:, None],
     )
 
 
@@ -192,6 +196,11 @@
     return jnp.where((lanes // 2) % 2 == 0, 1.0, -1.0).astype(f32)
 
 
+def reversal():
+    row = lax.broadcasted_iota(jnp.int32, (LOW, LOW), 0)
+    return (row + lane_of((LOW, LOW)) == LOW - 1).astype(f32).astype(bf16)
+
+
 def fold(pair, flip):
     x = jnp.concatenate(pair, axis=1)
     low = jnp.concatenate([x[i * GROUPS : i * GROUPS + HALF] for i in range(BAND)], axis=0)
@@ -201,12 +210,10 @@
     return [[x[:, :128], x[:, 128:]] for x in both]
 
 
-def unfold(even, odd, flip, weight):
+def unfold(even, odd, flip):
     even, odd = jnp.concatenate(even, axis=1), jnp.concatenate(odd, axis=1)
     low = even + odd
     high = (even - odd) * order_sign(lane_of(low.shape))
-    if weight is not None:
-        low, high = low * weight, high * weight
     high = dot(flip, high.astype(bf16))
     pieces = []
     for i in range(BAND):
@@ -247,7 +254,7 @@
     return merge_blocks(sums)
 
 
-def synthesise(tiles, flip, weight, table, ready):
+def synthesise(tiles, table, ready):
     sums = ([], [])
     order = (lane_of((LOW, 256)) % 8) // 2
     for t in range(BLOCKS):
@@ -261,7 +268,8 @@
                 total = jnp.where(order == k, part[k * LOW : (k + 1) * LOW], total)
             sums[odd].append(total)
     even, odd = merge_blocks(sums[0]), merge_blocks(sums[1])
-    return from_tiles([unfold(e, o, flip, weight) for e, o in zip(even, odd)])
+    flip = reversal()
+    return from_tiles([unfold(e, o, flip) for e, o in zip(even, odd)])
 
 
 def permute_rows(matrix, tiles):
@@ -382,7 +390,7 @@
 
 
 def first_kernel(
-    received, analysis, degree_col, flip, carried, early, out, stage_in, stage, table, sems
+    received, analysis, degree_col, carried, early, out, stage_in, stage, table, sems
 ):
     copies = table_copies(analysis, table, sems, STARTS)
     for copy in copies:
@@ -401,7 +409,7 @@
         ]
         for q in range(PARTS)
     ]
-    sums = analyse(parts, flip[...], table, lambda t: copies[t].wait())
+    sums = analyse(parts, reversal(), table, lambda t: copies[t].wait())
     slot_rows_out(sums, degree_col, carried, stage, out)
 
 
@@ -413,7 +421,7 @@
 
 
 def middle_kernel(
-    received, one, two, analysis, synthesis, degree_row, degree_col, flip, inverse_source, turned_source, out,
+    received, one, two, analysis, synthesis, degree_row, degree_col, inverse_source, turned_source, out,
     inverse, inverse_t, rows_one, rows_two, stage_one, stage_two, stage, table, table_s, row_sems, sems, sems_s,
 ):
     copies_s = table_copies(synthesis, table_s, sems_s, STEPS)
@@ -427,7 +435,7 @@
     for copy in (*copies_s, *fetches, *copies):
         copy.start()
     tiles = slot_rows_in(received, degree_row, stage)
-    synth = synthesise(tiles, flip[...], None, table_s, lambda t: copies_s[t].wait())
+    synth = synthesise(tiles, table_s, lambda t: copies_s[t].wait())
     for fetch in fetches:
         fetch.wait()
     stage_one[...] = rows_one[...].astype(f32).reshape(GROUPS * 16, 128)
@@ -452,18 +460,13 @@
         upstream = (cotangent * gelu_slope(response)).astype(bf16)
         grad = dot(upstream, inverse[...])
         parts.append([grad[:, :128], grad[:, 128:]])
-    sums = analyse(parts, flip[...], table, lambda t: copies[t].wait())
+    sums = analyse(parts, reversal(), table, lambda t: copies[t].wait())
     slot_rows_out(sums, degree_col, None, stage, out)
 
 
-def last_kernel(received, synthesis, degree_row, weight_rows, flip, out, stage, stage_out, table_s, sems_s):
-    copies_s = table_copies(synthesis, table_s, sems_s, STEPS)
-    for copy in copies_s:
-        copy.start()
+def last_kernel(received, table, degree_row, out, stage, stage_out):
     tiles = slot_rows_in(received, degree_row, stage)
-    synth = synthesise(
-        tiles, flip[...], weight_rows[...], table_s, lambda t: copies_s[t].wait()
-    )
+    synth = synthesise(tiles, table, lambda t: None)
     for q in range(PARTS):
         for h in range(2):
             scaled = synth[q][h]
@@ -576,23 +579,23 @@
     )(in_hbm(fields), in_hbm(cotangent), in_hbm(forward))
 
 
-def first(received, weighted, degree_col, flip, carried, early):
+def first(received, weighted, degree_col, carried, early):
     return call(
         first_kernel,
         message(SENT_ROWS),
-        [VMEM, ANY, VMEM, VMEM, VMEM, ANY],
+        [VMEM, ANY, VMEM, VMEM, ANY],
         [stage_of(SENT_ROWS), stage_of(SENT_ROWS), TABLE, sems(BLOCKS)],
         10**9, 6 * 10**6, "first",
-    )(received, in_hbm(weighted), degree_col, flip, carried, early)
+    )(received, in_hbm(weighted), degree_col, carried, early)
 
 
 def middle(
-    received, one, two, analysis, synthesis, degree_row, degree_col, flip, inverse, inverse_t
+    received, one, two, analysis, synthesis, degree_row, degree_col, inverse, inverse_t
 ):
     return call(
         middle_kernel,
         message(SLOT_ROWS),
-        [VMEM, ANY, ANY, ANY, ANY, VMEM, VMEM, VMEM, ANY, ANY],
+        [VMEM, ANY, ANY, ANY, ANY, VMEM, VMEM, ANY, ANY],
         [
             pltpu.VMEM((LONS, COEFS), bf16), pltpu.VMEM((COEFS, LONS), bf16),
             pltpu.VMEM((GROUPS, 16, 128), bf16), pltpu.VMEM((GROUPS, 32, 128), bf16),
@@ -600,18 +603,18 @@
             TABLE, TABLE_S, sems(4), sems(BLOCKS), sems(BLOCKS),
         ],
         3 * 10**9, 12 * 10**6, "middle",
-    )(received, one, two, in_hbm(analysis), in_hbm(synthesis), degree_row, degree_col, flip,
+    )(received, one, two, in_hbm(analysis), in_hbm(synthesis), degree_row, degree_col,
       in_hbm(inverse), in_hbm(inverse_t))
 
 
-def last(received, synthesis, degree_row, weight_rows, flip):
+def last(received, table, degree_row):
     return call(
         last_kernel,
-        message(LAST_ROWS),
-        [VMEM, ANY, VMEM, VMEM, VMEM],
-        [stage_of(SLOT_ROWS), stage_of(LAST_ROWS), TABLE_S, sems(BLOCKS)],
+        pltpu.HBM((GROUPS * LAST_ROWS, 128), bf16),
+        [VMEM, VMEM, VMEM],
+        [stage_of(SLOT_ROWS), stage_of(LAST_ROWS)],
         10**9, 7 * 10**6, "last",
-    )(received, in_hbm(synthesis), degree_row, weight_rows, flip)
+    )(received, table, degree_row)
 
 
 def gather(received, forward, cotangent, weight_grads):
@@ -684,7 +687,7 @@
     turned_weights = jnp.swapaxes(weights, 2, 3)
     sent, cot_two, cot_three = spread(fields[0], cotangent[0], table["forward"])
     one = exchange(sent)
-    two = exchange(first(one, table["weighted"], degree_col, table["flip"], cot_two, turned_weights))
+    two = exchange(first(one, table["weighted"], degree_col, cot_two, turned_weights))
     filtered, coeffs = mix(False, two, turned_weights, table["turn"], cot_three)
     all_coeffs = lax.all_gather(coeffs, "batch", axis=0)
     three = exchange(filtered)
@@ -692,7 +695,7 @@
     four = exchange(
         middle(
             three, one.reshape(as_sent), two.reshape(as_sent), table["analysis"],
-            table["synthesis"], degree_row, degree_col, table["flip"],
+            table["synthesis"], degree_row, degree_col,
             table["inverse"], table["inverse_t"],
         )
     )
@@ -700,7 +703,7 @@
     all_grads = lax.all_gather(grads, "batch", axis=0)
     grad_weights = weight_gradient(all_coeffs, all_grads, table["turn"])
     five = exchange(grad_coeffs)
-    six = exchange(last(five, table["synthesis"], degree_row, table["weight_rows"], table["flip"]))
+    six = exchange(last(five, table["weighted_synthesis"], degree_row))
     grad_fields = gather(six, table["forward"], cotangent[0], grad_weights)[None]
     return grad_fields, grad_weights
 

time: 204 us -> 201 us (0.985)
  Pallas kernels: 34 us -> 31.9 us
    pallas_call x2, Pallas kernels: 9.32 us -> 7.2 us  [the longest x1 4.35 us: first(): call(first_kernel, message(SENT_ROWS), [VMEM, ANY, VMEM, VMEM, ANY], [sta...]
  transfers between devices with their start and end apart: 5 -> 5, of which waited for: 3 -> 3; matrix products, arithmetic and copies ran while one was open for 1% -> 1% of each run, Pallas kernels for 11% -> 10%
where the time goes in v7:
time: 201 us
  blocking collectives  69.6 us (35%)
  waiting for transfers between devices  55.2 us (27%)
  Pallas kernels  31.9 us (16%)
  starting transfers between devices  27.6 us (14%)
  between operations  14.2 us (7%)
  local copies, waits for them, and re-layouts  2.18 us (1%)
    all_to_all x3, blocking collectives, exchange(): lax.all_to_all(rows.reshape(GROUPS, count, 128), 'lat', split_axis=0, con...  69.6 us
    all_to_all x3, waiting for transfers between devices, exchange(): lax.all_to_all(rows.reshape(GROUPS, count, 128), 'lat', split_axis=0, con...  55.1 us
    all_to_all x3, starting transfers between devices, exchange(): lax.all_to_all(rows.reshape(GROUPS, count, 128), 'lat', split_axis=0, con...  27.4 us
    pallas_call x1, Pallas kernels, middle(): call(middle_kernel, message(SLOT_ROWS), [VMEM, ANY, ANY, ANY, ANY, VMEM,...  8.69 us
    pallas_call x1, Pallas kernels, weight_gradient(): call(gradient_kernel, jax.ShapeDtypeStruct((SLOTS, 2, CHANNELS, CHANNELS)...  7.38 us
    pallas_call x1, Pallas kernels, first(): call(first_kernel, message(SENT_ROWS), [VMEM, ANY, VMEM, VMEM, ANY], [sta...  4.35 us
  transfers between devices with their start and end apart: 5, of which 3 were waited for; matrix products, arithmetic and copies ran while one was open for 1% of the time, Pallas kernels for 10%

profile of v7, /device:TPU:6, one launch (start us, length us, event | category | flops | bytes accessed | tf_op | source)
XLA Modules:
  0.0 200.7 jit_solution(13960418854627927077)
XLA Ops:
  7.2 3.9 %spread.1 = (bf16[3072,128]{1,0:T(8,128)(2,1)}, bf16[1536,128]{1,0:T(8,128)(2,1)S(1)}, bf16[1536,128]{1,0:T(8,128)(2,1)S(1)}) custom-call(bf16[3,384,384]{2,1,0:T(8,128)(2,1)} %bitcast.33, bf16[3,384,384]{2,1,0:T(8,128)(2,1)} %bitcast.21, bf16[384,256]{1,0:T(8,128)(2,1)} %constant.20.clone.forward_source.forward), custom_call_target="tpu_custom_call" | custom-call | flops 300000000 | bytes 4000000 | tf_op jit(solution)/shard_map/spread/pallas_call | solution.py:570
  11.1 16.6 %all-to-all-start = ((bf16[64,48,128]{2,1,0:T(8,128)(2,1)}), bf16[64,48,128]{2,1,0:T(8,128)(2,1)S(1)}, u32[]{:S(2)}, u32[]{:S(2)}) async-start(bf16[64,48,128]{2,1,0:T(8,128)(2,1)} %bitcast.2), calls=%async_computation | async-start | bytes 1572864 | tf_op jit(solution)/shard_map/all_to_all | solution.py:643
  27.7 0.0 all-gather.5.cloned.1.call-start
  27.8 0.1 reshape.45
  27.9 0.1 copy.24
  28.0 0.2 broadcast_in_dim_reshape.8.degree_col
  28.1 1.7 copy.25
  29.9 22.1 %all-to-all-done.one = bf16[64,48,128]{2,1,0:T(8,128)(2,1)S(1)} async-done(((bf16[64,48,128]{2,1,0:T(8,128)(2,1)}), bf16[64,48,128]{2,1,0:T(8,128)(2,1)S(1)}, u32[]{:S(2)}, u32[]{:S(2)}) %all-to-all-start) | async-done | bytes 786464 | tf_op jit(solution)/shard_map/all_to_all | solution.py:643
  51.9 4.4 %first.1 = bf16[3072,128]{1,0:T(8,128)(2,1)S(1)} custom-call(bf16[3072,128]{1,0:T(8,128)(2,1)S(1)} %bitcast.24, bf16[4608,192]{1,0:T(8,128)(2,1)} %constant.17.clone.analysis, s32[128,1]{1,0:T(8,128)S(1)} %broadcast_in_dim_reshape.8.degree_col, bf16[1536,128]{1,0:T(8,128)(2,1)S(1)} %get-tuple-element.10.carried, bf16[2,2,384,384]{3,2,1,0:T(8,128)(2,1)S(1)} %bitcast.19), custom_call_target="tpu_custom_call" | custom-call | flops 1000000000 | bytes 6000000 | tf_op jit(solution)/shard_map/first/pallas_call | solution.py:583
  56.3 29.7 %all_to_all.30.two = bf16[64,48,128]{2,1,0:T(8,128)(2,1)S(1)} all-to-all(bf16[64,48,128]{2,1,0:T(8,128)(2,1)S(1)} %bitcast.25), channel_id=1, replica_groups=mesh['lat'=64,'batch'=8] {'lat'}, dimensions={0} | all-to-all | bytes 1572864 | tf_op jit(solution)/shard_map/all_to_all | solution.py:643
  86.0 0.0 copy-done.4
  86.0 2.0 mix.1
  87.9 0.0 all-gather.5.cloned.1.call-update
  88.0 5.9 %all-to-all-start.2 = ((bf16[64,48,128]{2,1,0:T(8,128)(2,1)}), bf16[64,48,128]{2,1,0:T(8,128)(2,1)S(1)}, u32[]{:S(2)}, u32[]{:S(2)}) async-start(bf16[64,48,128]{2,1,0:T(8,128)(2,1)} %bitcast.8), calls=%async_computation.2 | async-start | bytes 1572864 | tf_op jit(solution)/shard_map/all_to_all | solution.py:643
  93.9 0.2 all-gather.7.cloned.1.call-start
  94.1 0.1 broadcast_in_dim_reshape.7.degree_row
  94.2 22.5 %all-to-all-done.2 = bf16[64,48,128]{2,1,0:T(8,128)(2,1)S(1)} async-done(((bf16[64,48,128]{2,1,0:T(8,128)(2,1)}), bf16[64,48,128]{2,1,0:T(8,128)(2,1)S(1)}, u32[]{:S(2)}, u32[]{:S(2)}) %all-to-all-start.2) | async-done | bytes 786464 | tf_op jit(solution)/shard_map/all_to_all | solution.py:643
  116.7 8.7 %middle.1 = bf16[1536,128]{1,0:T(8,128)(2,1)S(1)} custom-call(bf16[3072,128]{1,0:T(8,128)(2,1)S(1)} %bitcast.28, bf16[64,48,128]{2,1,0:T(8,128)(2,1)S(1)} %all-to-all-done.one, bf16[64,48,128]{2,1,0:T(8,128)(2,1)S(1)} %all_to_all.30.two, bf16[4608,192]{1,0:T(8,128)(2,1)} %constant.16.clone.analysis, bf16[6144,256]{1,0:T(8,128)(2,1)} %constant.18.clone.synthesis, ...), custom_call_target="tpu_custom_call" | custom-call | flops 3000000000 | bytes 12000000 | tf_op jit(solution)/shard_map/middle/pallas_call | solution.py:595
  125.4 0.0 copy-start.1
  125.4 21.0 %all_to_all.31 = bf16[64,24,128]{2,1,0:T(8,128)(2,1)S(1)} all-to-all(bf16[64,24,128]{2,1,0:T(8,128)(2,1)S(1)} %bitcast.30), channel_id=1, replica_groups=mesh['lat'=64,'batch'=8] {'lat'}, dimensions={0} | all-to-all | bytes 786432 | tf_op jit(solution)/shard_map/all_to_all | solution.py:643
  146.4 1.3 adjoint_mix.1
  147.7 0.0 all-gather.7.cloned.1.call-update
  147.8 19.0 %all_to_all.32 = bf16[64,24,128]{2,1,0:T(8,128)(2,1)S(1)} all-to-all(bf16[64,24,128]{2,1,0:T(8,128)(2,1)S(1)} %bitcast.29), channel_id=1, replica_groups=mesh['lat'=64,'batch'=8] {'lat'}, dimensions={0} | all-to-all | bytes 786432 | tf_op jit(solution)/shard_map/all_to_all | solution.py:643
  166.7 2.8 %last.1 = bf16[2560,128]{1,0:T(8,128)(2,1)} custom-call(bf16[1536,128]{1,0:T(8,128)(2,1)S(1)} %bitcast.27, bf16[6144,256]{1,0:T(8,128)(2,1)S(1)} %copy-done.1, s32[1,128]{1,0:T(1,128)S(1)} %broadcast_in_dim_reshape.7.degree_row), custom_call_target="tpu_custom_call" | custom-call | flops 1000000000 | bytes 7000000 | tf_op jit(solution)/shard_map/last/pallas_call | solution.py:611
  169.6 4.9 %all-to-all-start.5 = ((bf16[64,40,128]{2,1,0:T(8,128)(2,1)}), bf16[64,40,128]{2,1,0:T(8,128)(2,1)S(1)}, u32[]{:S(2)}, u32[]{:S(2)}) async-start(bf16[64,40,128]{2,1,0:T(8,128)(2,1)} %bitcast.32), calls=%async_computation.5 | async-start | bytes 1310720 | tf_op jit(solution)/shard_map/all_to_all | solution.py:643
  174.4 0.0 all-gather.5.cloned.1.call-done
  174.5 0.0 all-gather.7.cloned.1.call-done
  174.5 0.0 copy-start
  174.5 0.0 copy-start.3
  174.5 7.4 %weight_gradient.1.weight_grads = bf16[2,2,384,384]{3,2,1,0:T(8,128)(2,1)} custom-call(bf16[8,2,384,256]{3,2,1,0:T(8,128)(2,1)} %bitcast.36, bf16[8,2,384,256]{3,2,1,0:T(8,128)(2,1)} %bitcast.37, bf16[256,256]{1,0:T(8,128)(2,1)S(1)} %copy-done.6), custom_call_target="tpu_custom_call" | custom-call | flops 5000000000 | bytes 8000000 | tf_op jit(solution)/shard_map/weight_gradient/pallas_call | solution.py:674
  181.9 10.5 %all-to-all-done.5 = bf16[64,40,128]{2,1,0:T(8,128)(2,1)S(1)} async-done(((bf16[64,40,128]{2,1,0:T(8,128)(2,1)}), bf16[64,40,128]{2,1,0:T(8,128)(2,1)S(1)}, u32[]{:S(2)}, u32[]{:S(2)}) %all-to-all-start.5) | async-done | bytes 655392 | tf_op jit(solution)/shard_map/all_to_all | solution.py:643
  192.5 1.5 gather.1
  (12 shorter events, 0.0 us)
Async XLA Ops:
  7.2 20.6 %copy-start.7 = (s32[128]{0:T(128)S(1)}, s32[128]{0:T(128)}, u32[]{:S(2)}) copy-start(s32[128]{0:T(128)} %param.15) | copy-start | bytes 1540
  11.1 40.8 %all-to-all-start = ((bf16[64,48,128]{2,1,0:T(8,128)(2,1)}), bf16[64,48,128]{2,1,0:T(8,128)(2,1)S(1)}, u32[]{:S(2)}, u32[]{:S(2)}) async-start(bf16[64,48,128]{2,1,0:T(8,128)(2,1)} %bitcast.2), calls=%async_computation | async-start | bytes 1572864 | tf_op jit(solution)/shard_map/all_to_all | solution.py:643
  27.7 146.7 %all-gather.5.cloned.1.call-start = ((), (), s32[]{:S(2)}) async-start(), calls=%async_computation.6 | async-start | bytes 3538944 | tf_op jit(solution)/shard_map/all_gather | solution.py:692
  51.9 34.0 %copy-start.4 = (bf16[256,256]{1,0:T(8,128)(2,1)S(1)}, bf16[256,256]{1,0:T(8,128)(2,1)}, u32[]{:S(2)}) copy-start(bf16[256,256]{1,0:T(8,128)(2,1)} %constant.23.clone.turn) | copy-start | bytes 393220
  88.0 28.7 %all-to-all-start.2 = ((bf16[64,48,128]{2,1,0:T(8,128)(2,1)}), bf16[64,48,128]{2,1,0:T(8,128)(2,1)S(1)}, u32[]{:S(2)}, u32[]{:S(2)}) async-start(bf16[64,48,128]{2,1,0:T(8,128)(2,1)} %bitcast.8), calls=%async_computation.2 | async-start | bytes 1572864 | tf_op jit(solution)/shard_map/all_to_all | solution.py:643
  93.9 80.6 %all-gather.7.cloned.1.call-start = ((), (), s32[]{:S(2)}) async-start(), calls=%async_computation.7 | async-start | bytes 3538944 | tf_op jit(solution)/shard_map/all_gather | solution.py:703
  116.7 29.7 %copy-start.2 = (bf16[2,2,384,384]{3,2,1,0:T(8,128)(2,1)S(1)}, bf16[2,2,384,384]{3,2,1,0:T(8,128)(2,1)}, u32[]{:S(2)}) copy-start(bf16[2,2,384,384]{3,2,1,0:T(8,128)(2,1)} %weights.1) | copy-start | bytes 3538948
  116.7 29.7 %copy-start.5 = (bf16[256,256]{1,0:T(8,128)(2,1)S(1)}, bf16[256,256]{1,0:T(8,128)(2,1)}, u32[]{:S(2)}) copy-start(bf16[256,256]{1,0:T(8,128)(2,1)} %constant.23.clone.turn) | copy-start | bytes 393220
  125.4 41.3 %copy-start.1 = (bf16[6144,256]{1,0:T(8,128)(2,1)S(1)}, bf16[6144,256]{1,0:T(8,128)(2,1)}, u32[]{:S(2)}) copy-start(bf16[6144,256]{1,0:T(8,128)(2,1)} %constant.19.clone.table) | copy-start | bytes 9437188
  166.7 7.8 %copy-start.6 = (bf16[256,256]{1,0:T(8,128)(2,1)S(1)}, bf16[256,256]{1,0:T(8,128)(2,1)}, u32[]{:S(2)}) copy-start(bf16[256,256]{1,0:T(8,128)(2,1)} %constant.23.clone.turn) | copy-start | bytes 393220
  169.6 22.9 %all-to-all-start.5 = ((bf16[64,40,128]{2,1,0:T(8,128)(2,1)}), bf16[64,40,128]{2,1,0:T(8,128)(2,1)S(1)}, u32[]{:S(2)}, u32[]{:S(2)}) async-start(bf16[64,40,128]{2,1,0:T(8,128)(2,1)} %bitcast.32), calls=%async_computation.5 | async-start | bytes 1310720 | tf_op jit(solution)/shard_map/all_to_all | solution.py:643
  174.5 18.0 %copy-start = (bf16[1,3,384,384]{3,2,1,0:T(8,128)(2,1)S(1)}, bf16[1,3,384,384]{3,2,1,0:T(8,128)(2,1)}, u32[]{:S(2)}) copy-start(bf16[1,3,384,384]{3,2,1,0:T(8,128)(2,1)} %param.13) | copy-start | bytes 2654212
  174.5 17.9 %copy-start.3 = (bf16[384,256]{1,0:T(8,128)(2,1)S(1)}, bf16[384,256]{1,0:T(8,128)(2,1)}, u32[]{:S(2)}) copy-start(bf16[384,256]{1,0:T(8,128)(2,1)} %constant.20.clone.forward_source.forward) | copy-start | bytes 589828
Sparse Core Ops, SparseCore 0:
  88.1 25.8 all-gather.4
  147.9 24.6 all-gather.6

commit v8 on v7

--- a/solution.py
+++ b/solution.py
@@ -272,10 +272,18 @@
     return from_tiles([unfold(e, o, flip) for e, o in zip(even, odd)])
 
 
-def permute_rows(matrix, tiles):
+def slot_choice(degrees):
+    shape = (DEGREES, DEGREES)
+    row, column = lax.broadcasted_iota(jnp.int32, shape, 0), lane_of(shape)
+    held = degrees[...] == 2 * (row % GROUPS) + row // GROUPS
+    moved = row == SLOTS * (column % GROUPS) + column // GROUPS
+    return dot(*[x.astype(f32).astype(bf16) for x in (held, moved)]).astype(bf16)
+
+
+def permute_rows(matrix, tiles, dims=NN):
     out = []
     for tile in tiles:
-        moved = dot(matrix, jnp.concatenate(tile, axis=1))
+        moved = dot(matrix, jnp.concatenate(tile, axis=1), dims)
         out.append(tuple(moved[:, 128 * n : 128 * (n + 1)] for n in range(3)))
     return out
 
@@ -315,16 +323,14 @@
     ]
 
 
-def slot_rows_out(tiles, degree_col, carried, stage, out):
-    row = lane_of((DEGREES, DEGREES))
-    pick = (degree_col[...] == 2 * (row % GROUPS) + row // GROUPS).astype(f32).astype(bf16)
-    put_slots(from_tiles(permute_rows(pick, as_bf16(tiles))), carried, stage, out)
-
-
-def slot_rows_in(received, degree_row, stage):
-    row = lax.broadcasted_iota(jnp.int32, (DEGREES, DEGREES), 0)
-    pick = (degree_row[...] == 2 * (row % GROUPS) + row // GROUPS).astype(f32).astype(bf16)
-    return as_bf16(permute_rows(pick, as_bf16(to_tiles(get_slots(received, stage)))))
+def slot_rows_out(tiles, degrees, carried, stage, out):
+    moved = permute_rows(slot_choice(degrees), as_bf16(tiles), TN)
+    put_slots(from_tiles(moved), carried, stage, out)
+
+
+def slot_rows_in(received, degrees, stage):
+    tiles = as_bf16(to_tiles(get_slots(received, stage)))
+    return as_bf16(permute_rows(slot_choice(degrees), tiles))
 
 
 def table_copies(source, target, sems, bounds):
@@ -390,11 +396,8 @@
 
 
 def first_kernel(
-    received, analysis, degree_col, carried, early, out, stage_in, stage, table, sems
+    received, table, degrees, carried, out, stage_in, stage
 ):
-    copies = table_copies(analysis, table, sems, STARTS)
-    for copy in copies:
-        copy.start()
     stage_in[...] = received[...].astype(f32)
     parts = [
         [
@@ -409,8 +412,8 @@
         ]
         for q in range(PARTS)
     ]
-    sums = analyse(parts, reversal(), table, lambda t: copies[t].wait())
-    slot_rows_out(sums, degree_col, carried, stage, out)
+    sums = analyse(parts, reversal(), table, lambda t: None)
+    slot_rows_out(sums, degrees, carried, stage, out)
 
 
 def gelu_slope(x):
@@ -421,7 +424,7 @@
 
 
 def middle_kernel(
-    received, one, two, analysis, synthesis, degree_row, degree_col, inverse_source, turned_source, out,
+    received, one, two, analysis, synthesis, degrees, inverse_source, turned_source, out,
     inverse, inverse_t, rows_one, rows_two, stage_one, stage_two, stage, table, table_s, row_sems, sems, sems_s,
 ):
     copies_s = table_copies(synthesis, table_s, sems_s, STEPS)
@@ -434,7 +437,7 @@
     )
     for copy in (*copies_s, *fetches, *copies):
         copy.start()
-    tiles = slot_rows_in(received, degree_row, stage)
+    tiles = slot_rows_in(received, degrees, stage)
     synth = synthesise(tiles, table_s, lambda t: copies_s[t].wait())
     for fetch in fetches:
         fetch.wait()
@@ -461,11 +464,11 @@
         grad = dot(upstream, inverse[...])
         parts.append([grad[:, :128], grad[:, 128:]])
     sums = analyse(parts, reversal(), table, lambda t: copies[t].wait())
-    slot_rows_out(sums, degree_col, None, stage, out)
-
-
-def last_kernel(received, table, degree_row, out, stage, stage_out):
-    tiles = slot_rows_in(received, degree_row, stage)
+    slot_rows_out(sums, degrees, None, stage, out)
+
+
+def last_kernel(received, table, degrees, out, stage, stage_out):
+    tiles = slot_rows_in(received, degrees, stage)
     synth = synthesise(tiles, table, lambda t: None)
     for q in range(PARTS):
         for h in range(2):
@@ -512,7 +515,8 @@
         if adjoint:
             turned = -turned
         turned = turned.astype(bf16)
-        results.append(dot(weights[j, 0], held) + dot(weights[j, 1], turned))
+        dims = NN if adjoint else TN
+        results.append(dot(weights[j, 0], held, dims) + dot(weights[j, 1], turned, dims))
     mixed = [
         [
             jnp.concatenate(
@@ -579,23 +583,23 @@
     )(in_hbm(fields), in_hbm(cotangent), in_hbm(forward))
 
 
-def first(received, weighted, degree_col, carried, early):
+def first(received, weighted, degrees, carried):
     return call(
         first_kernel,
         message(SENT_ROWS),
-        [VMEM, ANY, VMEM, VMEM, ANY],
-        [stage_of(SENT_ROWS), stage_of(SENT_ROWS), TABLE, sems(BLOCKS)],
+        [VMEM, VMEM, VMEM, VMEM],
+        [stage_of(SENT_ROWS), stage_of(SENT_ROWS)],
         10**9, 6 * 10**6, "first",
-    )(received, in_hbm(weighted), degree_col, carried, early)
+    )(received, weighted, degrees, carried)
 
 
 def middle(
-    received, one, two, analysis, synthesis, degree_row, degree_col, inverse, inverse_t
+    received, one, two, analysis, synthesis, degrees, inverse, inverse_t
 ):
     return call(
         middle_kernel,
         message(SLOT_ROWS),
-        [VMEM, ANY, ANY, ANY, ANY, VMEM, VMEM, ANY, ANY],
+        [VMEM, ANY, ANY, ANY, ANY, VMEM, ANY, ANY],
         [
             pltpu.VMEM((LONS, COEFS), bf16), pltpu.VMEM((COEFS, LONS), bf16),
             pltpu.VMEM((GROUPS, 16, 128), bf16), pltpu.VMEM((GROUPS, 32, 128), bf16),
@@ -603,18 +607,18 @@
             TABLE, TABLE_S, sems(4), sems(BLOCKS), sems(BLOCKS),
         ],
         3 * 10**9, 12 * 10**6, "middle",
-    )(received, one, two, in_hbm(analysis), in_hbm(synthesis), degree_row, degree_col,
+    )(received, one, two, in_hbm(analysis), in_hbm(synthesis), degrees,
       in_hbm(inverse), in_hbm(inverse_t))
 
 
-def last(received, table, degree_row):
+def last(received, table, degrees):
     return call(
         last_kernel,
         pltpu.HBM((GROUPS * LAST_ROWS, 128), bf16),
         [VMEM, VMEM, VMEM],
         [stage_of(SLOT_ROWS), stage_of(LAST_ROWS)],
         10**9, 7 * 10**6, "last",
-    )(received, table, degree_row)
+    )(received, table, degrees)
 
 
 def gather(received, forward, cotangent, weight_grads):
@@ -682,20 +686,18 @@
 
 def local(fields, cotangent, weights, degree_of):
     table = {k: jnp.asarray(v) for k, v in constants().items()}
-    slots = degree_of.reshape(GROUPS, SLOTS).T.reshape(DEGREES)
-    degree_col, degree_row = slots[:, None], slots[None, :]
-    turned_weights = jnp.swapaxes(weights, 2, 3)
+    degrees = degree_of[None, :]
     sent, cot_two, cot_three = spread(fields[0], cotangent[0], table["forward"])
     one = exchange(sent)
-    two = exchange(first(one, table["weighted"], degree_col, cot_two, turned_weights))
-    filtered, coeffs = mix(False, two, turned_weights, table["turn"], cot_three)
+    two = exchange(first(one, table["weighted"], degrees, cot_two))
+    filtered, coeffs = mix(False, two, weights, table["turn"], cot_three)
     all_coeffs = lax.all_gather(coeffs, "batch", axis=0)
     three = exchange(filtered)
     as_sent = (GROUPS, SENT_ROWS, 128)
     four = exchange(
         middle(
             three, one.reshape(as_sent), two.reshape(as_sent), table["analysis"],
-            table["synthesis"], degree_row, degree_col,
+            table["synthesis"], degrees,
             table["inverse"], table["inverse_t"],
         )
     )
@@ -703,7 +705,7 @@
     all_grads = lax.all_gather(grads, "batch", axis=0)
     grad_weights = weight_gradient(all_coeffs, all_grads, table["turn"])
     five = exchange(grad_coeffs)
-    six = exchange(last(five, table["weighted_synthesis"], degree_row))
+    six = exchange(last(five, table["weighted_synthesis"], degrees))
     grad_fields = gather(six, table["forward"], cotangent[0], grad_weights)[None]
     return grad_fields, grad_weights
 

time: 201 us -> 197 us (0.980)
  blocking collectives: 69.6 us -> 139 us
  waiting for transfers between devices: 55.2 us -> 10.6 us
  starting transfers between devices: 27.6 us -> 4.94 us
  Pallas kernels: 31.9 us -> 28.5 us
  local copies, waits for them, and re-layouts: 2.18 us -> 0.05 us
    all_to_all x3 -> x5, blocking collectives: 69.6 us -> 139 us  [exchange(): lax.all_to_all(rows.reshape(GROUPS, count, 128), 'lat', split_axis=0, con...]
    all_to_all x3 -> x1, waiting for transfers between devices: 55.1 us -> 10.5 us  [exchange(): lax.all_to_all(rows.reshape(GROUPS, count, 128), 'lat', split_axis=0, con...]
    all_to_all x3 -> x1, starting transfers between devices: 27.4 us -> 4.86 us  [exchange(): lax.all_to_all(rows.reshape(GROUPS, count, 128), 'lat', split_axis=0, con...]
    pallas_call x1, Pallas kernels: 4.35 us -> 2.24 us  [first(): call(first_kernel, message(SENT_ROWS), [VMEM, VMEM, VMEM, VMEM], [stage_o...]
  transfers between devices with their start and end apart: 5 -> 3, of which waited for: 3 -> 1; matrix products, arithmetic and copies ran while one was open for 1% -> 0% of each run, Pallas kernels for 10% -> 10%
where the time goes in v8:
time: 197 us
  blocking collectives  139 us (71%)
  Pallas kernels  28.5 us (14%)
  between operations  14.2 us (7%)
  waiting for transfers between devices  10.6 us (5%)
  starting transfers between devices  4.94 us (3%)
    all_to_all x5, blocking collectives, exchange(): lax.all_to_all(rows.reshape(GROUPS, count, 128), 'lat', split_axis=0, con...  139 us
    all_to_all x1, waiting for transfers between devices, exchange(): lax.all_to_all(rows.reshape(GROUPS, count, 128), 'lat', split_axis=0, con...  10.5 us
    pallas_call x1, Pallas kernels, middle(): call(middle_kernel, message(SLOT_ROWS), [VMEM, ANY, ANY, ANY, ANY, VMEM,...  8.83 us
    pallas_call x1, Pallas kernels, weight_gradient(): call(gradient_kernel, jax.ShapeDtypeStruct((SLOTS, 2, CHANNELS, CHANNELS)...  7.38 us
    all_to_all x1, starting transfers between devices, exchange(): lax.all_to_all(rows.reshape(GROUPS, count, 128), 'lat', split_axis=0, con...  4.86 us
  transfers between devices with their start and end apart: 3, of which 1 were waited for; matrix products, arithmetic and copies ran while one was open for 0% of the time, Pallas kernels for 10%

profile of v8, /device:TPU:6, one launch (start us, length us, event | category | flops | bytes accessed | tf_op | source)
XLA Modules:
  0.0 197.1 jit_solution(3616003043877754004)
XLA Ops:
  7.2 0.0 copy-start.2
  7.2 0.0 copy-start.9
  7.2 0.0 all-gather.5.cloned.1.call-start
  7.2 3.2 %spread.1 = (bf16[3072,128]{1,0:T(8,128)(2,1)S(1)}, bf16[1536,128]{1,0:T(8,128)(2,1)S(1)}, bf16[1536,128]{1,0:T(8,128)(2,1)S(1)}) custom-call(bf16[3,384,384]{2,1,0:T(8,128)(2,1)} %bitcast.35, bf16[3,384,384]{2,1,0:T(8,128)(2,1)} %bitcast.18, bf16[384,256]{1,0:T(8,128)(2,1)} %constant.20.clone.forward_source.forward), custom_call_target="tpu_custom_call" | custom-call | flops 300000000 | bytes 4000000 | tf_op jit(solution)/shard_map/spread/pallas_call | solution.py:574
  10.4 40.6 %all_to_all.30.one = bf16[64,48,128]{2,1,0:T(8,128)(2,1)S(1)} all-to-all(bf16[64,48,128]{2,1,0:T(8,128)(2,1)S(1)} %bitcast.27), channel_id=1, replica_groups=mesh['lat'=64,'batch'=8] {'lat'}, dimensions={0} | all-to-all | bytes 1572864 | tf_op jit(solution)/shard_map/all_to_all | solution.py:647
  51.0 0.0 copy-done.2
  51.0 0.0 copy-done.9
  51.0 2.2 %first.1 = bf16[3072,128]{1,0:T(8,128)(2,1)S(1)} custom-call(bf16[3072,128]{1,0:T(8,128)(2,1)S(1)} %bitcast.20, bf16[4608,192]{1,0:T(8,128)(2,1)S(1)} %copy-done.2, s32[1,128]{1,0:T(1,128)S(1)} %bitcast.31, bf16[1536,128]{1,0:T(8,128)(2,1)S(1)} %get-tuple-element.10.carried), custom_call_target="tpu_custom_call" | custom-call | flops 1000000000 | bytes 6000000 | tf_op jit(solution)/shard_map/first/pallas_call | solution.py:587
  53.3 29.7 %all_to_all.31.two = bf16[64,48,128]{2,1,0:T(8,128)(2,1)S(1)} all-to-all(bf16[64,48,128]{2,1,0:T(8,128)(2,1)S(1)} %bitcast.22), channel_id=1, replica_groups=mesh['lat'=64,'batch'=8] {'lat'}, dimensions={0} | all-to-all | bytes 1572864 | tf_op jit(solution)/shard_map/all_to_all | solution.py:647
  83.0 0.0 copy-done.3
  83.0 0.0 copy-done.6
  83.0 1.2 mix.1
  84.2 0.0 all-gather.5.cloned.1.call-update
  84.2 0.0 all-gather.7.cloned.1.call-start
  84.3 28.6 %all_to_all.32 = bf16[64,48,128]{2,1,0:T(8,128)(2,1)S(1)} all-to-all(bf16[64,48,128]{2,1,0:T(8,128)(2,1)S(1)} %bitcast.25), channel_id=1, replica_groups=mesh['lat'=64,'batch'=8] {'lat'}, dimensions={0} | all-to-all | bytes 1572864 | tf_op jit(solution)/shard_map/all_to_all | solution.py:647
  112.8 8.8 %middle.1 = bf16[1536,128]{1,0:T(8,128)(2,1)S(1)} custom-call(bf16[3072,128]{1,0:T(8,128)(2,1)S(1)} %bitcast.26, bf16[64,48,128]{2,1,0:T(8,128)(2,1)S(1)} %all_to_all.30.one, bf16[64,48,128]{2,1,0:T(8,128)(2,1)S(1)} %all_to_all.31.two, bf16[4608,192]{1,0:T(8,128)(2,1)} %constant.16.clone.analysis, bf16[6144,256]{1,0:T(8,128)(2,1)} %constant.18.clone.synthesis, ...), custom_call_target="tpu_custom_call" | custom-call | flops 3000000000 | bytes 12000000 | tf_op jit(solution)/shard_map/middle/pallas_call | solution.py:599
  121.7 0.0 copy-start.1
  121.7 21.0 %all_to_all.33 = bf16[64,24,128]{2,1,0:T(8,128)(2,1)S(1)} all-to-all(bf16[64,24,128]{2,1,0:T(8,128)(2,1)S(1)} %bitcast.29), channel_id=1, replica_groups=mesh['lat'=64,'batch'=8] {'lat'}, dimensions={0} | all-to-all | bytes 786432 | tf_op jit(solution)/shard_map/all_to_all | solution.py:647
  142.7 1.3 adjoint_mix.1
  144.0 0.0 all-gather.7.cloned.1.call-update
  144.1 19.0 %all_to_all.34 = bf16[64,24,128]{2,1,0:T(8,128)(2,1)S(1)} all-to-all(bf16[64,24,128]{2,1,0:T(8,128)(2,1)S(1)} %bitcast.28), channel_id=1, replica_groups=mesh['lat'=64,'batch'=8] {'lat'}, dimensions={0} | all-to-all | bytes 786432 | tf_op jit(solution)/shard_map/all_to_all | solution.py:647
  163.1 0.0 copy-done.1
  163.1 2.9 %last.1 = bf16[2560,128]{1,0:T(8,128)(2,1)} custom-call(bf16[1536,128]{1,0:T(8,128)(2,1)S(1)} %bitcast.24, bf16[6144,256]{1,0:T(8,128)(2,1)S(1)} %copy-done.1, s32[1,128]{1,0:T(1,128)S(1)} %bitcast.33), custom_call_target="tpu_custom_call" | custom-call | flops 1000000000 | bytes 7000000 | tf_op jit(solution)/shard_map/last/pallas_call | solution.py:615
  166.0 4.9 %all-to-all-start.5 = ((bf16[64,40,128]{2,1,0:T(8,128)(2,1)}), bf16[64,40,128]{2,1,0:T(8,128)(2,1)S(1)}, u32[]{:S(2)}, u32[]{:S(2)}) async-start(bf16[64,40,128]{2,1,0:T(8,128)(2,1)} %bitcast.34), calls=%async_computation.5 | async-start | bytes 1310720 | tf_op jit(solution)/shard_map/all_to_all | solution.py:647
  170.8 0.0 all-gather.5.cloned.1.call-done
  170.9 0.0 all-gather.7.cloned.1.call-done
  170.9 0.0 copy-start
  170.9 0.0 copy-start.5
  170.9 7.4 %weight_gradient.1.weight_grads = bf16[2,2,384,384]{3,2,1,0:T(8,128)(2,1)} custom-call(bf16[8,2,384,256]{3,2,1,0:T(8,128)(2,1)} %bitcast.37, bf16[8,2,384,256]{3,2,1,0:T(8,128)(2,1)} %bitcast.38, bf16[256,256]{1,0:T(8,128)(2,1)S(1)} %copy-done.8), custom_call_target="tpu_custom_call" | custom-call | flops 5000000000 | bytes 8000000 | tf_op jit(solution)/shard_map/weight_gradient/pallas_call | solution.py:678
  178.3 10.5 %all-to-all-done.5 = bf16[64,40,128]{2,1,0:T(8,128)(2,1)S(1)} async-done(((bf16[64,40,128]{2,1,0:T(8,128)(2,1)}), bf16[64,40,128]{2,1,0:T(8,128)(2,1)S(1)}, u32[]{:S(2)}, u32[]{:S(2)}) %all-to-all-start.5) | async-done | bytes 655392 | tf_op jit(solution)/shard_map/all_to_all | solution.py:647
  188.8 0.0 copy-done.5
  188.8 1.5 gather.1
  (9 shorter events, 0.0 us)
Async XLA Ops:
  7.2 43.9 %copy-start.2 = (bf16[4608,192]{1,0:T(8,128)(2,1)S(1)}, bf16[4608,192]{1,0:T(8,128)(2,1)}, u32[]{:S(2)}) copy-start(bf16[4608,192]{1,0:T(8,128)(2,1)} %constant.17.clone.table) | copy-start | bytes 5308420
  7.2 43.9 %copy-start.9 = (s32[128]{0:T(128)S(1)}, s32[128]{0:T(128)}, u32[]{:S(2)}) copy-start(s32[128]{0:T(128)} %param.15) | copy-start | bytes 1540
  7.2 163.7 %all-gather.5.cloned.1.call-start = ((), (), s32[]{:S(2)}) async-start(), calls=%async_computation.6 | async-start | bytes 3538944 | tf_op jit(solution)/shard_map/all_gather | solution.py:694
  51.0 32.0 %copy-start.3 = (bf16[2,2,384,384]{3,2,1,0:T(8,128)(2,1)S(1)}, bf16[2,2,384,384]{3,2,1,0:T(8,128)(2,1)}, u32[]{:S(2)}) copy-start(bf16[2,2,384,384]{3,2,1,0:T(8,128)(2,1)} %weights.3) | copy-start | bytes 3538948
  51.0 32.0 %copy-start.6 = (bf16[256,256]{1,0:T(8,128)(2,1)S(1)}, bf16[256,256]{1,0:T(8,128)(2,1)}, u32[]{:S(2)}) copy-start(bf16[256,256]{1,0:T(8,128)(2,1)} %constant.23.clone.turn) | copy-start | bytes 393220
  84.2 86.7 %all-gather.7.cloned.1.call-start = ((), (), s32[]{:S(2)}) async-start(), calls=%async_computation.7 | async-start | bytes 3538944 | tf_op jit(solution)/shard_map/all_gather | solution.py:705
  112.8 29.9 %copy-start.4 = (bf16[2,2,384,384]{3,2,1,0:T(8,128)(2,1)S(1)}, bf16[2,2,384,384]{3,2,1,0:T(8,128)(2,1)}, u32[]{:S(2)}) copy-start(bf16[2,2,384,384]{3,2,1,0:T(8,128)(2,1)} %weights.3) | copy-start | bytes 3538948
  112.8 29.9 %copy-start.7 = (bf16[256,256]{1,0:T(8,128)(2,1)S(1)}, bf16[256,256]{1,0:T(8,128)(2,1)}, u32[]{:S(2)}) copy-start(bf16[256,256]{1,0:T(8,128)(2,1)} %constant.23.clone.turn) | copy-start | bytes 393220
  121.7 41.4 %copy-start.1 = (bf16[6144,256]{1,0:T(8,128)(2,1)S(1)}, bf16[6144,256]{1,0:T(8,128)(2,1)}, u32[]{:S(2)}) copy-start(bf16[6144,256]{1,0:T(8,128)(2,1)} %constant.19.clone.table) | copy-start | bytes 9437188
  163.1 7.8 %copy-start.8 = (bf16[256,256]{1,0:T(8,128)(2,1)S(1)}, bf16[256,256]{1,0:T(8,128)(2,1)}, u32[]{:S(2)}) copy-start(bf16[256,256]{1,0:T(8,128)(2,1)} %constant.23.clone.turn) | copy-start | bytes 393220
  166.0 22.8 %all-to-all-start.5 = ((bf16[64,40,128]{2,1,0:T(8,128)(2,1)}), bf16[64,40,128]{2,1,0:T(8,128)(2,1)S(1)}, u32[]{:S(2)}, u32[]{:S(2)}) async-start(bf16[64,40,128]{2,1,0:T(8,128)(2,1)} %bitcast.34), calls=%async_computation.5 | async-start | bytes 1310720 | tf_op jit(solution)/shard_map/all_to_all | solution.py:647
  170.9 17.9 %copy-start = (bf16[1,3,384,384]{3,2,1,0:T(8,128)(2,1)S(1)}, bf16[1,3,384,384]{3,2,1,0:T(8,128)(2,1)}, u32[]{:S(2)}) copy-start(bf16[1,3,384,384]{3,2,1,0:T(8,128)(2,1)} %param.13) | copy-start | bytes 2654212
  170.9 17.9 %copy-start.5 = (bf16[384,256]{1,0:T(8,128)(2,1)S(1)}, bf16[384,256]{1,0:T(8,128)(2,1)}, u32[]{:S(2)}) copy-start(bf16[384,256]{1,0:T(8,128)(2,1)} %constant.20.clone.forward_source.forward) | copy-start | bytes 589828
Sparse Core Ops, SparseCore 0:
  84.3 25.8 all-gather.4
  144.2 24.4 all-gather.6

commit v9 on v8

--- a/solution.py
+++ b/solution.py
@@ -21,8 +21,10 @@
 COEFS = 2 * ORDERS
 BLOCKS = ORDERS // 16
 SPEC_ROWS = BAND * PARTS * 2
-SENT_ROWS = 48
-COT_CUTS = (0, 12, 36, 54)
+FIRST_ROWS = 64
+SENT_ROWS = 40
+CARRIED_ROWS = 16
+COT_CUTS = (0, 28, 44, 54)
 SLOT_ROWS = SLOTS * PARTS * 2
 LAST_ROWS = 40
 HALF = GROUPS // 2
@@ -300,7 +302,7 @@
         out[...] = stage[pl.ds(0, GROUPS * SLOT_ROWS), :].astype(bf16)
     else:
         rows = stage[...].reshape(GROUPS, SENT_ROWS, 128)[:, :SLOT_ROWS]
-        more = carried[...].astype(f32).reshape(GROUPS, SLOT_ROWS, 128)
+        more = carried[...].astype(f32).reshape(GROUPS, CARRIED_ROWS, 128)
         both = jnp.concatenate([rows, more], axis=1)
         out[...] = both.reshape(GROUPS * SENT_ROWS, 128).astype(bf16)
 
@@ -364,7 +366,7 @@
         for copy in pair:
             copy.start()
     stage, stage_two, stage_three = stages.at[0], stages.at[1], stages.at[2]
-    spots = ((stage, SPEC_ROWS, SENT_ROWS), (stage_two, 0, SLOT_ROWS), (stage_three, 0, SLOT_ROWS))
+    spots = ((stage, SPEC_ROWS, FIRST_ROWS), (stage_two, 0, CARRIED_ROWS), (stage_three, 0, CARRIED_ROWS))
     for i in range(BAND):
         if i == 0:
             fetch.wait()
@@ -374,7 +376,7 @@
             rows = slice(q * GROUPS, (q + 1) * GROUPS)
             at = (i * PARTS + q) * 2
             for h in range(2):
-                stage[pl.ds(at + h, GROUPS, stride=SENT_ROWS), :] = spectra[
+                stage[pl.ds(at + h, GROUPS, stride=FIRST_ROWS), :] = spectra[
                     rows, 128 * h : 128 * (h + 1)
                 ]
         copies[i][1].wait()
@@ -387,10 +389,10 @@
                 place[pl.ds(base + at, GROUPS, stride=stride), :] = turned[
                     rows, 128 * h : 128 * (h + 1)
                 ]
-    for row in range(COT_CUTS[3] - COT_CUTS[2], SLOT_ROWS):
-        stage_three[pl.ds(row, GROUPS, stride=SLOT_ROWS), :] = jnp.zeros((GROUPS, 128), f32)
+    for row in range(COT_CUTS[3] - COT_CUTS[2], CARRIED_ROWS):
+        stage_three[pl.ds(row, GROUPS, stride=CARRIED_ROWS), :] = jnp.zeros((GROUPS, 128), f32)
     out[...] = stage[...].astype(bf16)
-    short = GROUPS * SLOT_ROWS
+    short = GROUPS * CARRIED_ROWS
     cot_two[...] = stage_two[pl.ds(0, short), :].astype(bf16)
     cot_three[...] = stage_three[pl.ds(0, short), :].astype(bf16)
 
@@ -403,7 +405,7 @@
         [
             jnp.concatenate(
                 [
-                    stage_in[pl.ds((i * PARTS + q) * 2 + h, GROUPS, stride=SENT_ROWS), :]
+                    stage_in[pl.ds((i * PARTS + q) * 2 + h, GROUPS, stride=FIRST_ROWS), :]
                     for i in range(BAND)
                 ],
                 axis=0,
@@ -430,8 +432,8 @@
     copies_s = table_copies(synthesis, table_s, sems_s, STEPS)
     copies = table_copies(analysis, table, sems, STARTS)
     fetches = (
-        pltpu.make_async_copy(one.at[:, pl.ds(32, 16), :], rows_one, row_sems.at[0]),
-        pltpu.make_async_copy(two.at[:, pl.ds(16, 32), :], rows_two, row_sems.at[1]),
+        pltpu.make_async_copy(one.at[:, pl.ds(32, 32), :], rows_one, row_sems.at[0]),
+        pltpu.make_async_copy(two, rows_two, row_sems.at[1]),
         pltpu.make_async_copy(inverse_source, inverse, row_sems.at[2]),
         pltpu.make_async_copy(turned_source, inverse_t, row_sems.at[3]),
     )
@@ -441,9 +443,9 @@
     synth = synthesise(tiles, table_s, lambda t: copies_s[t].wait())
     for fetch in fetches:
         fetch.wait()
-    stage_one[...] = rows_one[...].astype(f32).reshape(GROUPS * 16, 128)
-    stage_two[...] = rows_two[...].astype(f32).reshape(GROUPS * 32, 128)
-    spots = ((stage_one, SPEC_ROWS - 32, 16), (stage_two, 8, 32), (stage, SLOT_ROWS, SENT_ROWS))
+    stage_one[...] = rows_one[...].astype(f32).reshape(GROUPS * 32, 128)
+    stage_two[...] = rows_two[...].astype(f32)
+    spots = ((stage_one, SPEC_ROWS - 32, 32), (stage_two, SLOT_ROWS, SENT_ROWS), (stage, SLOT_ROWS, SENT_ROWS))
 
     def cot_rows(i, q, h):
         which, at = cot_place(i, q, h)
@@ -573,11 +575,11 @@
     cycle = pltpu.VMEM((BAND, LONS, CHANNELS), bf16)
     return call(
         spread_kernel,
-        [message(SENT_ROWS), message(SLOT_ROWS), message(SLOT_ROWS)],
+        [message(FIRST_ROWS), message(CARRIED_ROWS), message(CARRIED_ROWS)],
         [ANY, ANY, ANY],
         [
             cycle, cycle, pltpu.VMEM((LONS, COEFS), bf16),
-            pltpu.VMEM((3, GROUPS * SENT_ROWS, 128), f32), sems(2 * BAND + 1),
+            pltpu.VMEM((3, GROUPS * FIRST_ROWS, 128), f32), sems(2 * BAND + 1),
         ],
         3 * 10**8, 4 * 10**6, "spread",
     )(in_hbm(fields), in_hbm(cotangent), in_hbm(forward))
@@ -588,7 +590,7 @@
         first_kernel,
         message(SENT_ROWS),
         [VMEM, VMEM, VMEM, VMEM],
-        [stage_of(SENT_ROWS), stage_of(SENT_ROWS)],
+        [stage_of(FIRST_ROWS), stage_of(SENT_ROWS)],
         10**9, 6 * 10**6, "first",
     )(received, weighted, degrees, carried)
 
@@ -602,8 +604,8 @@
         [VMEM, ANY, ANY, ANY, ANY, VMEM, ANY, ANY],
         [
             pltpu.VMEM((LONS, COEFS), bf16), pltpu.VMEM((COEFS, LONS), bf16),
-            pltpu.VMEM((GROUPS, 16, 128), bf16), pltpu.VMEM((GROUPS, 32, 128), bf16),
-            stage_of(16), stage_of(32), stage_of(SENT_ROWS),
+            pltpu.VMEM((GROUPS, 32, 128), bf16), pltpu.VMEM((GROUPS * SENT_ROWS, 128), bf16),
+            stage_of(32), stage_of(SENT_ROWS), stage_of(SENT_ROWS),
             TABLE, TABLE_S, sems(4), sems(BLOCKS), sems(BLOCKS),
         ],
         3 * 10**9, 12 * 10**6, "middle",
@@ -693,10 +695,9 @@
     filtered, coeffs = mix(False, two, weights, table["turn"], cot_three)
     all_coeffs = lax.all_gather(coeffs, "batch", axis=0)
     three = exchange(filtered)
-    as_sent = (GROUPS, SENT_ROWS, 128)
     four = exchange(
         middle(
-            three, one.reshape(as_sent), two.reshape(as_sent), table["analysis"],
+            three, one.reshape(GROUPS, FIRST_ROWS, 128), two, table["analysis"],
             table["synthesis"], degrees,
             table["inverse"], table["inverse_t"],
         )

time: 197 us -> 200 us (1.015)
  no operation moved by 1% of the time
where the time goes in v9:
time: 200 us; the launch traced here: 199 us
  blocking collectives  140 us (70%)
  Pallas kernels  29.5 us (15%)
  between operations  14.1 us (7%)
  waiting for transfers between devices  11 us (6%)
  starting transfers between devices  4.94 us (2%)
    all_to_all x5, blocking collectives, exchange(): lax.all_to_all(rows.reshape(GROUPS, count, 128), 'lat', split_axis=0, con...  140 us
    all_to_all x1, waiting for transfers between devices, exchange(): lax.all_to_all(rows.reshape(GROUPS, count, 128), 'lat', split_axis=0, con...  10.9 us
    pallas_call x1, Pallas kernels, middle(): call(middle_kernel, message(SLOT_ROWS), [VMEM, ANY, ANY, ANY, ANY, VMEM,...  8.83 us
    pallas_call x1, Pallas kernels, weight_gradient(): call(gradient_kernel, jax.ShapeDtypeStruct((SLOTS, 2, CHANNELS, CHANNELS)...  7.38 us
    all_to_all x1, starting transfers between devices, exchange(): lax.all_to_all(rows.reshape(GROUPS, count, 128), 'lat', split_axis=0, con...  4.86 us
    pallas_call x1, Pallas kernels, spread(): call(spread_kernel, [message(FIRST_ROWS), message(CARRIED_ROWS), message(...  4.06 us
  transfers between devices with their start and end apart: 3, of which 1 were waited for; matrix products, arithmetic and copies ran while one was open for 0% of the time, Pallas kernels for 10%

profile of v9, /device:TPU:6, one launch (start us, length us, event | category | flops | bytes accessed | tf_op | source)
XLA Modules:
  0.0 199.4 jit_solution(16403547691425720889)
XLA Ops:
  7.2 0.0 copy-start.2
  7.2 0.0 copy-start.9
  7.2 0.0 all-gather.5.cloned.1.call-start
  7.2 4.1 %spread.1 = (bf16[4096,128]{1,0:T(8,128)(2,1)S(1)}, bf16[1024,128]{1,0:T(8,128)(2,1)S(1)}, bf16[1024,128]{1,0:T(8,128)(2,1)S(1)}) custom-call(bf16[3,384,384]{2,1,0:T(8,128)(2,1)} %bitcast.36, bf16[3,384,384]{2,1,0:T(8,128)(2,1)} %bitcast.19, bf16[384,256]{1,0:T(8,128)(2,1)} %constant.20.clone.forward_source.forward), custom_call_target="tpu_custom_call" | custom-call | flops 300000000 | bytes 4000000 | tf_op jit(solution)/shard_map/spread/pallas_call | solution.py:576
  11.3 46.2 %all_to_all.30.one = bf16[64,64,128]{2,1,0:T(8,128)(2,1)S(1)} all-to-all(bf16[64,64,128]{2,1,0:T(8,128)(2,1)S(1)} %bitcast.26), channel_id=1, replica_groups=mesh['lat'=64,'batch'=8] {'lat'}, dimensions={0} | all-to-all | bytes 2097152 | tf_op jit(solution)/shard_map/all_to_all | solution.py:649
  57.5 0.0 copy-done.2
  57.5 0.0 copy-done.9
  57.5 2.5 %first.1 = bf16[2560,128]{1,0:T(8,128)(2,1)S(1)} custom-call(bf16[4096,128]{1,0:T(8,128)(2,1)S(1)} %bitcast.18, bf16[4608,192]{1,0:T(8,128)(2,1)S(1)} %copy-done.2, s32[1,128]{1,0:T(1,128)S(1)} %bitcast.32, bf16[1024,128]{1,0:T(8,128)(2,1)S(1)} %get-tuple-element.10.carried), custom_call_target="tpu_custom_call" | custom-call | flops 1000000000 | bytes 6000000 | tf_op jit(solution)/shard_map/first/pallas_call | solution.py:589
  60.0 27.3 %all_to_all.31 = bf16[64,40,128]{2,1,0:T(8,128)(2,1)S(1)} all-to-all(bf16[64,40,128]{2,1,0:T(8,128)(2,1)S(1)} %bitcast.21), channel_id=1, replica_groups=mesh['lat'=64,'batch'=8] {'lat'}, dimensions={0} | all-to-all | bytes 1310720 | tf_op jit(solution)/shard_map/all_to_all | solution.py:649
  87.4 0.0 copy-done.3
  87.4 0.0 copy-done.6
  87.4 1.0 mix.1
  88.4 0.0 all-gather.5.cloned.1.call-update
  88.4 0.0 all-gather.7.cloned.1.call-start
  88.5 26.0 %all_to_all.32 = bf16[64,40,128]{2,1,0:T(8,128)(2,1)S(1)} all-to-all(bf16[64,40,128]{2,1,0:T(8,128)(2,1)S(1)} %bitcast.27), channel_id=1, replica_groups=mesh['lat'=64,'batch'=8] {'lat'}, dimensions={0} | all-to-all | bytes 1310720 | tf_op jit(solution)/shard_map/all_to_all | solution.py:649
  114.4 8.8 %middle.1 = bf16[1536,128]{1,0:T(8,128)(2,1)S(1)} custom-call(bf16[2560,128]{1,0:T(8,128)(2,1)S(1)} %bitcast.28, bf16[64,64,128]{2,1,0:T(8,128)(2,1)S(1)} %all_to_all.30.one, bf16[2560,128]{1,0:T(8,128)(2,1)S(1)} %bitcast.23, bf16[4608,192]{1,0:T(8,128)(2,1)} %constant.16.clone.analysis, bf16[6144,256]{1,0:T(8,128)(2,1)} %constant.18.clone.synthesis, ...), custom_call_target="tpu_custom_call" | custom-call | flops 3000000000 | bytes 12000000 | tf_op jit(solution)/shard_map/middle/pallas_call | solution.py:601
  123.3 0.0 copy-start.1
  123.3 21.0 %all_to_all.33 = bf16[64,24,128]{2,1,0:T(8,128)(2,1)S(1)} all-to-all(bf16[64,24,128]{2,1,0:T(8,128)(2,1)S(1)} %bitcast.30), channel_id=1, replica_groups=mesh['lat'=64,'batch'=8] {'lat'}, dimensions={0} | all-to-all | bytes 786432 | tf_op jit(solution)/shard_map/all_to_all | solution.py:649
  144.3 0.0 copy-done.4
  144.3 1.3 adjoint_mix.1
  145.6 0.0 all-gather.7.cloned.1.call-update
  145.6 19.3 %all_to_all.34 = bf16[64,24,128]{2,1,0:T(8,128)(2,1)S(1)} all-to-all(bf16[64,24,128]{2,1,0:T(8,128)(2,1)S(1)} %bitcast.29), channel_id=1, replica_groups=mesh['lat'=64,'batch'=8] {'lat'}, dimensions={0} | all-to-all | bytes 786432 | tf_op jit(solution)/shard_map/all_to_all | solution.py:649
  164.9 2.9 %last.1 = bf16[2560,128]{1,0:T(8,128)(2,1)} custom-call(bf16[1536,128]{1,0:T(8,128)(2,1)S(1)} %bitcast.25, bf16[6144,256]{1,0:T(8,128)(2,1)S(1)} %copy-done.1, s32[1,128]{1,0:T(1,128)S(1)} %bitcast.34), custom_call_target="tpu_custom_call" | custom-call | flops 1000000000 | bytes 7000000 | tf_op jit(solution)/shard_map/last/pallas_call | solution.py:617
  167.8 4.9 %all-to-all-start.5 = ((bf16[64,40,128]{2,1,0:T(8,128)(2,1)}), bf16[64,40,128]{2,1,0:T(8,128)(2,1)S(1)}, u32[]{:S(2)}, u32[]{:S(2)}) async-start(bf16[64,40,128]{2,1,0:T(8,128)(2,1)} %bitcast.35), calls=%async_computation.5 | async-start | bytes 1310720 | tf_op jit(solution)/shard_map/all_to_all | solution.py:649
  172.7 0.0 all-gather.5.cloned.1.call-done
  172.7 0.0 all-gather.7.cloned.1.call-done
  172.7 0.0 copy-start
  172.8 0.0 copy-start.5
  172.8 7.4 %weight_gradient.1.weight_grads = bf16[2,2,384,384]{3,2,1,0:T(8,128)(2,1)} custom-call(bf16[8,2,384,256]{3,2,1,0:T(8,128)(2,1)} %bitcast.38, bf16[8,2,384,256]{3,2,1,0:T(8,128)(2,1)} %bitcast.39, bf16[256,256]{1,0:T(8,128)(2,1)S(1)} %copy-done.8), custom_call_target="tpu_custom_call" | custom-call | flops 5000000000 | bytes 8000000 | tf_op jit(solution)/shard_map/weight_gradient/pallas_call | solution.py:680
  180.2 10.9 %all-to-all-done.5 = bf16[64,40,128]{2,1,0:T(8,128)(2,1)S(1)} async-done(((bf16[64,40,128]{2,1,0:T(8,128)(2,1)}), bf16[64,40,128]{2,1,0:T(8,128)(2,1)S(1)}, u32[]{:S(2)}, u32[]{:S(2)}) %all-to-all-start.5) | async-done | bytes 655392 | tf_op jit(solution)/shard_map/all_to_all | solution.py:649
  191.1 0.0 copy-done
  191.1 1.5 gather.1
  (9 shorter events, 0.0 us)
Async XLA Ops:
  7.2 50.3 %copy-start.2 = (bf16[4608,192]{1,0:T(8,128)(2,1)S(1)}, bf16[4608,192]{1,0:T(8,128)(2,1)}, u32[]{:S(2)}) copy-start(bf16[4608,192]{1,0:T(8,128)(2,1)} %constant.17.clone.table) | copy-start | bytes 5308420
  7.2 50.3 %copy-start.9 = (s32[128]{0:T(128)S(1)}, s32[128]{0:T(128)}, u32[]{:S(2)}) copy-start(s32[128]{0:T(128)} %param.15) | copy-start | bytes 1540
  7.2 165.5 %all-gather.5.cloned.1.call-start = ((), (), s32[]{:S(2)}) async-start(), calls=%async_computation.6 | async-start | bytes 3538944 | tf_op jit(solution)/shard_map/all_gather | solution.py:696
  57.5 29.9 %copy-start.3 = (bf16[2,2,384,384]{3,2,1,0:T(8,128)(2,1)S(1)}, bf16[2,2,384,384]{3,2,1,0:T(8,128)(2,1)}, u32[]{:S(2)}) copy-start(bf16[2,2,384,384]{3,2,1,0:T(8,128)(2,1)} %weights.3) | copy-start | bytes 3538948
  57.5 29.9 %copy-start.6 = (bf16[256,256]{1,0:T(8,128)(2,1)S(1)}, bf16[256,256]{1,0:T(8,128)(2,1)}, u32[]{:S(2)}) copy-start(bf16[256,256]{1,0:T(8,128)(2,1)} %constant.23.clone.turn) | copy-start | bytes 393220
  88.4 84.3 %all-gather.7.cloned.1.call-start = ((), (), s32[]{:S(2)}) async-start(), calls=%async_computation.7 | async-start | bytes 3538944 | tf_op jit(solution)/shard_map/all_gather | solution.py:706
  114.4 29.8 %copy-start.4 = (bf16[2,2,384,384]{3,2,1,0:T(8,128)(2,1)S(1)}, bf16[2,2,384,384]{3,2,1,0:T(8,128)(2,1)}, u32[]{:S(2)}) copy-start(bf16[2,2,384,384]{3,2,1,0:T(8,128)(2,1)} %weights.3) | copy-start | bytes 3538948
  114.4 29.8 %copy-start.7 = (bf16[256,256]{1,0:T(8,128)(2,1)S(1)}, bf16[256,256]{1,0:T(8,128)(2,1)}, u32[]{:S(2)}) copy-start(bf16[256,256]{1,0:T(8,128)(2,1)} %constant.23.clone.turn) | copy-start | bytes 393220
  123.3 41.7 %copy-start.1 = (bf16[6144,256]{1,0:T(8,128)(2,1)S(1)}, bf16[6144,256]{1,0:T(8,128)(2,1)}, u32[]{:S(2)}) copy-start(bf16[6144,256]{1,0:T(8,128)(2,1)} %constant.19.clone.table) | copy-start | bytes 9437188
  164.9 7.8 %copy-start.8 = (bf16[256,256]{1,0:T(8,128)(2,1)S(1)}, bf16[256,256]{1,0:T(8,128)(2,1)}, u32[]{:S(2)}) copy-start(bf16[256,256]{1,0:T(8,128)(2,1)} %constant.23.clone.turn) | copy-start | bytes 393220
  167.8 23.3 %all-to-all-start.5 = ((bf16[64,40,128]{2,1,0:T(8,128)(2,1)}), bf16[64,40,128]{2,1,0:T(8,128)(2,1)S(1)}, u32[]{:S(2)}, u32[]{:S(2)}) async-start(bf16[64,40,128]{2,1,0:T(8,128)(2,1)} %bitcast.35), calls=%async_computation.5 | async-start | bytes 1310720 | tf_op jit(solution)/shard_map/all_to_all | solution.py:649
  172.7 18.3 %copy-start = (bf16[1,3,384,384]{3,2,1,0:T(8,128)(2,1)S(1)}, bf16[1,3,384,384]{3,2,1,0:T(8,128)(2,1)}, u32[]{:S(2)}) copy-start(bf16[1,3,384,384]{3,2,1,0:T(8,128)(2,1)} %param.13) | copy-start | bytes 2654212
  172.8 18.3 %copy-start.5 = (bf16[384,256]{1,0:T(8,128)(2,1)S(1)}, bf16[384,256]{1,0:T(8,128)(2,1)}, u32[]{:S(2)}) copy-start(bf16[384,256]{1,0:T(8,128)(2,1)} %constant.20.clone.forward_source.forward) | copy-start | bytes 589828
Sparse Core Ops, SparseCore 0:
  88.5 25.3 all-gather.4
  145.7 24.4 all-gather.6

commit v10 on v8

--- a/solution.py
+++ b/solution.py
@@ -347,28 +347,29 @@
     return which, row - COT_CUTS[which]
 
 
-def spread_kernel(
-    fields, cotangent, forward_source, out, cot_two, cot_three, field, cot, forward, stages, sems
-):
-    copies = []
-    fetch = pltpu.make_async_copy(forward_source, forward, sems.at[2 * BAND])
-    fetch.start()
+def put_cotangent(turned, i, parts, wanted, spots):
+    for q in parts:
+        rows = slice(q * GROUPS, (q + 1) * GROUPS)
+        for h in range(3):
+            which, at = cot_place(i, q, h)
+            if which in wanted:
+                place, base, stride = spots[which]
+                place[pl.ds(base + at, GROUPS, stride=stride), :] = turned[
+                    rows, 128 * h : 128 * (h + 1)
+                ]
+
+
+def spread_kernel(fields, cotangent, forward_source, out, field, cot, forward, stage, sems):
+    copies = [
+        pltpu.make_async_copy(forward_source, forward, sems.at[BAND]),
+        *[pltpu.make_async_copy(fields.at[i], field.at[i], sems.at[i]) for i in range(BAND)],
+    ]
+    fetch = pltpu.make_async_copy(cotangent.at[0], cot, sems.at[BAND + 1])
+    for copy in (*copies, fetch):
+        copy.start()
+    copies[0].wait()
     for i in range(BAND):
-        copies.append(
-            (
-                pltpu.make_async_copy(fields.at[i], field.at[i], sems.at[2 * i]),
-                pltpu.make_async_copy(cotangent.at[i], cot.at[i], sems.at[2 * i + 1]),
-            )
-        )
-    for pair in copies:
-        for copy in pair:
-            copy.start()
-    stage, stage_two, stage_three = stages.at[0], stages.at[1], stages.at[2]
-    spots = ((stage, SPEC_ROWS, SENT_ROWS), (stage_two, 0, SLOT_ROWS), (stage_three, 0, SLOT_ROWS))
-    for i in range(BAND):
-        if i == 0:
-            fetch.wait()
-        copies[i][0].wait()
+        copies[i + 1].wait()
         spectra = dot(field[i], forward[...], TN)
         for q in range(PARTS):
             rows = slice(q * GROUPS, (q + 1) * GROUPS)
@@ -377,27 +378,34 @@
                 stage[pl.ds(at + h, GROUPS, stride=SENT_ROWS), :] = spectra[
                     rows, 128 * h : 128 * (h + 1)
                 ]
-        copies[i][1].wait()
+    fetch.wait()
+    turned = jnp.transpose(cot[:, : 4 * GROUPS].astype(f32))
+    put_cotangent(turned, 0, range(4), (0,), ((stage, SPEC_ROWS, SENT_ROWS),))
+    out[...] = stage[...].astype(bf16)
+
+
+def spread_rest_kernel(cotangent, early, cot_two, cot_three, cot, stages, sems):
+    copies = [pltpu.make_async_copy(cotangent.at[i], cot.at[i], sems.at[i]) for i in range(BAND)]
+    for copy in copies:
+        copy.start()
+    two, three = stages.at[0], stages.at[1]
+    for i in range(BAND):
+        copies[i].wait()
         turned = jnp.transpose(cot[i].astype(f32))
-        for q in range(PARTS):
-            rows = slice(q * GROUPS, (q + 1) * GROUPS)
-            for h in range(3):
-                which, at = cot_place(i, q, h)
-                place, base, stride = spots[which]
-                place[pl.ds(base + at, GROUPS, stride=stride), :] = turned[
-                    rows, 128 * h : 128 * (h + 1)
-                ]
+        put_cotangent(
+            turned, i, range(PARTS), (1, 2), (None, (two, 0, SLOT_ROWS), (three, 0, SLOT_ROWS))
+        )
     for row in range(COT_CUTS[3] - COT_CUTS[2], SLOT_ROWS):
-        stage_three[pl.ds(row, GROUPS, stride=SLOT_ROWS), :] = jnp.zeros((GROUPS, 128), f32)
-    out[...] = stage[...].astype(bf16)
-    short = GROUPS * SLOT_ROWS
-    cot_two[...] = stage_two[pl.ds(0, short), :].astype(bf16)
-    cot_three[...] = stage_three[pl.ds(0, short), :].astype(bf16)
+        three[pl.ds(row, GROUPS, stride=SLOT_ROWS), :] = jnp.zeros((GROUPS, 128), f32)
+    cot_two[...] = two[...].astype(bf16)
+    cot_three[...] = three[...].astype(bf16)
 
 
 def first_kernel(
-    received, table, degrees, carried, out, stage_in, stage
+    received, table, degrees, carried_source, out, stage_in, stage, carried, sem
 ):
+    fetch = pltpu.make_async_copy(carried_source, carried, sem)
+    fetch.start()
     stage_in[...] = received[...].astype(f32)
     parts = [
         [
@@ -413,6 +421,7 @@
         for q in range(PARTS)
     ]
     sums = analyse(parts, reversal(), table, lambda t: None)
+    fetch.wait()
     slot_rows_out(sums, degrees, carried, stage, out)
 
 
@@ -570,27 +579,42 @@
 
 
 def spread(fields, cotangent, forward):
-    cycle = pltpu.VMEM((BAND, LONS, CHANNELS), bf16)
     return call(
         spread_kernel,
-        [message(SENT_ROWS), message(SLOT_ROWS), message(SLOT_ROWS)],
+        message(SENT_ROWS),
         [ANY, ANY, ANY],
         [
-            cycle, cycle, pltpu.VMEM((LONS, COEFS), bf16),
-            pltpu.VMEM((3, GROUPS * SENT_ROWS, 128), f32), sems(2 * BAND + 1),
+            pltpu.VMEM((BAND, LONS, CHANNELS), bf16), pltpu.VMEM((LONS, CHANNELS), bf16),
+            pltpu.VMEM((LONS, COEFS), bf16), stage_of(SENT_ROWS), sems(BAND + 2),
         ],
-        3 * 10**8, 4 * 10**6, "spread",
+        3 * 10**8, 3 * 10**6, "spread",
     )(in_hbm(fields), in_hbm(cotangent), in_hbm(forward))
+
+
+def spread_rest(cotangent, early):
+    return call(
+        spread_rest_kernel,
+        [pltpu.HBM((GROUPS * SLOT_ROWS, 128), bf16)] * 2,
+        [ANY, ANY],
+        [
+            pltpu.VMEM((BAND, LONS, CHANNELS), bf16),
+            pltpu.VMEM((2, GROUPS * SLOT_ROWS, 128), f32), sems(BAND),
+        ],
+        10**7, 3 * 10**6, "spread_rest",
+    )(in_hbm(cotangent), early)
 
 
 def first(received, weighted, degrees, carried):
     return call(
         first_kernel,
         message(SENT_ROWS),
-        [VMEM, VMEM, VMEM, VMEM],
-        [stage_of(SENT_ROWS), stage_of(SENT_ROWS)],
+        [VMEM, VMEM, VMEM, ANY],
+        [
+            stage_of(SENT_ROWS), stage_of(SENT_ROWS),
+            pltpu.VMEM((GROUPS * SLOT_ROWS, 128), bf16), pltpu.SemaphoreType.DMA,
+        ],
         10**9, 6 * 10**6, "first",
-    )(received, weighted, degrees, carried)
+    )(received, weighted, degrees, in_hbm(carried))
 
 
 def middle(
@@ -687,7 +711,8 @@
 def local(fields, cotangent, weights, degree_of):
     table = {k: jnp.asarray(v) for k, v in constants().items()}
     degrees = degree_of[None, :]
-    sent, cot_two, cot_three = spread(fields[0], cotangent[0], table["forward"])
+    sent = spread(fields[0], cotangent[0], table["forward"])
+    cot_two, cot_three = spread_rest(cotangent[0], sent)
     one = exchange(sent)
     two = exchange(first(one, table["weighted"], degrees, cot_two))
     filtered, coeffs = mix(False, two, weights, table["turn"], cot_three)

time: 197 us -> 199 us (1.010)
  blocking collectives: 139 us -> 98.3 us
  waiting for transfers between devices: 10.6 us -> 32.3 us
  starting transfers between devices: 4.94 us -> 21.5 us
  Pallas kernels: 28.5 us -> 32.2 us
    all_to_all x5 -> x4, blocking collectives: 139 us -> 98.3 us  [exchange(): lax.all_to_all(rows.reshape(GROUPS, count, 128), 'lat', split_axis=0, con...]
    all_to_all x1 -> x2, waiting for transfers between devices: 10.5 us -> 32.2 us  [exchange(): lax.all_to_all(rows.reshape(GROUPS, count, 128), 'lat', split_axis=0, con...]
    all_to_all x1 -> x2, starting transfers between devices: 4.86 us -> 21.5 us  [exchange(): lax.all_to_all(rows.reshape(GROUPS, count, 128), 'lat', split_axis=0, con...]
    pallas_call x2 -> x3, Pallas kernels: 5.43 us -> 9.15 us  [the longest x1 3.57 us: spread(): call(spread_kernel, message(SENT_ROWS), [ANY, ANY, ANY], [pltpu.VMEM((BAN...]
  transfers between devices with their start and end apart: 3 -> 4, of which waited for: 1 -> 2; matrix products, arithmetic and copies ran while one was open for 0% -> 0% of each run, Pallas kernels for 10% -> 12%
where the time goes in v10:
time: 199 us
  blocking collectives  98.3 us (49%)
  waiting for transfers between devices  32.3 us (16%)
  Pallas kernels  32.2 us (16%)
  starting transfers between devices  21.5 us (11%)
  between operations  14.2 us (7%)
    all_to_all x4, blocking collectives, exchange(): lax.all_to_all(rows.reshape(GROUPS, count, 128), 'lat', split_axis=0, con...  98.3 us
    all_to_all x2, waiting for transfers between devices, exchange(): lax.all_to_all(rows.reshape(GROUPS, count, 128), 'lat', split_axis=0, con...  32.2 us
    all_to_all x2, starting transfers between devices, exchange(): lax.all_to_all(rows.reshape(GROUPS, count, 128), 'lat', split_axis=0, con...  21.5 us
    pallas_call x1, Pallas kernels, middle(): call(middle_kernel, message(SLOT_ROWS), [VMEM, ANY, ANY, ANY, ANY, VMEM,...  8.86 us
    pallas_call x1, Pallas kernels, weight_gradient(): call(gradient_kernel, jax.ShapeDtypeStruct((SLOTS, 2, CHANNELS, CHANNELS)...  7.37 us
  transfers between devices with their start and end apart: 4, of which 2 were waited for; matrix products, arithmetic and copies ran while one was open for 0% of the time, Pallas kernels for 12%

profile of v10, /device:TPU:6, one launch (start us, length us, event | category | flops | bytes accessed | tf_op | source)
XLA Modules:
  0.0 198.6 jit_solution(15068161758497361319)
XLA Ops:
  7.2 0.0 copy-start.2
  7.2 0.0 copy-start.10
  7.2 3.6 %spread.1.early = bf16[3072,128]{1,0:T(8,128)(2,1)} custom-call(bf16[3,384,384]{2,1,0:T(8,128)(2,1)} %bitcast.35, bf16[3,384,384]{2,1,0:T(8,128)(2,1)} %bitcast.18, bf16[384,256]{1,0:T(8,128)(2,1)} %constant.20.clone.forward_source.forward), custom_call_target="tpu_custom_call" | custom-call | flops 300000000 | bytes 3000000 | tf_op jit(solution)/shard_map/spread/pallas_call | solution.py:582
  10.8 16.6 %all-to-all-start = ((bf16[64,48,128]{2,1,0:T(8,128)(2,1)}), bf16[64,48,128]{2,1,0:T(8,128)(2,1)S(1)}, u32[]{:S(2)}, u32[]{:S(2)}) async-start(bf16[64,48,128]{2,1,0:T(8,128)(2,1)} %bitcast.2), calls=%async_computation | async-start | bytes 1572864 | tf_op jit(solution)/shard_map/all_to_all | solution.py:671
  27.4 0.0 all-gather.5.cloned.1.call-start
  27.4 2.4 %spread_rest.1 = (bf16[1536,128]{1,0:T(8,128)(2,1)}, bf16[1536,128]{1,0:T(8,128)(2,1)}) custom-call(bf16[3,384,384]{2,1,0:T(8,128)(2,1)} %bitcast.19, bf16[3072,128]{1,0:T(8,128)(2,1)} %spread.1.early), custom_call_target="tpu_custom_call" | custom-call | flops 10000000 | bytes 3000000 | tf_op jit(solution)/shard_map/spread_rest/pallas_call | solution.py:595
  29.8 0.0 copy-start.6
  29.8 21.7 %all-to-all-done.one = bf16[64,48,128]{2,1,0:T(8,128)(2,1)S(1)} async-done(((bf16[64,48,128]{2,1,0:T(8,128)(2,1)}), bf16[64,48,128]{2,1,0:T(8,128)(2,1)S(1)}, u32[]{:S(2)}, u32[]{:S(2)}) %all-to-all-start) | async-done | bytes 786464 | tf_op jit(solution)/shard_map/all_to_all | solution.py:671
  51.6 3.2 %first.1 = bf16[3072,128]{1,0:T(8,128)(2,1)S(1)} custom-call(bf16[3072,128]{1,0:T(8,128)(2,1)S(1)} %bitcast.21, bf16[4608,192]{1,0:T(8,128)(2,1)S(1)} %copy-done.2, s32[1,128]{1,0:T(1,128)S(1)} %bitcast.31, bf16[1536,128]{1,0:T(8,128)(2,1)} %get-tuple-element.8.carried_source), custom_call_target="tpu_custom_call" | custom-call | flops 1000000000 | bytes 6000000 | tf_op jit(solution)/shard_map/first/pallas_call | solution.py:608
  54.8 29.7 %all_to_all.30.two = bf16[64,48,128]{2,1,0:T(8,128)(2,1)S(1)} all-to-all(bf16[64,48,128]{2,1,0:T(8,128)(2,1)S(1)} %bitcast.23), channel_id=1, replica_groups=mesh['lat'=64,'batch'=8] {'lat'}, dimensions={0} | all-to-all | bytes 1572864 | tf_op jit(solution)/shard_map/all_to_all | solution.py:671
  84.5 0.0 copy-done.6
  84.5 0.0 copy-done.7
  84.5 1.2 mix.1
  85.7 0.0 all-gather.5.cloned.1.call-update
  85.7 0.0 all-gather.7.cloned.1.call-start
  85.7 28.6 %all_to_all.31 = bf16[64,48,128]{2,1,0:T(8,128)(2,1)S(1)} all-to-all(bf16[64,48,128]{2,1,0:T(8,128)(2,1)S(1)} %bitcast.26), channel_id=1, replica_groups=mesh['lat'=64,'batch'=8] {'lat'}, dimensions={0} | all-to-all | bytes 1572864 | tf_op jit(solution)/shard_map/all_to_all | solution.py:671
  114.4 8.9 %middle.1 = bf16[1536,128]{1,0:T(8,128)(2,1)S(1)} custom-call(bf16[3072,128]{1,0:T(8,128)(2,1)S(1)} %bitcast.27, bf16[64,48,128]{2,1,0:T(8,128)(2,1)S(1)} %all-to-all-done.one, bf16[64,48,128]{2,1,0:T(8,128)(2,1)S(1)} %all_to_all.30.two, bf16[4608,192]{1,0:T(8,128)(2,1)} %constant.16.clone.analysis, bf16[6144,256]{1,0:T(8,128)(2,1)} %constant.18.clone.synthesis, ...), custom_call_target="tpu_custom_call" | custom-call | flops 3000000000 | bytes 12000000 | tf_op jit(solution)/shard_map/middle/pallas_call | solution.py:623
  123.2 0.0 copy-start.1
  123.2 21.0 %all_to_all.32 = bf16[64,24,128]{2,1,0:T(8,128)(2,1)S(1)} all-to-all(bf16[64,24,128]{2,1,0:T(8,128)(2,1)S(1)} %bitcast.29), channel_id=1, replica_groups=mesh['lat'=64,'batch'=8] {'lat'}, dimensions={0} | all-to-all | bytes 786432 | tf_op jit(solution)/shard_map/all_to_all | solution.py:671
  144.2 0.0 copy-done.8
  144.2 1.3 adjoint_mix.1
  145.5 0.0 all-gather.7.cloned.1.call-update
  145.6 19.0 %all_to_all.33 = bf16[64,24,128]{2,1,0:T(8,128)(2,1)S(1)} all-to-all(bf16[64,24,128]{2,1,0:T(8,128)(2,1)S(1)} %bitcast.28), channel_id=1, replica_groups=mesh['lat'=64,'batch'=8] {'lat'}, dimensions={0} | all-to-all | bytes 786432 | tf_op jit(solution)/shard_map/all_to_all | solution.py:671
  164.6 2.9 %last.1 = bf16[2560,128]{1,0:T(8,128)(2,1)} custom-call(bf16[1536,128]{1,0:T(8,128)(2,1)S(1)} %bitcast.25, bf16[6144,256]{1,0:T(8,128)(2,1)S(1)} %copy-done.1, s32[1,128]{1,0:T(1,128)S(1)} %bitcast.33), custom_call_target="tpu_custom_call" | custom-call | flops 1000000000 | bytes 7000000 | tf_op jit(solution)/shard_map/last/pallas_call | solution.py:639
  167.5 4.9 %all-to-all-start.5 = ((bf16[64,40,128]{2,1,0:T(8,128)(2,1)}), bf16[64,40,128]{2,1,0:T(8,128)(2,1)S(1)}, u32[]{:S(2)}, u32[]{:S(2)}) async-start(bf16[64,40,128]{2,1,0:T(8,128)(2,1)} %bitcast.34), calls=%async_computation.5 | async-start | bytes 1310720 | tf_op jit(solution)/shard_map/all_to_all | solution.py:671
  172.3 0.0 all-gather.5.cloned.1.call-done
  172.4 0.0 all-gather.7.cloned.1.call-done
  172.4 0.0 copy-start
  172.4 0.0 copy-start.5
  172.4 7.4 %weight_gradient.1.weight_grads = bf16[2,2,384,384]{3,2,1,0:T(8,128)(2,1)} custom-call(bf16[8,2,384,256]{3,2,1,0:T(8,128)(2,1)} %bitcast.37, bf16[8,2,384,256]{3,2,1,0:T(8,128)(2,1)} %bitcast.38, bf16[256,256]{1,0:T(8,128)(2,1)S(1)} %copy-done.9), custom_call_target="tpu_custom_call" | custom-call | flops 5000000000 | bytes 8000000 | tf_op jit(solution)/shard_map/weight_gradient/pallas_call | solution.py:702
  179.8 10.5 %all-to-all-done.5 = bf16[64,40,128]{2,1,0:T(8,128)(2,1)S(1)} async-done(((bf16[64,40,128]{2,1,0:T(8,128)(2,1)}), bf16[64,40,128]{2,1,0:T(8,128)(2,1)S(1)}, u32[]{:S(2)}, u32[]{:S(2)}) %all-to-all-start.5) | async-done | bytes 655392 | tf_op jit(solution)/shard_map/all_to_all | solution.py:671
  190.3 1.5 gather.1
  (13 shorter events, 0.0 us)
Async XLA Ops:
  7.2 44.4 %copy-start.2 = (bf16[4608,192]{1,0:T(8,128)(2,1)S(1)}, bf16[4608,192]{1,0:T(8,128)(2,1)}, u32[]{:S(2)}) copy-start(bf16[4608,192]{1,0:T(8,128)(2,1)} %constant.17.clone.table) | copy-start | bytes 5308420
  7.2 44.4 %copy-start.10 = (s32[128]{0:T(128)S(1)}, s32[128]{0:T(128)}, u32[]{:S(2)}) copy-start(s32[128]{0:T(128)} %param.15) | copy-start | bytes 1540
  10.8 40.8 %all-to-all-start = ((bf16[64,48,128]{2,1,0:T(8,128)(2,1)}), bf16[64,48,128]{2,1,0:T(8,128)(2,1)S(1)}, u32[]{:S(2)}, u32[]{:S(2)}) async-start(bf16[64,48,128]{2,1,0:T(8,128)(2,1)} %bitcast.2), calls=%async_computation | async-start | bytes 1572864 | tf_op jit(solution)/shard_map/all_to_all | solution.py:671
  27.4 145.0 %all-gather.5.cloned.1.call-start = ((), (), s32[]{:S(2)}) async-start(), calls=%async_computation.6 | async-start | bytes 3538944 | tf_op jit(solution)/shard_map/all_gather | solution.py:719
  29.8 54.7 %copy-start.6 = (bf16[1536,128]{1,0:T(8,128)(2,1)S(1)}, bf16[1536,128]{1,0:T(8,128)(2,1)}, u32[]{:S(2)}) copy-start(bf16[1536,128]{1,0:T(8,128)(2,1)} %get-tuple-element.9.rest_0_) | copy-start | bytes 1179652
  51.6 32.9 %copy-start.3 = (bf16[2,2,384,384]{3,2,1,0:T(8,128)(2,1)S(1)}, bf16[2,2,384,384]{3,2,1,0:T(8,128)(2,1)}, u32[]{:S(2)}) copy-start(bf16[2,2,384,384]{3,2,1,0:T(8,128)(2,1)} %weights.3) | copy-start | bytes 3538948
  51.6 32.9 %copy-start.7 = (bf16[256,256]{1,0:T(8,128)(2,1)S(1)}, bf16[256,256]{1,0:T(8,128)(2,1)}, u32[]{:S(2)}) copy-start(bf16[256,256]{1,0:T(8,128)(2,1)} %constant.23.clone.turn) | copy-start | bytes 393220
  85.7 86.7 %all-gather.7.cloned.1.call-start = ((), (), s32[]{:S(2)}) async-start(), calls=%async_computation.7 | async-start | bytes 3538944 | tf_op jit(solution)/shard_map/all_gather | solution.py:730
  114.3 29.9 %copy-start.4 = (bf16[2,2,384,384]{3,2,1,0:T(8,128)(2,1)S(1)}, bf16[2,2,384,384]{3,2,1,0:T(8,128)(2,1)}, u32[]{:S(2)}) copy-start(bf16[2,2,384,384]{3,2,1,0:T(8,128)(2,1)} %weights.3) | copy-start | bytes 3538948
  114.3 29.9 %copy-start.8 = (bf16[256,256]{1,0:T(8,128)(2,1)S(1)}, bf16[256,256]{1,0:T(8,128)(2,1)}, u32[]{:S(2)}) copy-start(bf16[256,256]{1,0:T(8,128)(2,1)} %constant.23.clone.turn) | copy-start | bytes 393220
  123.2 41.4 %copy-start.1 = (bf16[6144,256]{1,0:T(8,128)(2,1)S(1)}, bf16[6144,256]{1,0:T(8,128)(2,1)}, u32[]{:S(2)}) copy-start(bf16[6144,256]{1,0:T(8,128)(2,1)} %constant.19.clone.table) | copy-start | bytes 9437188
  164.6 7.8 %copy-start.9 = (bf16[256,256]{1,0:T(8,128)(2,1)S(1)}, bf16[256,256]{1,0:T(8,128)(2,1)}, u32[]{:S(2)}) copy-start(bf16[256,256]{1,0:T(8,128)(2,1)} %constant.23.clone.turn) | copy-start | bytes 393220
  167.5 22.8 %all-to-all-start.5 = ((bf16[64,40,128]{2,1,0:T(8,128)(2,1)}), bf16[64,40,128]{2,1,0:T(8,128)(2,1)S(1)}, u32[]{:S(2)}, u32[]{:S(2)}) async-start(bf16[64,40,128]{2,1,0:T(8,128)(2,1)} %bitcast.34), calls=%async_computation.5 | async-start | bytes 1310720 | tf_op jit(solution)/shard_map/all_to_all | solution.py:671
  172.4 17.9 %copy-start = (bf16[1,3,384,384]{3,2,1,0:T(8,128)(2,1)S(1)}, bf16[1,3,384,384]{3,2,1,0:T(8,128)(2,1)}, u32[]{:S(2)}) copy-start(bf16[1,3,384,384]{3,2,1,0:T(8,128)(2,1)} %param.13) | copy-start | bytes 2654212
  172.4 17.9 %copy-start.5 = (bf16[384,256]{1,0:T(8,128)(2,1)S(1)}, bf16[384,256]{1,0:T(8,128)(2,1)}, u32[]{:S(2)}) copy-start(bf16[384,256]{1,0:T(8,128)(2,1)} %constant.20.clone.forward_source.forward) | copy-start | bytes 589828
Sparse Core Ops, SparseCore 0:
  85.8 25.8 all-gather.4
  145.7 24.5 all-gather.6

commit v11 on v8

--- a/solution.py
+++ b/solution.py
@@ -104,6 +104,10 @@
         )
 
     synthesis = for_synthesis(table[:, :, low])
+    half = 8 * LOW * (BLOCKS // 2)
+    upper = synthesis[half:].reshape(BLOCKS // 4, 2, 8 * LOW, 4, 2, HALF)[:, :, :, :, 1]
+    upper = upper.reshape(BLOCKS // 4, 2, 8 * LOW, 128).transpose(0, 2, 1, 3).reshape(-1, 256)
+    synthesis = np.concatenate([synthesis[:half], upper], axis=0)
     weighted_synthesis = for_synthesis((table * quadrature)[:, :, low])
     forward, inverse = fourier_tables()
     turn = np.zeros((COEFS, COEFS), np.float32)
@@ -254,15 +258,18 @@
     return merge_blocks(sums)
 
 
-def synthesise(tiles, table, ready):
+def synthesise(tiles, table, ready, packed=False):
     sums = ([], [])
     order = (lane_of((LOW, 256)) % 8) // 2
     for t in range(BLOCKS):
         ready(t)
         operand = block_operand(tiles, t)
         for odd in (0, 1):
-            rows = operand[odd * GROUPS : (odd + 1) * GROUPS]
-            part = dot(table[pl.ds(STEPS[t] + odd * 4 * LOW, 4 * LOW), :], stacked(rows, 4, 4))
+            least, start, lanes = 0, STEPS[t], pl.ds(0, 256)
+            if packed and t >= BLOCKS // 2:
+                least, start, lanes = HALF, STEPS[(t + BLOCKS // 2) // 2], pl.ds(t % 2 * 128, 128)
+            rows = operand[odd * GROUPS + least : (odd + 1) * GROUPS]
+            part = dot(table[pl.ds(start + odd * 4 * LOW, 4 * LOW), lanes], stacked(rows, 4, 4))
             total = part[:LOW]
             for k in range(1, 4):
                 total = jnp.where(order == k, part[k * LOW : (k + 1) * LOW], total)
@@ -335,7 +342,7 @@
 
 def table_copies(source, target, sems, bounds):
     copies = []
-    for t in range(BLOCKS):
+    for t in range(len(bounds) - 1):
         rows = pl.ds(bounds[t], bounds[t + 1] - bounds[t])
         copies.append(pltpu.make_async_copy(source.at[rows, :], target.at[rows, :], sems.at[t]))
     return copies
@@ -427,7 +434,7 @@
     received, one, two, analysis, synthesis, degrees, inverse_source, turned_source, out,
     inverse, inverse_t, rows_one, rows_two, stage_one, stage_two, stage, table, table_s, row_sems, sems, sems_s,
 ):
-    copies_s = table_copies(synthesis, table_s, sems_s, STEPS)
+    copies_s = table_copies(synthesis, table_s, sems_s, STEPS[:7])
     copies = table_copies(analysis, table, sems, STARTS)
     fetches = (
         pltpu.make_async_copy(one.at[:, pl.ds(32, 16), :], rows_one, row_sems.at[0]),
@@ -438,7 +445,14 @@
     for copy in (*copies_s, *fetches, *copies):
         copy.start()
     tiles = slot_rows_in(received, degrees, stage)
-    synth = synthesise(tiles, table_s, lambda t: copies_s[t].wait())
+
+    def ready(t):
+        if t < BLOCKS // 2:
+            copies_s[t].wait()
+        elif t % 2 == 0:
+            copies_s[(t + BLOCKS // 2) // 2].wait()
+
+    synth = synthesise(tiles, table_s, ready, True)
     for fetch in fetches:
         fetch.wait()
     stage_one[...] = rows_one[...].astype(f32).reshape(GROUPS * 16, 128)
@@ -558,7 +572,7 @@
 
 
 TABLE = pltpu.VMEM((STARTS[-1], LATS), bf16)
-TABLE_S = pltpu.VMEM((STEPS[-1], 256), bf16)
+TABLE_S = pltpu.VMEM((STEPS[6], 256), bf16)
 
 
 def sems(count):

time: 197 us -> 197 us (level)
  no operation moved by 1% of the time
where the time goes in v11:
time: 197 us
  blocking collectives  139 us (71%)
  Pallas kernels  28.2 us (14%)
  between operations  14.2 us (7%)
  waiting for transfers between devices  10.6 us (5%)
  starting transfers between devices  4.94 us (3%)
    all_to_all x5, blocking collectives, exchange(): lax.all_to_all(rows.reshape(GROUPS, count, 128), 'lat', split_axis=0, con...  139 us
    all_to_all x1, waiting for transfers between devices, exchange(): lax.all_to_all(rows.reshape(GROUPS, count, 128), 'lat', split_axis=0, con...  10.5 us
    pallas_call x1, Pallas kernels, middle(): call(middle_kernel, message(SLOT_ROWS), [VMEM, ANY, ANY, ANY, ANY, VMEM,...  8.51 us
    pallas_call x1, Pallas kernels, weight_gradient(): call(gradient_kernel, jax.ShapeDtypeStruct((SLOTS, 2, CHANNELS, CHANNELS)...  7.38 us
    all_to_all x1, starting transfers between devices, exchange(): lax.all_to_all(rows.reshape(GROUPS, count, 128), 'lat', split_axis=0, con...  4.86 us
  transfers between devices with their start and end apart: 3, of which 1 were waited for; matrix products, arithmetic and copies ran while one was open for 0% of the time, Pallas kernels for 10%

profile of v11, /device:TPU:6, one launch (start us, length us, event | category | flops | bytes accessed | tf_op | source)
XLA Modules:
  0.0 196.7 jit_solution(16217970295631359265)
XLA Ops:
  7.2 0.0 copy-start.2
  7.2 0.0 copy-start.9
  7.2 0.0 all-gather.5.cloned.1.call-start
  7.2 3.2 %spread.1 = (bf16[3072,128]{1,0:T(8,128)(2,1)S(1)}, bf16[1536,128]{1,0:T(8,128)(2,1)S(1)}, bf16[1536,128]{1,0:T(8,128)(2,1)S(1)}) custom-call(bf16[3,384,384]{2,1,0:T(8,128)(2,1)} %bitcast.35, bf16[3,384,384]{2,1,0:T(8,128)(2,1)} %bitcast.18, bf16[384,256]{1,0:T(8,128)(2,1)} %constant.20.clone.forward_source.forward), custom_call_target="tpu_custom_call" | custom-call | flops 300000000 | bytes 4000000 | tf_op jit(solution)/shard_map/spread/pallas_call | solution.py:588
  10.4 40.6 %all_to_all.30.one = bf16[64,48,128]{2,1,0:T(8,128)(2,1)S(1)} all-to-all(bf16[64,48,128]{2,1,0:T(8,128)(2,1)S(1)} %bitcast.27), channel_id=1, replica_groups=mesh['lat'=64,'batch'=8] {'lat'}, dimensions={0} | all-to-all | bytes 1572864 | tf_op jit(solution)/shard_map/all_to_all | solution.py:661
  51.0 0.0 copy-done.2
  51.0 0.0 copy-done.9
  51.0 2.2 %first.1 = bf16[3072,128]{1,0:T(8,128)(2,1)S(1)} custom-call(bf16[3072,128]{1,0:T(8,128)(2,1)S(1)} %bitcast.20, bf16[4608,192]{1,0:T(8,128)(2,1)S(1)} %copy-done.2, s32[1,128]{1,0:T(1,128)S(1)} %bitcast.31, bf16[1536,128]{1,0:T(8,128)(2,1)S(1)} %get-tuple-element.10.carried), custom_call_target="tpu_custom_call" | custom-call | flops 1000000000 | bytes 6000000 | tf_op jit(solution)/shard_map/first/pallas_call | solution.py:601
  53.3 29.7 %all_to_all.31.two = bf16[64,48,128]{2,1,0:T(8,128)(2,1)S(1)} all-to-all(bf16[64,48,128]{2,1,0:T(8,128)(2,1)S(1)} %bitcast.22), channel_id=1, replica_groups=mesh['lat'=64,'batch'=8] {'lat'}, dimensions={0} | all-to-all | bytes 1572864 | tf_op jit(solution)/shard_map/all_to_all | solution.py:661
  83.0 0.0 copy-done.3
  83.0 1.2 mix.1
  84.2 0.0 all-gather.5.cloned.1.call-update
  84.2 0.0 all-gather.7.cloned.1.call-start
  84.3 28.6 %all_to_all.32 = bf16[64,48,128]{2,1,0:T(8,128)(2,1)S(1)} all-to-all(bf16[64,48,128]{2,1,0:T(8,128)(2,1)S(1)} %bitcast.25), channel_id=1, replica_groups=mesh['lat'=64,'batch'=8] {'lat'}, dimensions={0} | all-to-all | bytes 1572864 | tf_op jit(solution)/shard_map/all_to_all | solution.py:661
  112.8 8.5 %middle.1 = bf16[1536,128]{1,0:T(8,128)(2,1)S(1)} custom-call(bf16[3072,128]{1,0:T(8,128)(2,1)S(1)} %bitcast.26, bf16[64,48,128]{2,1,0:T(8,128)(2,1)S(1)} %all_to_all.30.one, bf16[64,48,128]{2,1,0:T(8,128)(2,1)S(1)} %all_to_all.31.two, bf16[4608,192]{1,0:T(8,128)(2,1)} %constant.16.clone.analysis, bf16[4608,256]{1,0:T(8,128)(2,1)} %constant.18.clone.synthesis, ...), custom_call_target="tpu_custom_call" | custom-call | flops 3000000000 | bytes 12000000 | tf_op jit(solution)/shard_map/middle/pallas_call | solution.py:613
  121.4 0.0 copy-start.1
  121.4 21.0 %all_to_all.33 = bf16[64,24,128]{2,1,0:T(8,128)(2,1)S(1)} all-to-all(bf16[64,24,128]{2,1,0:T(8,128)(2,1)S(1)} %bitcast.29), channel_id=1, replica_groups=mesh['lat'=64,'batch'=8] {'lat'}, dimensions={0} | all-to-all | bytes 786432 | tf_op jit(solution)/shard_map/all_to_all | solution.py:661
  142.4 0.0 copy-done.7
  142.4 1.3 adjoint_mix.1
  143.7 0.0 all-gather.7.cloned.1.call-update
  143.7 19.0 %all_to_all.34 = bf16[64,24,128]{2,1,0:T(8,128)(2,1)S(1)} all-to-all(bf16[64,24,128]{2,1,0:T(8,128)(2,1)S(1)} %bitcast.28), channel_id=1, replica_groups=mesh['lat'=64,'batch'=8] {'lat'}, dimensions={0} | all-to-all | bytes 786432 | tf_op jit(solution)/shard_map/all_to_all | solution.py:661
  162.7 0.0 copy-done.1
  162.7 2.9 %last.1 = bf16[2560,128]{1,0:T(8,128)(2,1)} custom-call(bf16[1536,128]{1,0:T(8,128)(2,1)S(1)} %bitcast.24, bf16[6144,256]{1,0:T(8,128)(2,1)S(1)} %copy-done.1, s32[1,128]{1,0:T(1,128)S(1)} %bitcast.33), custom_call_target="tpu_custom_call" | custom-call | flops 1000000000 | bytes 7000000 | tf_op jit(solution)/shard_map/last/pallas_call | solution.py:629
  165.6 4.9 %all-to-all-start.5 = ((bf16[64,40,128]{2,1,0:T(8,128)(2,1)}), bf16[64,40,128]{2,1,0:T(8,128)(2,1)S(1)}, u32[]{:S(2)}, u32[]{:S(2)}) async-start(bf16[64,40,128]{2,1,0:T(8,128)(2,1)} %bitcast.34), calls=%async_computation.5 | async-start | bytes 1310720 | tf_op jit(solution)/shard_map/all_to_all | solution.py:661
  170.5 0.0 all-gather.5.cloned.1.call-done
  170.5 0.0 all-gather.7.cloned.1.call-done
  170.6 0.0 copy-start
  170.6 0.0 copy-start.5
  170.6 7.4 %weight_gradient.1.weight_grads = bf16[2,2,384,384]{3,2,1,0:T(8,128)(2,1)} custom-call(bf16[8,2,384,256]{3,2,1,0:T(8,128)(2,1)} %bitcast.37, bf16[8,2,384,256]{3,2,1,0:T(8,128)(2,1)} %bitcast.38, bf16[256,256]{1,0:T(8,128)(2,1)S(1)} %copy-done.8), custom_call_target="tpu_custom_call" | custom-call | flops 5000000000 | bytes 8000000 | tf_op jit(solution)/shard_map/weight_gradient/pallas_call | solution.py:692
  178.0 10.5 %all-to-all-done.5 = bf16[64,40,128]{2,1,0:T(8,128)(2,1)S(1)} async-done(((bf16[64,40,128]{2,1,0:T(8,128)(2,1)}), bf16[64,40,128]{2,1,0:T(8,128)(2,1)S(1)}, u32[]{:S(2)}, u32[]{:S(2)}) %all-to-all-start.5) | async-done | bytes 655392 | tf_op jit(solution)/shard_map/all_to_all | solution.py:661
  188.4 0.0 copy-done
  188.5 1.5 gather.1
  (9 shorter events, 0.0 us)
Async XLA Ops:
  7.2 43.9 %copy-start.2 = (bf16[4608,192]{1,0:T(8,128)(2,1)S(1)}, bf16[4608,192]{1,0:T(8,128)(2,1)}, u32[]{:S(2)}) copy-start(bf16[4608,192]{1,0:T(8,128)(2,1)} %constant.17.clone.table) | copy-start | bytes 5308420
  7.2 43.9 %copy-start.9 = (s32[128]{0:T(128)S(1)}, s32[128]{0:T(128)}, u32[]{:S(2)}) copy-start(s32[128]{0:T(128)} %param.15) | copy-start | bytes 1540
  7.2 163.3 %all-gather.5.cloned.1.call-start = ((), (), s32[]{:S(2)}) async-start(), calls=%async_computation.6 | async-start | bytes 3538944 | tf_op jit(solution)/shard_map/all_gather | solution.py:708
  51.0 32.0 %copy-start.3 = (bf16[2,2,384,384]{3,2,1,0:T(8,128)(2,1)S(1)}, bf16[2,2,384,384]{3,2,1,0:T(8,128)(2,1)}, u32[]{:S(2)}) copy-start(bf16[2,2,384,384]{3,2,1,0:T(8,128)(2,1)} %weights.3) | copy-start | bytes 3538948
  51.0 32.0 %copy-start.6 = (bf16[256,256]{1,0:T(8,128)(2,1)S(1)}, bf16[256,256]{1,0:T(8,128)(2,1)}, u32[]{:S(2)}) copy-start(bf16[256,256]{1,0:T(8,128)(2,1)} %constant.23.clone.turn) | copy-start | bytes 393220
  84.2 86.3 %all-gather.7.cloned.1.call-start = ((), (), s32[]{:S(2)}) async-start(), calls=%async_computation.7 | async-start | bytes 3538944 | tf_op jit(solution)/shard_map/all_gather | solution.py:719
  112.8 29.5 %copy-start.4 = (bf16[2,2,384,384]{3,2,1,0:T(8,128)(2,1)S(1)}, bf16[2,2,384,384]{3,2,1,0:T(8,128)(2,1)}, u32[]{:S(2)}) copy-start(bf16[2,2,384,384]{3,2,1,0:T(8,128)(2,1)} %weights.3) | copy-start | bytes 3538948
  112.8 29.5 %copy-start.7 = (bf16[256,256]{1,0:T(8,128)(2,1)S(1)}, bf16[256,256]{1,0:T(8,128)(2,1)}, u32[]{:S(2)}) copy-start(bf16[256,256]{1,0:T(8,128)(2,1)} %constant.23.clone.turn) | copy-start | bytes 393220
  121.4 41.4 %copy-start.1 = (bf16[6144,256]{1,0:T(8,128)(2,1)S(1)}, bf16[6144,256]{1,0:T(8,128)(2,1)}, u32[]{:S(2)}) copy-start(bf16[6144,256]{1,0:T(8,128)(2,1)} %constant.19.clone.table) | copy-start | bytes 9437188
  162.7 7.8 %copy-start.8 = (bf16[256,256]{1,0:T(8,128)(2,1)S(1)}, bf16[256,256]{1,0:T(8,128)(2,1)}, u32[]{:S(2)}) copy-start(bf16[256,256]{1,0:T(8,128)(2,1)} %constant.23.clone.turn) | copy-start | bytes 393220
  165.6 22.8 %all-to-all-start.5 = ((bf16[64,40,128]{2,1,0:T(8,128)(2,1)}), bf16[64,40,128]{2,1,0:T(8,128)(2,1)S(1)}, u32[]{:S(2)}, u32[]{:S(2)}) async-start(bf16[64,40,128]{2,1,0:T(8,128)(2,1)} %bitcast.34), calls=%async_computation.5 | async-start | bytes 1310720 | tf_op jit(solution)/shard_map/all_to_all | solution.py:661
  170.6 17.9 %copy-start = (bf16[1,3,384,384]{3,2,1,0:T(8,128)(2,1)S(1)}, bf16[1,3,384,384]{3,2,1,0:T(8,128)(2,1)}, u32[]{:S(2)}) copy-start(bf16[1,3,384,384]{3,2,1,0:T(8,128)(2,1)} %param.13) | copy-start | bytes 2654212
  170.6 17.9 %copy-start.5 = (bf16[384,256]{1,0:T(8,128)(2,1)S(1)}, bf16[384,256]{1,0:T(8,128)(2,1)}, u32[]{:S(2)}) copy-start(bf16[384,256]{1,0:T(8,128)(2,1)} %constant.20.clone.forward_source.forward) | copy-start | bytes 589828
Sparse Core Ops, SparseCore 0:
  84.3 25.8 all-gather.4
  143.9 24.4 all-gather.6
